TPU v7x, 512 devices: a whole 4x8x8 slice. The times are simulated.
512 devices in a mesh: band: 32 (over z, y_lo, core), row: 4 (over x), col: 4 (over y_hi).
Axes of the slice: x: 4, y: 8 (y_hi: 4, y_lo: 2; y = y_hi * 2 + y_lo), z: 8, core: 2. Of those that a mesh axis runs over, the one named last changes fastest.
Arguments:
- cond_orbitals: bfloat16 [512, 512000], P(('band', 'row', 'col')), may hold values from -6 to 6
- val_orbitals: bfloat16 [256, 512000], P(None, ('band', 'row', 'col')), may hold values from -6 to 6
- val_index: int32 [1], replicated, may hold values from 0 to 255
- val_energy: float32 [256], replicated, may hold values from -20 to -2
- cond_energy: float32 [512], replicated, may hold values from 1 to 40
- band_list: int32 [512], P(('band', 'row', 'col')), may hold values from 0 to 511, each once
- g_index: int32 [10240], replicated, may hold values from 0 to 511999, as said below
- chi_old: float32 [10240, 10240], P(('band', 'row'), 'col'), may hold values from -4 to 4
Outputs:
- chi_new: float32 [10240, 10240], P(('band', 'row'), 'col')
Inputs may be any that keep to these rules, and one draw needn't show every extreme that they name: `g_index`: distinct flat grid indices (gx * 80 + gy) * 80 + gz of the 10240 frequencies nearest to zero, where a frequency above 40 counts as that frequency minus 80; equal distances in random order, listed by rising distance. `band_list`: each band number once.
All inputs are finite; a program needn't handle non-finite values.
Results may differ from a plain program's by a relative error of at most 0.013.
Values may be sent and summed in bfloat16 or wider, within the bound.
No kernel may reach another device: no remote copies, remote signals or barrier semaphores. Data moves between devices by JAX's collectives and lax.ppermute only.
A program may use at most 64 MiB of HBM per device.

v0:
```python
import math

import jax
import jax.numpy as jnp
import numpy as np
from jax import lax
from jax.sharding import PartitionSpec as P

NS = 80
NG = 10240


HIGHER = lax.Precision.HIGH


def sphere_extent(count, number):
    steps = np.arange(count)
    signed = np.where(steps > count // 2, steps - count, steps)
    radius = signed[:, None, None] ** 2 + signed[None, :, None] ** 2 + signed[None, None, :] ** 2
    largest = int(np.sort(radius.reshape(-1))[number - 1])
    return min(math.isqrt(largest), count // 2)


def kept_tables(count, extent):
    kept = (jnp.arange(2 * extent + 1, dtype=jnp.int32) - extent) % count
    steps = jnp.arange(count, dtype=jnp.int32)
    phase = kept[:, None] * steps[None, :] % count
    angle = phase.astype(jnp.float32) * (2.0 * math.pi / count)
    return (jnp.cos(angle), jnp.sin(angle))


def split_bf16(table):
    upper = table.astype(jnp.bfloat16)
    lower = (table - upper.astype(jnp.float32)).astype(jnp.bfloat16)
    return (upper, lower)


def sphere_index(g_index, count, extent):
    freq_z = g_index % count
    freq_y = g_index // count % count
    freq_x = g_index // (count * count)
    signed_z = jnp.where(freq_z > count // 2, freq_z - count, freq_z)
    signed_y = jnp.where(freq_y > count // 2, freq_y - count, freq_y)
    signed_x = jnp.where(freq_x > count // 2, freq_x - count, freq_x)
    side = 2 * extent + 1
    return ((signed_z + extent) * side + (signed_y + extent)) * side + (signed_x + extent)


def plane_values(orbital, valence, tables_x, cosine, sine, flat_index):
    count = cosine.shape[1]
    cos_hi, cos_lo, sin_hi, sin_lo = tables_x
    kept = cosine.shape[0]
    product = valence.astype(jnp.float32) * orbital.astype(jnp.float32)
    density = product.astype(jnp.bfloat16).reshape(count, count * count)
    first_re = jnp.dot(cos_hi, density, preferred_element_type=jnp.float32) + jnp.dot(
        cos_lo, density, preferred_element_type=jnp.float32
    )
    first_im = -(
        jnp.dot(sin_hi, density, preferred_element_type=jnp.float32)
        + jnp.dot(sin_lo, density, preferred_element_type=jnp.float32)
    )
    first_re = first_re.reshape(kept, count, count)
    first_im = first_im.reshape(kept, count, count)
    second_re = jnp.einsum("vy,gyz->zvg", cosine, first_re, precision=HIGHER) + jnp.einsum(
        "vy,gyz->zvg", sine, first_im, precision=HIGHER
    )
    second_im = jnp.einsum("vy,gyz->zvg", cosine, first_im, precision=HIGHER) - jnp.einsum(
        "vy,gyz->zvg", sine, first_re, precision=HIGHER
    )
    flat_re = second_re.reshape(count, kept * kept)
    flat_im = second_im.reshape(count, kept * kept)
    third_re = jnp.dot(
        cosine, flat_re, precision=HIGHER, preferred_element_type=jnp.float32
    ) + jnp.dot(sine, flat_im, precision=HIGHER, preferred_element_type=jnp.float32)
    third_im = jnp.dot(
        cosine, flat_im, precision=HIGHER, preferred_element_type=jnp.float32
    ) - jnp.dot(sine, flat_re, precision=HIGHER, preferred_element_type=jnp.float32)
    combined = (third_re - third_im).reshape(-1)
    picked = jnp.take(combined, flat_index)
    return (picked / math.sqrt(count**3)).astype(jnp.bfloat16)


def make_adder(panel, total, piece):
    rows = lax.slice_in_dim(panel, 0, piece.shape[0], axis=0)
    term = lax.dot_general(
        rows, piece, (((0,), (0,)), ((), ())), preferred_element_type=jnp.float32
    )
    return total + term


def body(
    cond_orbitals, val_orbitals, val_index, val_energy, cond_energy, band_list, g_index, chi_old
):
    pick = val_index[0]
    local_valence = lax.dynamic_index_in_dim(val_orbitals, pick, 0, keepdims=False)
    valence = lax.all_gather(local_valence, ("band", "row", "col"), axis=0, tiled=True)
    nval = val_energy.shape[0]
    e_val = jnp.sum(jnp.where(jnp.arange(nval, dtype=jnp.int32) == pick, val_energy, 0.0))
    ncond = cond_energy.shape[0]
    match = band_list[:, None] == jnp.arange(ncond, dtype=jnp.int32)[None, :]
    e_cond = jnp.sum(jnp.where(match, cond_energy[None, :], 0.0), axis=1)
    weight = 4.0 / ((e_val - e_cond) * math.sqrt(ncond))
    extent = sphere_extent(NS, NG)
    cosine, sine = kept_tables(NS, extent)
    tables_x = split_bf16(cosine) + split_bf16(sine)
    flat_index = sphere_index(g_index, NS, extent)
    local_count = cond_orbitals.shape[0]
    values = jnp.stack(
        [plane_values(cond_orbitals[0], valence, tables_x, cosine, sine, flat_index)]
    )
    scaled = (weight[:, None] * values.astype(jnp.float32)).astype(jnp.bfloat16)
    n_band = lax.axis_size("band")
    n_row = lax.axis_size("row")
    n_col = lax.axis_size("col")
    row_slices = lax.all_to_all(scaled, ("band", "row"), split_axis=1, concat_axis=0, tiled=True)
    row_panel = lax.all_gather(row_slices, "col", axis=0, tiled=True)
    width = row_panel.shape[1]
    row_panel = (
        row_panel.reshape(n_col, n_band * n_row, local_count, width)
        .transpose(1, 0, 2, 3)
        .reshape(-1, width)
    )
    col_slices = lax.all_to_all(values, "col", split_axis=1, concat_axis=0, tiled=True)
    start_total = jnp.zeros((width, col_slices.shape[1]), jnp.float32)
    update = make_adder(
        row_panel, start_total, lax.all_gather(col_slices, ("band", "row"), axis=0, tiled=True)
    )
    return chi_old + update


def solution(mesh):
    return jax.shard_map(
        body,
        mesh=mesh,
        in_specs=(
            P(("band", "row", "col"), None),
            P(None, ("band", "row", "col")),
            P(),
            P(),
            P(),
            P(("band", "row", "col")),
            P(),
            P(("band", "row"), "col"),
        ),
        out_specs=P(("band", "row"), "col"),
        check_vma=False,
    )
```

profile of v0, /device:TPU:1, one launch (start us, length us, event | category | flops | bytes accessed | tf_op | source)
XLA Modules:
  0.0 771.9 jit_solution(8170703136856712898)
XLA Ops:
  6.5 0.0 all-reduce.3.cloned.1.call-start
  7.3 0.3 copy-done
  7.6 0.2 dynamic-slice_reduce_fusion
  7.8 0.1 broadcast.112
  7.9 0.2 dynamic-update-slice
  8.2 1.0 copy-done.1
  9.2 0.0 all-reduce.3.cloned.1.call-update
  9.2 0.0 all-gather.5.cloned.1.call-start
  9.9 0.7 select_reduce_fusion
  10.6 0.6 fusion.86
  12.5 0.1 broadcast_clamp_fusion
  12.6 277.3 %all-reduce.3.cloned.1.call-done = bf16[512000]{0:T(1024)(128)(2,1)} async-done(((bf16[512000]{0:T(1024)(128)(2,1)}), bf16[512000]{0:T(1024)(128)(2,1)}) %all-reduce.3.cloned.1.call-update) | async-done | bytes 1024016
  290.0 1.5 convert_element_type.130
  291.5 0.4 copy-done.2
  291.8 21.4 %convert_reduce_fusion = bf16[512000]{0:T(1024)(128)(2,1)S(1)} fusion(f32[1,512000]{1,0:T(1,128)S(1)} %bitcast.48, bf16[1,512000]{1,0:T(2,128)(2,1)S(1)} %copy-done.2), kind=kLoop, calls=%fused_computation.7 | loop fusion | flops 1536000 | bytes 4096000 | tf_op jit(solution)/shard_map/convert_element_type | solution.py:54
  313.3 1.1 reshape.144
  314.4 0.4 fusion.81
  314.8 0.4 fusion.84
  315.2 1.3 fusion
  316.6 2.0 reshape.146
  318.5 1.3 fusion.19
  319.8 1.3 convolution_add_fusion.1
  321.2 2.0 reshape.145
  323.1 0.5 fusion.21
  323.7 0.5 copy-done.3
  324.1 0.5 fusion.3
  324.7 0.5 fusion.4
  325.2 0.2 copy.22
  325.5 0.2 copy.23
  325.8 0.4 fusion.28
  326.2 0.4 fusion.30
  326.6 0.4 convolution_add_fusion.4
  327.0 0.4 fusion.5
  327.5 0.1 reshape.149
  327.6 56.8 %gather_fusion = f32[10240]{0:T(1024)S(1)} fusion(f32[19683]{0:T(1024)S(1)} %reshape.149, s32[10240]{0:T(1024)S(1)} %get-tuple-element.7), kind=kCustom, calls=%fused_computation | custom fusion | bytes 122880 | tf_op jit(solution)/shard_map/jit(_take)/gather | solution.py:79
  384.4 0.0 copy-start.4
  384.4 0.5 broadcast.129
  384.9 0.8 reduce.6
  385.7 10.9 %all_to_all.26 = bf16[4,2,1280]{2,1,0:T(2,128)(2,1)S(1)} all-to-all(bf16[4,2,1280]{2,1,0:T(2,128)(2,1)S(1)} %reshape.182), channel_id=1, replica_groups=mesh['band'=32,'row'=4,'col'=4] {'col'}, dimensions={0} | all-to-all | bytes 40960 | tf_op jit(solution)/shard_map/all_to_all | solution.py:123
  396.6 0.6 reshape.183
  397.2 0.0 all-gather.5.cloned.1.call-update
  397.3 0.1 reshape.179
  397.4 20.6 %all_to_all.27 = bf16[1,128,80]{2,0,1:T(2,128)(2,1)S(1)} all-to-all(bf16[1,128,80]{2,0,1:T(2,128)(2,1)S(1)} %reshape.179), channel_id=1, replica_groups=mesh['band'=32,'row'=4,'col'=4] {'band','row'}, dimensions={1} | all-to-all | bytes 40960 | tf_op jit(solution)/shard_map/all_to_all | solution.py:115
  418.0 0.1 copy.25
  418.1 10.4 %all-gather.1 = bf16[1,512,80]{1,2,0:T(8,128)(2,1)S(1)} all-gather(bf16[1,128,80]{1,2,0:T(8,128)(2,1)S(1)} %copy.25), channel_id=3, replica_groups=mesh['band'=32,'row'=4,'col'=4] {'col'}, dimensions={1}, use_global_device_ids=true | all-gather | bytes 102400 | tf_op jit(solution)/shard_map/all_gather | solution.py:116
  428.5 0.1 copy.26
  428.7 332.4 %all-gather.5.cloned.1.call-done = bf16[1,512,2560]{2,0,1:T(2,128)(2,1)} async-done(((bf16[1,4,2560]{2,0,1:T(2,128)(2,1)}), bf16[1,512,2560]{2,0,1:T(2,128)(2,1)}) %all-gather.5.cloned.1.call-update) | async-done | bytes 2621456 | tf_op jit(solution)/shard_map/all_gather | solution.py:126
  761.0 4.0 convolution_add_fusion.2
  (18 shorter events, 0.2 us)
Async XLA Ops:
  6.5 1.1 copy-start
  6.5 283.4 %all-reduce.3.cloned.1.call-start = ((), (), s32[]{:S(2)}) async-start(), calls=%async_computation.3 | async-start | bytes 2048000
  7.6 2.3 copy-start.6
  7.6 3.0 copy-start.7
  7.6 4.9 copy-start.5
  8.2 1.0 copy-start.1
  9.2 751.9 %all-gather.5.cloned.1.call-start = ((), (), s32[]{:S(2)}) async-start(), calls=%async_computation.2 | async-start | bytes 5283840 | tf_op jit(solution)/shard_map/all_gather | solution.py:126
  290.0 1.9 copy-start.2
  323.1 1.0 copy-start.3
  384.4 376.7 %copy-start.4 = (f32[80,2560]{1,0:T(8,128)S(1)}, f32[80,2560]{1,0:T(8,128)}, u32[]{:S(2)}) copy-start(f32[80,2560]{1,0:T(8,128)} %param.15) | copy-start | bytes 2457604
Sparse Core Ops, SparseCore 0:
  12.4 277.4 all-reduce.2
  397.4 363.6 all-gather.4
where the time goes:
time: 774 us; the launch traced here: 772 us
  waiting for transfers between devices  610 us (79%)
  local copies, waits for them, and re-layouts  66.8 us (9%)
  blocking collectives  41.9 us (5%)
  other arithmetic  25.1 us (3%)
  between operations  16.3 us (2%)
  matrix products  12 us (2%)
    all_gather x1, waiting for transfers between devices, body(): lax.all_gather(col_slices, ('band', 'row'), axis=0, tiled=True)  332 us
    unnamed x3, waiting for transfers between devices  277 us
    gather x1, local copies, waits for them, and re-layouts, plane_values(): picked = jnp.take(combined, flat_index)  56.8 us
    convert_element_type x1, other arithmetic, plane_values(): density = product.astype(jnp.bfloat16).reshape(count, count * count)  21.4 us
    all_to_all x1, blocking collectives, body(): lax.all_to_all(scaled, ('band', 'row'), split_axis=1, concat_axis=0, tile...  20.6 us
  transfers between devices with their start and end apart: 2, of which 2 were waited for; matrix products, arithmetic and copies ran while one was open for 0% of the time, Pallas kernels for 0%

commit v1 on v0

v1 whole, which is shorter than its diff:
```python
import math

import jax
import jax.numpy as jnp
import numpy as np
from jax import lax
from jax.experimental import pallas as pl
from jax.experimental.pallas import tpu as pltpu
from jax.sharding import Mesh, PartitionSpec as P

NS = 80
NG = 10240
NCOND = 512
GRID = NS**3
PIECE = 1000
KEPT = 14
BF16 = jnp.bfloat16
F32 = jnp.float32
AXES = ("za", "zb", "yl", "core", "x", "yh")
SIZES = (4, 2, 2, 2, 4, 4)
BAND = ("za", "zb", "yl", "core")
VMEM = pl.BlockSpec(memory_space=pltpu.VMEM)
SMEM = pl.BlockSpec(memory_space=pltpu.SMEM)


def tables():
    freq = np.arange(KEPT)
    angle = 2 * np.pi * np.outer(np.arange(NS), freq) / NS
    along_z = np.zeros((NS, 32))
    along_z[:, :KEPT] = np.cos(angle)
    along_z[:, 16 : 16 + KEPT] = np.sin(angle)
    first = np.kron(np.eye(8), along_z)
    row = np.arange(800)
    band = 2 * (row % 16) + row % 32 // 16
    line = 25 * band + row // 32
    angle = 2 * np.pi * np.outer(freq, line // 10) / NS
    along_x = np.zeros((32, 800))
    along_x[:KEPT] = np.cos(angle)
    along_x[16 : 16 + KEPT] = np.sin(angle)
    tens = line % 10
    along_q = np.concatenate(
        [
            np.cos(2 * np.pi * np.outer(np.arange(6), tens) / 10),
            np.sin(2 * np.pi * np.outer(np.arange(1, 5), tens) / 10),
        ]
    )
    second = (along_q[:, None, :] * along_x[None]).reshape(320, 800)
    angle = 2 * np.pi * np.outer(freq, np.arange(256) // 32) / NS
    third = np.zeros((32, 256))
    third[:KEPT] = np.cos(angle)
    third[16 : 16 + KEPT] = np.sin(angle)
    return first, second, third


def segments(m):
    found, lane = [], 0
    while lane < 128:
        piece, inside = divmod(128 * m + lane, PIECE)
        row, start = divmod(inside, 128)
        found.append((piece, row, lane))
        lane += min(128 - lane, 128 - start, PIECE - inside)
    return found


def index_parts(g_index):
    freq_z = g_index % NS
    freq_y = g_index // NS % NS
    freq_x = g_index // (NS * NS)

    def signed(freq):
        return jnp.where(freq > NS // 2, freq - NS, freq)

    x, y, z = signed(freq_x), signed(freq_y), signed(freq_z)
    sign = (x < 0).astype(jnp.int32) + 2 * (y < 0) + 4 * (z < 0)
    high = (jnp.abs(y) // 2) * 16 + jnp.abs(x)
    low = (jnp.abs(y) % 2) * 128 + sign * 16 + jnp.abs(z)
    return low, high


def values_kernel(
    pick_ref, energy_ref, own_ref, other_ref, cond_ref, low_ref, high_ref, bands_ref,
    first_ref, second_ref, third_ref, h_ref, weight_ref, val, block, rows,
):
    core = lax.axis_index("core")
    half = own_ref.shape[0]
    start = pl.multiple_of(core * half, half)
    val[pl.ds(start, half), :] = own_ref[...].astype(F32)
    val[pl.ds(pl.multiple_of(half - start, half), half), :] = other_ref[...].astype(F32)

    inside = (lax.axis_index("zb") * 2 + lax.axis_index("yl")) * 128 + lax.axis_index("x") * 32 + 7
    lane = lax.broadcasted_iota(jnp.int32, (16, 128), 1)
    tail = jnp.concatenate(
        [
            val[pl.ds(start + inside + 512 * za + 8 * yh, 1), :]
            for za in range(4)
            for yh in range(4)
        ],
        axis=0,
    )
    upper = jnp.sum(jnp.where(lane == 104, tail, 0.0), axis=1, keepdims=True)
    lower = jnp.sum(jnp.where(lane == 105, tail, 0.0), axis=1, keepdims=True)
    number = (2.0 * upper + lower).astype(jnp.int32)
    match = lax.broadcasted_iota(jnp.int32, (16, NCOND), 1) == number
    e_cond = jnp.sum(jnp.where(match, bands_ref[...], 0.0), axis=1, keepdims=True)
    e_val = energy_ref[pick_ref[0]]
    weight = 4.0 / ((e_val - e_cond) * math.sqrt(NCOND))
    weight_ref[...] = jnp.broadcast_to(weight, (16, 128))

    lane = lax.broadcasted_iota(jnp.int32, (32, 128), 1)
    turned = {}

    def turn(piece, row):
        if (piece, row) not in turned:
            found = val[pl.ds(8 * piece + row, 32, stride=128), :]
            shift = 104 * piece % 128
            turned[piece, row] = pltpu.roll(found, shift, 1) if shift else found
        return turned[piece, row]

    parts = []
    for n in range(25):
        for t in range(5):
            m = 5 * n + t
            valence = None
            for piece, row, begin in segments(m):
                found = turn(piece, row)
                valence = found if valence is None else jnp.where(lane >= begin, found, valence)
            orbital = jnp.concatenate(
                [cond_ref[pl.ds(m + 125 * c, 16, stride=250), :] for c in range(2)], axis=0
            )
            block[32 * n : 32 * n + 32, 128 * t : 128 * t + 128] = (valence * orbital).astype(BF16)
        if n % 5 == 4:
            parts.append(
                jnp.dot(
                    block[32 * (n - 4) : 32 * (n + 1), :],
                    first_ref[...],
                    preferred_element_type=F32,
                ).astype(BF16)
            )
    second = jnp.dot(second_ref[...], jnp.concatenate(parts, axis=0), preferred_element_type=F32)

    lane = lax.broadcasted_iota(jnp.int32, (16, 128), 1)
    group = lane // 16
    even = group % 2 == 0
    sx = jnp.where(group & 1 == 0, 1.0, -1.0)
    sy = jnp.where(group & 2 == 0, 1.0, -1.0)
    sz = jnp.where(group & 4 == 0, 1.0, -1.0)
    sxy, sxz, syz = sx * sy, sx * sz, sy * sz
    sxyz = sxy * sz

    def add_lanes(value):
        value = value[:, :128] + value[:, 128:]
        value = value + pltpu.roll(value, 64, 1)
        return value + pltpu.roll(value, 32, 1)

    def split(value):
        other = pltpu.roll(value, 16, 1)
        found = []
        for begin in (0, 16):
            a, b = value[begin : begin + 16], other[begin : begin + 16]
            found += [jnp.where(even, a, b), jnp.where(even, b, a)]
        return found

    planes = []
    for gy in range(KEPT):
        digit, sign = gy % 10, 1.0
        if digit > 5:
            digit, sign = 10 - digit, -1.0
        cosine, sine = third_ref[gy : gy + 1, :], third_ref[16 + gy : 17 + gy, :]
        even_q = second[32 * digit : 32 * digit + 32]
        re, im = even_q * cosine, even_q * sine
        if 1 <= digit <= 4:
            odd_q = second[32 * (digit + 5) : 32 * (digit + 5) + 32]
            re, im = re - (sign * sine) * odd_q, im + (sign * cosine) * odd_q
        ccc, ccs, scc, scs = split(add_lanes(re))
        csc, css, ssc, sss = split(add_lanes(im))
        total = (
            (ccc - syz * css) + (sz * ccs + sy * csc) + (sx * scc - sxz * scs) - (sxy * ssc + sxyz * sss)
        )
        planes.append((total * (1.0 / math.sqrt(GRID))).astype(BF16))
    cube = jnp.concatenate(
        [jnp.concatenate(planes[2 * i : 2 * i + 2], axis=1) for i in range(7)], axis=0
    )

    width = 1280
    place = lax.broadcasted_iota(jnp.int32, (112, width), 0)
    inner = lax.broadcasted_iota(jnp.int32, (256, width), 0)
    for c in range(NG // width):
        part = slice(c * width, (c + 1) * width)
        chosen = jnp.where(inner == low_ref[:, part], 1.0, 0.0).astype(BF16)
        found = jnp.dot(cube, chosen, preferred_element_type=F32)
        found = jnp.sum(jnp.where(place == high_ref[:, part], found, 0.0), axis=0, keepdims=True)
        for k in range(width // 128):
            rows[c * (width // 128) + k : c * (width // 128) + k + 1, :] = found[:, 128 * k : 128 * k + 128]
    mine = rows[...].astype(BF16)
    for k in range(16):
        h_ref[k] = mine


def pack_kernel(h_ref, weight_ref, out_ref, wide, full):
    wide[...] = h_ref[...].reshape(16 * 80, 128).astype(F32)
    for k in range(80):
        full[:, 128 * k : 128 * k + 128] = wide[pl.ds(k, 16, stride=80), :]
    col = lax.axis_index("yh") * 2560
    for c in range(2):
        cols = full[:, pl.ds(pl.multiple_of(col + 1280 * c, 128), 1280)].astype(BF16)
        for k in range(32):
            if k // 4 % 2 == c:
                out_ref[k, :, 0:1280] = cols
    rows = full[:, pl.ds(pl.multiple_of(lax.axis_index("za") * 2560, 128), 2560)]
    rows = weight_ref[:, 0:1] * rows
    for k in range(32):
        for at, piece in ((1280, k), (1408, k ^ 4)):
            begin = 80 * piece
            first, shift = begin // 128 * 128, begin % 128
            found = rows[:, first : first + 128]
            if shift:
                found = pltpu.roll(found, 128 - shift, 1)
                if shift > 48:
                    after = pltpu.roll(rows[:, first + 128 : first + 256], 128 - shift, 1)
                    lane = lax.broadcasted_iota(jnp.int32, (16, 128), 1)
                    found = jnp.where(lane < 128 - shift, found, after)
            out_ref[k, :, at : at + 128] = found.astype(BF16)


def product_kernel(begin, all_ref, out_ref):
    left = all_ref[:, begin : begin + 128]
    out_ref[...] = lax.dot_general(
        left, all_ref[:, 0:1280], (((0,), (0,)), ((), ())), preferred_element_type=F32
    )[0:80]


def finish_kernel(chi_ref, own_ref, other_ref, out_ref):
    core = lax.axis_index("core")
    at = pl.multiple_of(core * 1280, 1280)
    off = pl.multiple_of(1280 - core * 1280, 1280)
    out_ref[:, pl.ds(at, 1280)] = chi_ref[:, pl.ds(at, 1280)] + own_ref[...]
    out_ref[:, pl.ds(off, 1280)] = chi_ref[:, pl.ds(off, 1280)] + other_ref[...]


def call(kernel, out, in_specs, scratch=(), mib=16, flops=0, moved=0):
    return pl.pallas_call(
        kernel,
        out_shape=out,
        in_specs=in_specs,
        out_specs=jax.tree.map(lambda _: VMEM, out),
        scratch_shapes=scratch,
        compiler_params=pltpu.CompilerParams(vmem_limit_bytes=mib * 2**20),
        cost_estimate=pl.CostEstimate(flops=flops, bytes_accessed=moved, transcendentals=0),
    )


def body(cond_orbitals, val_orbitals, val_index, val_energy, cond_energy, band_list, g_index, chi_old):
    shape = jax.ShapeDtypeStruct
    pick = val_index[0]
    piece = lax.dynamic_index_in_dim(val_orbitals, pick, 0, keepdims=False)
    tail = jnp.concatenate([band_list // 2, band_list % 2]).astype(BF16)
    piece = jnp.concatenate([piece, tail, jnp.zeros((22,), BF16)]).reshape(1, 8, 128)
    own = lax.all_to_all(
        jnp.broadcast_to(piece, (256, 8, 128)), ("za", "zb", "yl", "x", "yh"), 0, 0, tiled=True
    ).reshape(2048, 128)
    other = lax.ppermute(own, "core", [(0, 1), (1, 0)])
    orbital = cond_orbitals.astype(F32).reshape(4000, 128)
    low, high = index_parts(g_index)
    first, second, third = tables()
    values, weight = call(
        values_kernel,
        (shape((16, 80, 128), BF16), shape((16, 128), F32)),
        [SMEM, SMEM] + [VMEM] * 9,
        [pltpu.VMEM((4096, 128), F32), pltpu.VMEM((800, 640), BF16), pltpu.VMEM((80, 128), F32)],
        mib=32,
    )(
        val_index, val_energy, own, other, orbital, low.reshape(1, NG), high.reshape(1, NG),
        cond_energy.reshape(1, NCOND), jnp.asarray(first, BF16), jnp.asarray(second, BF16), jnp.asarray(third, F32),
    )
    gathered = lax.all_to_all(values, ("za", "yh"), 0, 0, tiled=True)
    packed = call(
        pack_kernel,
        shape((32, 16, 1536), BF16),
        [VMEM] * 2,
        [pltpu.VMEM((1280, 128), F32), pltpu.VMEM((16, NG), F32)],
    )(gathered, weight)
    panel = lax.all_to_all(packed, ("zb", "yl", "core", "x"), 0, 0, tiled=True).reshape(512, 1536)
    block = shape((80, 1280), F32)
    given = call(lambda *refs: product_kernel(1408, *refs), block, [VMEM])(panel)
    taken = lax.ppermute(given, "core", [(0, 1), (1, 0)])
    kept = call(lambda *refs: product_kernel(1280, *refs), block, [VMEM])(panel)
    return call(finish_kernel, shape((80, 2560), F32), [VMEM] * 3)(chi_old, kept, taken)


def solution(mesh):
    fine = Mesh(mesh.devices.reshape(SIZES), AXES)
    every = AXES
    return jax.shard_map(
        body,
        mesh=fine,
        in_specs=(
            P(every, None),
            P(None, every),
            P(),
            P(),
            P(),
            P(every),
            P(),
            P(BAND + ("x",), "yh"),
        ),
        out_specs=P(BAND + ("x",), "yh"),
        check_vma=False,
    )
```

time: 774 us -> 109 us (0.14)
  waiting for transfers between devices: 610 us -> 0.97 us
  local copies, waits for them, and re-layouts: 66.8 us -> 0.36 us
  blocking collectives: 41.9 us -> 87.1 us
  other arithmetic: 25.1 us -> 3.98 us
  between operations: 16.3 us -> 1.55 us
  matrix products: 12 us -> 0 us
    all_gather x1 -> x0, waiting for transfers between devices: 332 us -> none  [body(): lax.all_gather(col_slices, ('band', 'row'), axis=0, tiled=True)]
    unnamed x3 -> x0, waiting for transfers between devices: 277 us -> none
    gather x1 -> x0, local copies, waits for them, and re-layouts: 56.8 us -> none  [plane_values(): picked = jnp.take(combined, flat_index)]
    all_to_all x2 -> x3, blocking collectives: 31.5 us -> 87.1 us  [the longest x1 41.2 us: body(): lax.all_to_all(jnp.broadcast_to(piece, (256, 8, 128)), ('za', 'zb', 'yl',...]
    convert_element_type x3 -> x0, other arithmetic: 22.9 us -> none  [the longest x1 21.4 us: plane_values(): density = product.astype(jnp.bfloat16).reshape(count, count * count)]
    dot_general x13 -> x0, matrix products: 12 us -> none  [the longest x1 3.98 us: make_adder(): lax.dot_general(rows, piece, (((0,), (0,)), ((), ())), preferred_element_...]
    all_gather x1 -> x0, blocking collectives: 10.4 us -> none  [body(): row_panel = lax.all_gather(row_slices, 'col', axis=0, tiled=True)]
  transfers between devices with their start and end apart: 2 -> 2, of which waited for: 2 -> 1; matrix products, arithmetic and copies ran while one was open for 0% -> 4% of each run, Pallas kernels for 0% -> 0%
where the time goes in v1:
time: 109 us
  blocking collectives  87.1 us (80%)
  starting transfers between devices  7.55 us (7%)
  Pallas kernels  7.48 us (7%)
  other arithmetic  3.98 us (4%)
  between operations  1.55 us (1%)
    all_to_all x1, blocking collectives, body(): lax.all_to_all(jnp.broadcast_to(piece, (256, 8, 128)), ('za', 'zb', 'yl',...  41.2 us
    all_to_all x1, blocking collectives, body(): lax.all_to_all(packed, ('zb', 'yl', 'core', 'x'), 0, 0, tiled=True)  28.5 us
    all_to_all x1, blocking collectives, body(): gathered = lax.all_to_all(values, ('za', 'yh'), 0, 0, tiled=True)  17.4 us
    pallas_call x1, Pallas kernels, body(): call(values_kernel, (shape((16, 80, 128), BF16), shape((16, 128), F32)),...  5.27 us
    ppermute x1, starting transfers between devices, body(): other = lax.ppermute(own, 'core', [(0, 1), (1, 0)])  4.91 us
    reshape x1, other arithmetic, body(): orbital = cond_orbitals.astype(F32).reshape(4000, 128)  3.73 us
    ppermute x1, starting transfers between devices, body(): taken = lax.ppermute(given, 'core', [(0, 1), (1, 0)])  2.63 us
  transfers between devices with their start and end apart: 2, of which 1 were waited for; matrix products, arithmetic and copies ran while one was open for 4% of the time, Pallas kernels for 0%

profile of v1, /device:TPU:1, one launch (start us, length us, event | category | flops | bytes accessed | tf_op | source)
XLA Modules:
  0.0 109.0 jit_solution(775950830876336881)
XLA Ops:
  0.0 0.0 copy-start
  1.4 0.0 copy-done
  1.4 0.2 dynamic-slice_reduce_fusion
  1.7 0.1 maximum_bitcast_fusion
  1.7 0.1 broadcast_in_dim.8
  1.8 41.2 %all_to_all.15 = bf16[256,8,128]{2,1,0:T(8,128)(2,1)S(1)} all-to-all(bf16[256,8,128]{2,1,0:T(8,128)(2,1)S(1)} %broadcast_in_dim.8), channel_id=1, replica_groups=mesh['za'=4,'zb'=2,'yl'=2,'core'=2,'x'=4,'yh'=4] {'za','zb','yl','x','yh'}, dimensions={0} | all-to-all | bytes 1048576 | tf_op jit(solution)/shard_map/all_to_all | solution.py:258
  43.0 0.0 copy-start.7
  43.0 0.0 copy-start.2
  43.0 0.0 copy-start.3
  43.0 0.0 copy-start.4
  43.0 0.0 copy-start.5
  43.1 0.0 copy-start.6
  43.1 4.9 %collective-permute-start = (bf16[2048,128]{1,0:T(8,128)(2,1)S(1)}, bf16[2048,128]{1,0:T(8,128)(2,1)S(1)}, u32[]{:S(2)}, u32[]{:S(2)}) collective-permute-start(bf16[2048,128]{1,0:T(8,128)(2,1)S(1)} %bitcast.15), channel_id=1, source_target_pairs={{0,16},{16,0},{1,17},{17,1},{2,18},{18,2},{3,19},{19,3},{4,20},{20... | collective-permute-start | bytes 1572872 | tf_op jit(solution)/shard_map/ppermute | solution.py:261
  48.0 3.7 %reshape.33 = f32[1,512000]{1,0:T(1,128)S(1)} convert(bf16[1,512000]{1,0:T(2,128)(2,1)} %param.11) | non-fusion elementwise | flops 512000 | bytes 3072000 | tf_op jit(solution)/shard_map/reshape | solution.py:262
  51.7 0.0 copy-done.7
  51.7 0.2 fusion.5
  51.9 0.0 collective-permute-done.other_ref
  51.9 0.0 copy-done.2
  51.9 0.0 copy-done.3
  51.9 0.0 copy-done.4
  52.0 0.0 copy-done.5
  52.0 0.0 copy-done.6
  52.0 5.3 %shard_map.109 = (bf16[16,80,128]{2,1,0:T(8,128)(2,1)S(1)}, f32[16,128]{1,0:T(8,128)S(1)}) custom-call(s32[1]{0:T(128)} %copy.12.pick_ref, f32[256]{0:T(256)S(1)} %copy-done.6, bf16[2048,128]{1,0:T(8,128)(2,1)S(1)} %bitcast.16, bf16[2048,128]{1,0:T(8,128)(2,1)S(1)} %collective-permute-done.other_ref, f32[4000,128]{1,0:T(8,128)S(1)} %bitcast.14, ...), custom_call_target="tpu_custom_call" | custom-call | tf_op jit(solution)/shard_map/pallas_call | solution.py:265
  57.2 17.4 %all_to_all.16.h_ref = bf16[16,80,128]{2,1,0:T(8,128)(2,1)S(1)} all-to-all(bf16[16,80,128]{2,1,0:T(8,128)(2,1)S(1)} %get-tuple-element.7), channel_id=1, replica_groups=mesh['za'=4,'zb'=2,'yl'=2,'core'=2,'x'=4,'yh'=4] {'za','yh'}, dimensions={0} | all-to-all | bytes 655360 | tf_op jit(solution)/shard_map/all_to_all | solution.py:275
  74.7 0.5 shard_map.110
  75.1 28.5 %all_to_all.17 = bf16[32,16,1536]{2,1,0:T(8,128)(2,1)S(1)} all-to-all(bf16[32,16,1536]{2,1,0:T(8,128)(2,1)S(1)} %shard_map.110), channel_id=1, replica_groups=mesh['za'=4,'zb'=2,'yl'=2,'core'=2,'x'=4,'yh'=4] {'zb','yl','core','x'}, dimensions={0} | all-to-all | bytes 3145728 | tf_op jit(solution)/shard_map/all_to_all | solution.py:282
  103.6 0.0 copy-start.1
  103.6 0.4 shard_map.112
  104.0 2.6 %collective-permute-start.1 = (f32[80,1280]{1,0:T(8,128)S(1)}, f32[80,1280]{1,0:T(8,128)S(1)}, u32[]{:S(2)}, u32[]{:S(2)}) collective-permute-start(f32[80,1280]{1,0:T(8,128)S(1)} %shard_map.112), channel_id=1, source_target_pairs={{0,16},{16,0},{1,17},{17,1},{2,18},{18,2},{3,19},{19,3},{4,20},{20... | collective-permute-start | bytes 1228808 | tf_op jit(solution)/shard_map/ppermute | solution.py:285
  106.7 0.4 shard_map.111.own_ref
  107.0 1.0 collective-permute-done.1.other_ref
  108.0 0.0 copy-done.1
  108.0 1.0 shard_map.113
  (1 shorter events, 0.0 us)
Async XLA Ops:
  0.0 1.4 %copy-start = (bf16[256,1000]{0,1:T(8,128)(2,1)S(1)}, bf16[256,1000]{0,1:T(8,128)(2,1)}, u32[]{:S(2)}) copy-start(bf16[256,1000]{0,1:T(8,128)(2,1)} %param.12) | copy-start | bytes 1536004
  43.0 8.7 %copy-start.7 = (s32[10240]{0:T(1024)S(1)}, s32[10240]{0:T(1024)}, u32[]{:S(2)}) copy-start(s32[10240]{0:T(1024)} %param.17) | copy-start | bytes 122884
  43.0 8.9 %copy-start.2 = (bf16[320,800]{1,0:T(8,128)(2,1)S(1)}, bf16[320,800]{1,0:T(8,128)(2,1)}, u32[]{:S(2)}) copy-start(bf16[320,800]{1,0:T(8,128)(2,1)} %constant.105.clone.second_ref) | copy-start | bytes 1536004
  43.0 8.9 %copy-start.3 = (bf16[640,256]{1,0:T(8,128)(2,1)S(1)}, bf16[640,256]{1,0:T(8,128)(2,1)}, u32[]{:S(2)}) copy-start(bf16[640,256]{1,0:T(8,128)(2,1)} %constant.104.clone.first_ref) | copy-start | bytes 983044
  43.0 8.9 %copy-start.4 = (f32[32,256]{1,0:T(8,128)S(1)}, f32[32,256]{1,0:T(8,128)}, u32[]{:S(2)}) copy-start(f32[32,256]{1,0:T(8,128)} %constant.106.clone.third_ref) | copy-start | bytes 98308
  43.0 8.9 %copy-start.5 = (f32[512]{0:T(512)S(1)}, f32[512]{0:T(512)}, u32[]{:S(2)}) copy-start(f32[512]{0:T(512)} %param.15) | copy-start | bytes 6148
  43.1 8.9 %copy-start.6 = (f32[256]{0:T(256)S(1)}, f32[256]{0:T(256)}, u32[]{:S(2)}) copy-start(f32[256]{0:T(256)} %energy_ref.1) | copy-start | bytes 3076
  43.1 8.8 %collective-permute-start = (bf16[2048,128]{1,0:T(8,128)(2,1)S(1)}, bf16[2048,128]{1,0:T(8,128)(2,1)S(1)}, u32[]{:S(2)}, u32[]{:S(2)}) collective-permute-start(bf16[2048,128]{1,0:T(8,128)(2,1)S(1)} %bitcast.15), channel_id=1, source_target_pairs={{0,16},{16,0},{1,17},{17,1},{2,18},{18,2},{3,19},{19,3},{4,20},{20... | collective-permute-start | bytes 1572872 | tf_op jit(solution)/shard_map/ppermute | solution.py:261
  103.6 4.4 %copy-start.1 = (f32[80,2560]{1,0:T(8,128)S(1)}, f32[80,2560]{1,0:T(8,128)}, u32[]{:S(2)}) copy-start(f32[80,2560]{1,0:T(8,128)} %chi_ref.1) | copy-start | bytes 2457604
  104.0 4.0 %collective-permute-start.1 = (f32[80,1280]{1,0:T(8,128)S(1)}, f32[80,1280]{1,0:T(8,128)S(1)}, u32[]{:S(2)}, u32[]{:S(2)}) collective-permute-start(f32[80,1280]{1,0:T(8,128)S(1)} %shard_map.112), channel_id=1, source_target_pairs={{0,16},{16,0},{1,17},{17,1},{2,18},{18,2},{3,19},{19,3},{4,20},{20... | collective-permute-start | bytes 1228808 | tf_op jit(solution)/shard_map/ppermute | solution.py:285

commit v2 on v1

--- a/solution.py
+++ b/solution.py
@@ -78,40 +78,29 @@
 
 
 def values_kernel(
-    pick_ref, energy_ref, own_ref, other_ref, cond_ref, low_ref, high_ref, bands_ref,
-    first_ref, second_ref, third_ref, h_ref, weight_ref, val, block, rows,
+    pick_ref, number_ref, val_energy_ref, cond_energy_ref, own_ref, other_ref, cond_ref, chosen_ref, high_ref,
+    first_ref, second_ref, third_ref, out_ref, val, block, rows, scaled, points, arrived,
 ):
+    fetch = pltpu.make_async_copy(chosen_ref, points, arrived)
+    fetch.start()
     core = lax.axis_index("core")
     half = own_ref.shape[0]
     start = pl.multiple_of(core * half, half)
     val[pl.ds(start, half), :] = own_ref[...].astype(F32)
     val[pl.ds(pl.multiple_of(half - start, half), half), :] = other_ref[...].astype(F32)
-
-    inside = (lax.axis_index("zb") * 2 + lax.axis_index("yl")) * 128 + lax.axis_index("x") * 32 + 7
-    lane = lax.broadcasted_iota(jnp.int32, (16, 128), 1)
-    tail = jnp.concatenate(
-        [
-            val[pl.ds(start + inside + 512 * za + 8 * yh, 1), :]
-            for za in range(4)
-            for yh in range(4)
-        ],
-        axis=0,
-    )
-    upper = jnp.sum(jnp.where(lane == 104, tail, 0.0), axis=1, keepdims=True)
-    lower = jnp.sum(jnp.where(lane == 105, tail, 0.0), axis=1, keepdims=True)
-    number = (2.0 * upper + lower).astype(jnp.int32)
-    match = lax.broadcasted_iota(jnp.int32, (16, NCOND), 1) == number
-    e_cond = jnp.sum(jnp.where(match, bands_ref[...], 0.0), axis=1, keepdims=True)
-    e_val = energy_ref[pick_ref[0]]
+    e_val = jnp.full((1, 128), val_energy_ref[pick_ref[0]], F32)
+    e_cond = jnp.full((1, 128), cond_energy_ref[number_ref[0]], F32)
     weight = 4.0 / ((e_val - e_cond) * math.sqrt(NCOND))
-    weight_ref[...] = jnp.broadcast_to(weight, (16, 128))
 
     lane = lax.broadcasted_iota(jnp.int32, (32, 128), 1)
     turned = {}
 
     def turn(piece, row):
         if (piece, row) not in turned:
-            found = val[pl.ds(8 * piece + row, 32, stride=128), :]
+            at = piece // 4 * 512 + piece % 4 * 8 + row
+            found = jnp.concatenate(
+                [val[pl.ds(at + half * c, 16, stride=32), :] for c in range(2)], axis=0
+            )
             shift = 104 * piece % 128
             turned[piece, row] = pltpu.roll(found, shift, 1) if shift else found
         return turned[piece, row]
@@ -183,58 +172,72 @@
 
     width = 1280
     place = lax.broadcasted_iota(jnp.int32, (112, width), 0)
+    fetch.wait()
+    for c in range(NG // width):
+        part = slice(c * width, (c + 1) * width)
+        found = jnp.dot(cube, points[:, part], preferred_element_type=F32)
+        found = jnp.sum(jnp.where(place == high_ref[:, part], found, 0.0), axis=0, keepdims=True)
+        found = found.astype(BF16).astype(F32)
+        for k in range(width // 128):
+            at = c * (width // 128) + k
+            piece = found[:, 128 * k : 128 * k + 128]
+            rows[at : at + 1, :] = piece
+            scaled[at : at + 1, :] = weight * piece
+    for k in range(16):
+        yh, za = k % 4, k // 4
+        out_ref[k] = jnp.concatenate(
+            [rows[20 * yh : 20 * yh + 20, :], scaled[20 * za : 20 * za + 20, :]], axis=0
+        ).astype(BF16)
+
+
+def chosen_kernel(low_ref, out_ref):
+    width = 1280
     inner = lax.broadcasted_iota(jnp.int32, (256, width), 0)
     for c in range(NG // width):
         part = slice(c * width, (c + 1) * width)
-        chosen = jnp.where(inner == low_ref[:, part], 1.0, 0.0).astype(BF16)
-        found = jnp.dot(cube, chosen, preferred_element_type=F32)
-        found = jnp.sum(jnp.where(place == high_ref[:, part], found, 0.0), axis=0, keepdims=True)
-        for k in range(width // 128):
-            rows[c * (width // 128) + k : c * (width // 128) + k + 1, :] = found[:, 128 * k : 128 * k + 128]
-    mine = rows[...].astype(BF16)
+        out_ref[:, part] = jnp.where(inner == low_ref[:, part], 1.0, 0.0).astype(BF16)
+
+
+def pack_kernel(h_ref, out_ref, wide, full):
+    wide[...] = h_ref[...].reshape(16 * 40, 128).astype(F32)
+    for k in range(40):
+        full[:, 128 * k : 128 * k + 128] = wide[pl.ds(k, 16, stride=40), :]
+    cols = full[:, 0:2560].astype(BF16)
+    lane = lax.broadcasted_iota(jnp.int32, (16, 128), 1)
+    core = lax.axis_index("core")
     for k in range(16):
-        h_ref[k] = mine
-
-
-def pack_kernel(h_ref, weight_ref, out_ref, wide, full):
-    wide[...] = h_ref[...].reshape(16 * 80, 128).astype(F32)
-    for k in range(80):
-        full[:, 128 * k : 128 * k + 128] = wide[pl.ds(k, 16, stride=80), :]
-    col = lax.axis_index("yh") * 2560
-    for c in range(2):
-        cols = full[:, pl.ds(pl.multiple_of(col + 1280 * c, 128), 1280)].astype(BF16)
-        for k in range(32):
-            if k // 4 % 2 == c:
-                out_ref[k, :, 0:1280] = cols
-    rows = full[:, pl.ds(pl.multiple_of(lax.axis_index("za") * 2560, 128), 2560)]
-    rows = weight_ref[:, 0:1] * rows
-    for k in range(32):
-        for at, piece in ((1280, k), (1408, k ^ 4)):
-            begin = 80 * piece
-            first, shift = begin // 128 * 128, begin % 128
-            found = rows[:, first : first + 128]
+        out_ref[k, :, 0:2560] = cols
+        pieces = []
+        for c in range(2):
+            begin = 80 * (k // 4 * 8 + 4 * c + k % 4)
+            first, shift = 2560 + begin // 128 * 128, begin % 128
+            found = full[:, first : first + 128]
             if shift:
                 found = pltpu.roll(found, 128 - shift, 1)
                 if shift > 48:
-                    after = pltpu.roll(rows[:, first + 128 : first + 256], 128 - shift, 1)
-                    lane = lax.broadcasted_iota(jnp.int32, (16, 128), 1)
+                    after = pltpu.roll(full[:, first + 128 : first + 256], 128 - shift, 1)
                     found = jnp.where(lane < 128 - shift, found, after)
-            out_ref[k, :, at : at + 128] = found.astype(BF16)
-
-
-def product_kernel(begin, all_ref, out_ref):
-    left = all_ref[:, begin : begin + 128]
-    out_ref[...] = lax.dot_general(
-        left, all_ref[:, 0:1280], (((0,), (0,)), ((), ())), preferred_element_type=F32
-    )[0:80]
-
-
-def finish_kernel(chi_ref, own_ref, other_ref, out_ref):
-    core = lax.axis_index("core")
-    at = pl.multiple_of(core * 1280, 1280)
-    off = pl.multiple_of(1280 - core * 1280, 1280)
-    out_ref[:, pl.ds(at, 1280)] = chi_ref[:, pl.ds(at, 1280)] + own_ref[...]
-    out_ref[:, pl.ds(off, 1280)] = chi_ref[:, pl.ds(off, 1280)] + other_ref[...]
+            pieces.append(found)
+        mine = jnp.where(core == 0, pieces[0], pieces[1])
+        theirs = jnp.where(core == 0, pieces[1], pieces[0])
+        out_ref[k, :, 2560:2688] = mine.astype(BF16)
+        out_ref[k, :, 2688:2816] = theirs.astype(BF16)
+
+
+def times(left, right):
+    return lax.dot_general(left, right, (((0,), (0,)), ((), ())), preferred_element_type=F32)[0:80]
+
+
+def given_kernel(all_ref, out_ref):
+    out_ref[...] = times(all_ref[:, 2688:2816], all_ref[:, 0:2560])
+
+
+def kept_kernel(all_ref, chi_ref, out_ref):
+    out_ref[...] = chi_ref[...] + times(all_ref[:, 2560:2688], all_ref[:, 0:2560])
+
+
+def finish_kernel(kept_ref, taken_ref, out_ref):
+    out_ref[...] = kept_ref[...] + taken_ref[...]
 
 
 def call(kernel, out, in_specs, scratch=(), mib=16, flops=0, moved=0):
@@ -251,40 +254,46 @@
 
 def body(cond_orbitals, val_orbitals, val_index, val_energy, cond_energy, band_list, g_index, chi_old):
     shape = jax.ShapeDtypeStruct
-    pick = val_index[0]
-    piece = lax.dynamic_index_in_dim(val_orbitals, pick, 0, keepdims=False)
-    tail = jnp.concatenate([band_list // 2, band_list % 2]).astype(BF16)
-    piece = jnp.concatenate([piece, tail, jnp.zeros((22,), BF16)]).reshape(1, 8, 128)
+    piece = lax.dynamic_index_in_dim(val_orbitals, val_index[0], 0, keepdims=False)
+    piece = jnp.pad(piece, (0, 24)).reshape(1, 8, 128)
     own = lax.all_to_all(
-        jnp.broadcast_to(piece, (256, 8, 128)), ("za", "zb", "yl", "x", "yh"), 0, 0, tiled=True
+        jnp.broadcast_to(piece, (64, 8, 128)), ("za", "zb", "yl", "yh"), 0, 0, tiled=True
+    )
+    orbital = cond_orbitals.astype(F32).reshape(4000, 128)
+    low, high = index_parts(g_index)
+    chosen = call(chosen_kernel, shape((256, NG), BF16), [VMEM], moved=2**23)(low.reshape(1, NG))
+    chosen = pltpu.with_memory_space_constraint(chosen, pltpu.HBM)
+    own, orbital, chosen, high = lax.optimization_barrier((own, orbital, chosen, high))
+    own = lax.all_to_all(
+        jnp.broadcast_to(own.reshape(1, 512, 128), (4, 512, 128)), "x", 0, 0, tiled=True
     ).reshape(2048, 128)
     other = lax.ppermute(own, "core", [(0, 1), (1, 0)])
-    orbital = cond_orbitals.astype(F32).reshape(4000, 128)
-    low, high = index_parts(g_index)
     first, second, third = tables()
-    values, weight = call(
+    values = call(
         values_kernel,
-        (shape((16, 80, 128), BF16), shape((16, 128), F32)),
-        [SMEM, SMEM] + [VMEM] * 9,
-        [pltpu.VMEM((4096, 128), F32), pltpu.VMEM((800, 640), BF16), pltpu.VMEM((80, 128), F32)],
-        mib=32,
+        shape((16, 40, 128), BF16),
+        [SMEM] * 4 + [VMEM] * 3 + [pl.BlockSpec(memory_space=pltpu.HBM)] + [VMEM] * 4,
+        [pltpu.VMEM((4096, 128), F32), pltpu.VMEM((800, 640), BF16)]
+        + [pltpu.VMEM((80, 128), F32)] * 2
+        + [pltpu.VMEM((256, NG), BF16), pltpu.SemaphoreType.DMA(())],
+        mib=24,
     )(
-        val_index, val_energy, own, other, orbital, low.reshape(1, NG), high.reshape(1, NG),
-        cond_energy.reshape(1, NCOND), jnp.asarray(first, BF16), jnp.asarray(second, BF16), jnp.asarray(third, F32),
+        val_index, band_list, val_energy, cond_energy, own, other, orbital, chosen, high.reshape(1, NG),
+        jnp.asarray(first, BF16), jnp.asarray(second, BF16), jnp.asarray(third, F32),
     )
     gathered = lax.all_to_all(values, ("za", "yh"), 0, 0, tiled=True)
     packed = call(
         pack_kernel,
-        shape((32, 16, 1536), BF16),
-        [VMEM] * 2,
-        [pltpu.VMEM((1280, 128), F32), pltpu.VMEM((16, NG), F32)],
-    )(gathered, weight)
-    panel = lax.all_to_all(packed, ("zb", "yl", "core", "x"), 0, 0, tiled=True).reshape(512, 1536)
-    block = shape((80, 1280), F32)
-    given = call(lambda *refs: product_kernel(1408, *refs), block, [VMEM])(panel)
+        shape((16, 16, 2816), BF16),
+        [VMEM],
+        [pltpu.VMEM((640, 128), F32), pltpu.VMEM((16, 5120), F32)],
+    )(gathered)
+    panel = lax.all_to_all(packed, ("zb", "yl", "x"), 0, 0, tiled=True).reshape(256, 2816)
+    block = shape((80, 2560), F32)
+    given = call(given_kernel, block, [VMEM])(panel)
     taken = lax.ppermute(given, "core", [(0, 1), (1, 0)])
-    kept = call(lambda *refs: product_kernel(1280, *refs), block, [VMEM])(panel)
-    return call(finish_kernel, shape((80, 2560), F32), [VMEM] * 3)(chi_old, kept, taken)
+    kept = call(kept_kernel, block, [VMEM] * 2)(panel, chi_old)
+    return call(finish_kernel, block, [VMEM] * 2)(kept, taken)
 
 
 def solution(mesh):

time: 109 us -> 105 us (0.963)
  blocking collectives: 87.1 us -> 51.4 us
  starting transfers between devices: 7.55 us -> 27.1 us
  waiting for transfers between devices: 0.97 us -> 6.85 us
  local copies, waits for them, and re-layouts: 0.36 us -> 4.57 us
  Pallas kernels: 7.48 us -> 9.54 us
    all_to_all x2, blocking collectives: 69.7 us -> 33.2 us  [the longest x1 22.4 us: body(): lax.all_to_all(packed, ('zb', 'yl', 'x'), 0, 0, tiled=True)]
    all_to_all x0 -> x1, starting transfers between devices: none -> 17.4 us  [body(): lax.all_to_all(jnp.broadcast_to(piece, (64, 8, 128)), ('za', 'zb', 'yl',...]
    all_to_all x0 -> x1, waiting for transfers between devices: none -> 4.43 us  [body(): lax.all_to_all(jnp.broadcast_to(piece, (64, 8, 128)), ('za', 'zb', 'yl',...]
    unnamed x16 -> x18, local copies, waits for them, and re-layouts: 0.04 us -> 2.66 us
    pallas_call x5 -> x6, Pallas kernels: 7.48 us -> 9.54 us  [the longest x1 6.8 us: body(): call(values_kernel, shape((16, 40, 128), BF16), [SMEM] * 4 + [VMEM] * 3 +...]
    ppermute x1, starting transfers between devices: 2.63 us -> 4.23 us  [body(): taken = lax.ppermute(given, 'core', [(0, 1), (1, 0)])]
    broadcast_in_dim x1 -> x3, local copies, waits for them, and re-layouts: 0.07 us -> 1.66 us  [the longest x1 0.97 us: body(): jnp.broadcast_to(own.reshape(1, 512, 128), (4, 512, 128))]
  transfers between devices with their start and end apart: 2 -> 3, of which waited for: 1 -> 3; matrix products, arithmetic and copies ran while one was open for 4% -> 4% of each run, Pallas kernels for 0% -> 1%
where the time goes in v2:
time: 105 us
  blocking collectives  51.4 us (49%)
  starting transfers between devices  27.1 us (26%)
  Pallas kernels  9.54 us (9%)
  waiting for transfers between devices  6.85 us (7%)
  local copies, waits for them, and re-layouts  4.57 us (4%)
  other arithmetic  3.9 us (4%)
  between operations  1.53 us (1%)
    all_to_all x1, blocking collectives, body(): lax.all_to_all(packed, ('zb', 'yl', 'x'), 0, 0, tiled=True)  22.4 us
    all_to_all x1, blocking collectives, body(): gathered = lax.all_to_all(values, ('za', 'yh'), 0, 0, tiled=True)  18.2 us
    all_to_all x1, starting transfers between devices, body(): lax.all_to_all(jnp.broadcast_to(piece, (64, 8, 128)), ('za', 'zb', 'yl',...  17.4 us
    all_to_all x1, blocking collectives, body(): lax.all_to_all(jnp.broadcast_to(own.reshape(1, 512, 128), (4, 512, 128)),...  10.8 us
    pallas_call x1, Pallas kernels, body(): call(values_kernel, shape((16, 40, 128), BF16), [SMEM] * 4 + [VMEM] * 3 +...  6.8 us
    ppermute x1, starting transfers between devices, body(): other = lax.ppermute(own, 'core', [(0, 1), (1, 0)])  5.46 us
    all_to_all x1, waiting for transfers between devices, body(): lax.all_to_all(jnp.broadcast_to(piece, (64, 8, 128)), ('za', 'zb', 'yl',...  4.43 us
    ppermute x1, starting transfers between devices, body(): taken = lax.ppermute(given, 'core', [(0, 1), (1, 0)])  4.23 us
  transfers between devices with their start and end apart: 3, of which 3 were waited for; matrix products, arithmetic and copies ran while one was open for 4% of the time, Pallas kernels for 1%

profile of v2, /device:TPU:1, one launch (start us, length us, event | category | flops | bytes accessed | tf_op | source)
XLA Modules:
  0.0 104.8 jit_solution(8486675208081082194)
XLA Ops:
  0.0 0.0 copy-start
  0.7 0.3 copy-done
  1.1 0.2 dynamic-slice_reduce_fusion
  1.3 0.7 broadcast_in_dim.15
  2.0 17.4 %all-to-all-start = ((bf16[64,8,128]{2,1,0:T(8,128)(2,1)}), bf16[64,8,128]{2,1,0:T(8,128)(2,1)}, u32[]{:S(2)}, u32[]{:S(2)}) async-start(bf16[64,8,128]{2,1,0:T(8,128)(2,1)} %broadcast_in_dim.15), calls=%async_computation | async-start | bytes 262144 | tf_op jit(solution)/shard_map/all_to_all | solution.py:259
  19.4 0.0 copy-start.8
  19.4 3.7 %reshape.28 = f32[1,512000]{1,0:T(1,128)S(1)} convert(bf16[1,512000]{1,0:T(2,128)(2,1)} %param.11) | non-fusion elementwise | flops 512000 | bytes 3072000 | tf_op jit(solution)/shard_map/reshape | solution.py:262
  23.2 0.0 copy-done.8
  23.2 0.2 fusion.5
  23.3 0.0 copy-start.4
  23.3 0.0 copy-start.5
  23.4 0.0 copy-start.6
  23.4 0.0 copy-start.7
  23.4 0.9 shard_map.109.chosen_ref
  24.2 0.0 copy-start.1
  24.3 2.3 %copy-done.1 = bf16[256,10240]{1,0:T(8,128)(2,1)} copy-done((bf16[256,10240]{1,0:T(8,128)(2,1)}, bf16[256,10240]{1,0:T(8,128)(2,1)S(1)}, u32[]{:S(2)}) %copy-start.1) | copy-done | bytes 5242904
  26.5 0.0 copy-start.3
  26.5 4.4 %all-to-all-done = bf16[64,8,128]{2,1,0:T(8,128)(2,1)} async-done(((bf16[64,8,128]{2,1,0:T(8,128)(2,1)}), bf16[64,8,128]{2,1,0:T(8,128)(2,1)}, u32[]{:S(2)}, u32[]{:S(2)}) %all-to-all-start) | async-done | bytes 131104 | tf_op jit(solution)/shard_map/all_to_all | solution.py:259
  31.0 1.0 broadcast_in_dim.17
  31.9 10.8 %all_to_all.20 = bf16[4,512,128]{2,1,0:T(8,128)(2,1)S(1)} all-to-all(bf16[4,512,128]{2,1,0:T(8,128)(2,1)S(1)} %broadcast_in_dim.17), channel_id=1, replica_groups=mesh['za'=4,'zb'=2,'yl'=2,'core'=2,'x'=4,'yh'=4] {'x'}, dimensions={0} | all-to-all | bytes 1048576 | tf_op jit(solution)/shard_map/all_to_all | solution.py:267
  42.7 5.5 %collective-permute-start = (bf16[2048,128]{1,0:T(8,128)(2,1)S(1)}, bf16[2048,128]{1,0:T(8,128)(2,1)S(1)}, u32[]{:S(2)}, u32[]{:S(2)}) collective-permute-start(bf16[2048,128]{1,0:T(8,128)(2,1)S(1)} %bitcast.15), channel_id=1, source_target_pairs={{0,16},{16,0},{1,17},{17,1},{2,18},{18,2},{3,19},{19,3},{4,20},{20... | collective-permute-start | bytes 1572872 | tf_op jit(solution)/shard_map/ppermute | solution.py:270
  48.8 0.9 collective-permute-done.other_ref
  49.7 0.0 copy-done.4
  49.7 0.0 copy-done.5
  49.7 0.0 copy-done.6
  49.7 0.0 copy-done.7
  49.7 0.0 copy-done.3
  49.7 6.8 %shard_map.110 = bf16[16,40,128]{2,1,0:T(8,128)(2,1)S(1)} custom-call(s32[1]{0:T(128)} %copy.12.pick_ref, s32[1]{0:T(128)S(6)} %copy.13.number_ref, f32[256]{0:T(256)S(1)} %copy-done.7, f32[512]{0:T(512)S(1)} %copy-done.6, bf16[2048,128]{1,0:T(8,128)(2,1)S(1)} %bitcast.16, bf16[2048,128]{1,0:T(8,128)(2,1)S(1)} %collective-permute-done.other_ref, ...), custom_call_target="tpu_custom_call" | custom-call | tf_op jit(solution)/shard_map/pallas_call | solution.py:272
  56.5 18.2 %all_to_all.21.h_ref = bf16[16,40,128]{2,1,0:T(8,128)(2,1)S(1)} all-to-all(bf16[16,40,128]{2,1,0:T(8,128)(2,1)S(1)} %shard_map.110), channel_id=1, replica_groups=mesh['za'=4,'zb'=2,'yl'=2,'core'=2,'x'=4,'yh'=4] {'za','yh'}, dimensions={0} | all-to-all | bytes 327680 | tf_op jit(solution)/shard_map/all_to_all | solution.py:284
  74.7 0.2 shard_map.111
  74.9 0.0 copy-start.2
  74.9 22.4 %all_to_all.22 = bf16[16,16,2816]{2,1,0:T(8,128)(2,1)S(1)} all-to-all(bf16[16,16,2816]{2,1,0:T(8,128)(2,1)S(1)} %shard_map.111), channel_id=1, replica_groups=mesh['za'=4,'zb'=2,'yl'=2,'core'=2,'x'=4,'yh'=4] {'zb','yl','x'}, dimensions={0} | all-to-all | bytes 2883584 | tf_op jit(solution)/shard_map/all_to_all | solution.py:291
  97.3 0.4 shard_map.113
  97.7 4.2 %collective-permute-start.1 = (f32[80,2560]{1,0:T(8,128)S(1)}, f32[80,2560]{1,0:T(8,128)S(1)}, u32[]{:S(2)}, u32[]{:S(2)}) collective-permute-start(f32[80,2560]{1,0:T(8,128)S(1)} %shard_map.113), channel_id=1, source_target_pairs={{0,16},{16,0},{1,17},{17,1},{2,18},{18,2},{3,19},{19,3},{4,20},{20... | collective-permute-start | bytes 2457608 | tf_op jit(solution)/shard_map/ppermute | solution.py:294
  101.9 0.0 copy-done.2
  101.9 0.4 shard_map.112.kept_ref
  102.3 1.6 %collective-permute-done.1.taken_ref = f32[80,2560]{1,0:T(8,128)S(1)} collective-permute-done((f32[80,2560]{1,0:T(8,128)S(1)}, f32[80,2560]{1,0:T(8,128)S(1)}, u32[]{:S(2)}, u32[]{:S(2)}) %collective-permute-start.1) | collective-permute-done | bytes 819232 | tf_op jit(solution)/shard_map/ppermute | solution.py:294
  103.9 1.0 shard_map.114
  (1 shorter events, 0.0 us)
Async XLA Ops:
  0.0 1.1 %copy-start = (bf16[256,1000]{0,1:T(8,128)(2,1)S(1)}, bf16[256,1000]{0,1:T(8,128)(2,1)}, u32[]{:S(2)}) copy-start(bf16[256,1000]{0,1:T(8,128)(2,1)} %param.12) | copy-start | bytes 1536004
  2.0 29.0 %all-to-all-start = ((bf16[64,8,128]{2,1,0:T(8,128)(2,1)}), bf16[64,8,128]{2,1,0:T(8,128)(2,1)}, u32[]{:S(2)}, u32[]{:S(2)}) async-start(bf16[64,8,128]{2,1,0:T(8,128)(2,1)} %broadcast_in_dim.15), calls=%async_computation | async-start | bytes 262144 | tf_op jit(solution)/shard_map/all_to_all | solution.py:259
  19.4 3.8 %copy-start.8 = (s32[10240]{0:T(1024)S(1)}, s32[10240]{0:T(1024)}, u32[]{:S(2)}) copy-start(s32[10240]{0:T(1024)} %param.17) | copy-start | bytes 122884
  23.3 26.4 %copy-start.4 = (bf16[640,256]{1,0:T(8,128)(2,1)S(1)}, bf16[640,256]{1,0:T(8,128)(2,1)}, u32[]{:S(2)}) copy-start(bf16[640,256]{1,0:T(8,128)(2,1)} %constant.78.clone.first_ref) | copy-start | bytes 983044
  23.3 26.4 %copy-start.5 = (f32[32,256]{1,0:T(8,128)S(1)}, f32[32,256]{1,0:T(8,128)}, u32[]{:S(2)}) copy-start(f32[32,256]{1,0:T(8,128)} %constant.80.clone.third_ref) | copy-start | bytes 98308
  23.4 26.3 %copy-start.6 = (f32[512]{0:T(512)S(1)}, f32[512]{0:T(512)}, u32[]{:S(2)}) copy-start(f32[512]{0:T(512)} %cond_energy_ref.1) | copy-start | bytes 6148
  23.4 26.3 %copy-start.7 = (f32[256]{0:T(256)S(1)}, f32[256]{0:T(256)}, u32[]{:S(2)}) copy-start(f32[256]{0:T(256)} %val_energy_ref.1) | copy-start | bytes 3076
  24.2 2.3 %copy-start.1 = (bf16[256,10240]{1,0:T(8,128)(2,1)}, bf16[256,10240]{1,0:T(8,128)(2,1)S(1)}, u32[]{:S(2)}) copy-start(bf16[256,10240]{1,0:T(8,128)(2,1)S(1)} %shard_map.109.chosen_ref) | copy-start | bytes 15728644
  26.5 23.2 %copy-start.3 = (bf16[320,800]{1,0:T(8,128)(2,1)S(1)}, bf16[320,800]{1,0:T(8,128)(2,1)}, u32[]{:S(2)}) copy-start(bf16[320,800]{1,0:T(8,128)(2,1)} %constant.79.clone.second_ref) | copy-start | bytes 1536004
  42.7 7.0 %collective-permute-start = (bf16[2048,128]{1,0:T(8,128)(2,1)S(1)}, bf16[2048,128]{1,0:T(8,128)(2,1)S(1)}, u32[]{:S(2)}, u32[]{:S(2)}) collective-permute-start(bf16[2048,128]{1,0:T(8,128)(2,1)S(1)} %bitcast.15), channel_id=1, source_target_pairs={{0,16},{16,0},{1,17},{17,1},{2,18},{18,2},{3,19},{19,3},{4,20},{20... | collective-permute-start | bytes 1572872 | tf_op jit(solution)/shard_map/ppermute | solution.py:270
  74.9 27.0 %copy-start.2 = (f32[80,2560]{1,0:T(8,128)S(1)}, f32[80,2560]{1,0:T(8,128)}, u32[]{:S(2)}) copy-start(f32[80,2560]{1,0:T(8,128)} %chi_ref.1) | copy-start | bytes 2457604
  97.7 6.2 %collective-permute-start.1 = (f32[80,2560]{1,0:T(8,128)S(1)}, f32[80,2560]{1,0:T(8,128)S(1)}, u32[]{:S(2)}, u32[]{:S(2)}) collective-permute-start(f32[80,2560]{1,0:T(8,128)S(1)} %shard_map.113), channel_id=1, source_target_pairs={{0,16},{16,0},{1,17},{17,1},{2,18},{18,2},{3,19},{19,3},{4,20},{20... | collective-permute-start | bytes 2457608 | tf_op jit(solution)/shard_map/ppermute | solution.py:294

commit v3 on v2

--- a/solution.py
+++ b/solution.py
@@ -30,9 +30,8 @@
     along_z[:, :KEPT] = np.cos(angle)
     along_z[:, 16 : 16 + KEPT] = np.sin(angle)
     first = np.kron(np.eye(8), along_z)
-    row = np.arange(800)
-    band = 2 * (row % 16) + row % 32 // 16
-    line = 25 * band + row // 32
+    core, row = np.divmod(np.arange(800), 400)
+    line = 25 * (2 * (row % 16) + core) + row // 16
     angle = 2 * np.pi * np.outer(freq, line // 10) / NS
     along_x = np.zeros((32, 800))
     along_x[:KEPT] = np.cos(angle)
@@ -44,7 +43,7 @@
             np.sin(2 * np.pi * np.outer(np.arange(1, 5), tens) / 10),
         ]
     )
-    second = (along_q[:, None, :] * along_x[None]).reshape(320, 800)
+    second = (along_q[:, None, :] * along_x[None]).reshape(320, 2, 400).transpose(1, 0, 2)
     angle = 2 * np.pi * np.outer(freq, np.arange(256) // 32) / NS
     third = np.zeros((32, 256))
     third[:KEPT] = np.cos(angle)
@@ -77,30 +76,30 @@
     return low, high
 
 
-def values_kernel(
-    pick_ref, number_ref, val_energy_ref, cond_energy_ref, own_ref, other_ref, cond_ref, chosen_ref, high_ref,
-    first_ref, second_ref, third_ref, out_ref, val, block, rows, scaled, points, arrived,
-):
-    fetch = pltpu.make_async_copy(chosen_ref, points, arrived)
-    fetch.start()
-    core = lax.axis_index("core")
-    half = own_ref.shape[0]
-    start = pl.multiple_of(core * half, half)
-    val[pl.ds(start, half), :] = own_ref[...].astype(F32)
-    val[pl.ds(pl.multiple_of(half - start, half), half), :] = other_ref[...].astype(F32)
-    e_val = jnp.full((1, 128), val_energy_ref[pick_ref[0]], F32)
-    e_cond = jnp.full((1, 128), cond_energy_ref[number_ref[0]], F32)
-    weight = 4.0 / ((e_val - e_cond) * math.sqrt(NCOND))
-
-    lane = lax.broadcasted_iota(jnp.int32, (32, 128), 1)
+def pick_kernel(pick_ref, val_ref, out_ref, line):
+    chosen = lax.broadcasted_iota(jnp.int32, (8, 256), 1) == pick_ref[0]
+    line[...] = jnp.zeros(line.shape, F32)
+    line[:, 0:PIECE] = lax.dot_general(
+        jnp.where(chosen, 1.0, 0.0).astype(BF16), val_ref[...], (((1,), (1,)), ((), ())), preferred_element_type=F32
+    )
+    row = lax.broadcasted_iota(jnp.int32, (8, 128), 0)
+    piece = line[:, 0:128]
+    for k in range(1, 8):
+        piece = jnp.where(row == k, line[:, 128 * k : 128 * k + 128], piece)
+    piece = piece.astype(BF16)
+    for k in range(64):
+        out_ref[k] = piece
+
+
+def half_grid(core, valence_ref, cond_ref, first_ref, second_ref, val, block):
+    val[...] = valence_ref[...].astype(F32)
+    lane = lax.broadcasted_iota(jnp.int32, (16, 128), 1)
     turned = {}
 
     def turn(piece, row):
         if (piece, row) not in turned:
             at = piece // 4 * 512 + piece % 4 * 8 + row
-            found = jnp.concatenate(
-                [val[pl.ds(at + half * c, 16, stride=32), :] for c in range(2)], axis=0
-            )
+            found = val[pl.ds(at, 16, stride=32), :]
             shift = 104 * piece % 128
             turned[piece, row] = pltpu.roll(found, shift, 1) if shift else found
         return turned[piece, row]
@@ -113,19 +112,33 @@
             for piece, row, begin in segments(m):
                 found = turn(piece, row)
                 valence = found if valence is None else jnp.where(lane >= begin, found, valence)
-            orbital = jnp.concatenate(
-                [cond_ref[pl.ds(m + 125 * c, 16, stride=250), :] for c in range(2)], axis=0
-            )
-            block[32 * n : 32 * n + 32, 128 * t : 128 * t + 128] = (valence * orbital).astype(BF16)
+            orbital = cond_ref[pl.ds(m + 125 * core, 16, stride=250), :]
+            block[16 * n : 16 * n + 16, 128 * t : 128 * t + 128] = (valence * orbital).astype(BF16)
         if n % 5 == 4:
             parts.append(
                 jnp.dot(
-                    block[32 * (n - 4) : 32 * (n + 1), :],
+                    block[16 * (n - 4) : 16 * (n + 1), :],
                     first_ref[...],
                     preferred_element_type=F32,
                 ).astype(BF16)
             )
-    second = jnp.dot(second_ref[...], jnp.concatenate(parts, axis=0), preferred_element_type=F32)
+    return jnp.dot(second_ref[core], jnp.concatenate(parts, axis=0), preferred_element_type=F32)
+
+
+def own_kernel(own_ref, cond_ref, first_ref, second_ref, out_ref, val, block):
+    core = lax.axis_index("core")
+    out_ref[...] = half_grid(core, own_ref, cond_ref, first_ref, second_ref, val, block)
+
+
+def values_kernel(
+    pick_ref, number_ref, val_energy_ref, cond_energy_ref, half_ref, other_ref, cond_ref, chosen_ref, high_ref,
+    first_ref, second_ref, third_ref, out_ref, val, block, rows, scaled,
+):
+    e_val = jnp.full((1, 128), val_energy_ref[pick_ref[0]], F32)
+    e_cond = jnp.full((1, 128), cond_energy_ref[number_ref[0]], F32)
+    weight = 4.0 / ((e_val - e_cond) * math.sqrt(NCOND))
+    core = 1 - lax.axis_index("core")
+    second = half_ref[...] + half_grid(core, other_ref, cond_ref, first_ref, second_ref, val, block)
 
     lane = lax.broadcasted_iota(jnp.int32, (16, 128), 1)
     group = lane // 16
@@ -172,10 +185,9 @@
 
     width = 1280
     place = lax.broadcasted_iota(jnp.int32, (112, width), 0)
-    fetch.wait()
     for c in range(NG // width):
         part = slice(c * width, (c + 1) * width)
-        found = jnp.dot(cube, points[:, part], preferred_element_type=F32)
+        found = jnp.dot(cube, chosen_ref[:, part], preferred_element_type=F32)
         found = jnp.sum(jnp.where(place == high_ref[:, part], found, 0.0), axis=0, keepdims=True)
         found = found.astype(BF16).astype(F32)
         for k in range(width // 128):
@@ -190,12 +202,18 @@
         ).astype(BF16)
 
 
-def chosen_kernel(low_ref, out_ref):
+def chosen_kernel(low_ref, out_ref, done_ref):
     width = 1280
+    done_ref[...] = jnp.zeros((8, 128), F32)
     inner = lax.broadcasted_iota(jnp.int32, (256, width), 0)
     for c in range(NG // width):
         part = slice(c * width, (c + 1) * width)
         out_ref[:, part] = jnp.where(inner == low_ref[:, part], 1.0, 0.0).astype(BF16)
+
+
+def spread_kernel(own_ref, done_ref, out_ref):
+    for k in range(4):
+        out_ref[k] = own_ref[...]
 
 
 def pack_kernel(h_ref, out_ref, wide, full):
@@ -236,16 +254,23 @@
     out_ref[...] = chi_ref[...] + times(all_ref[:, 2560:2688], all_ref[:, 0:2560])
 
 
-def finish_kernel(kept_ref, taken_ref, out_ref):
-    out_ref[...] = kept_ref[...] + taken_ref[...]
-
-
-def call(kernel, out, in_specs, scratch=(), mib=16, flops=0, moved=0):
+def finish_kernel(kept_ref, taken_ref, out_ref, total, sent):
+    copies = []
+    for k in range(5):
+        part = pl.ds(16 * k, 16)
+        total[part, :] = kept_ref[part, :] + taken_ref[part, :]
+        copies.append(pltpu.make_async_copy(total.at[part], out_ref.at[part], sent.at[k]))
+        copies[-1].start()
+    for copy in copies:
+        copy.wait()
+
+
+def call(kernel, out, in_specs, scratch=(), mib=16, flops=0, moved=0, where=VMEM):
     return pl.pallas_call(
         kernel,
         out_shape=out,
         in_specs=in_specs,
-        out_specs=jax.tree.map(lambda _: VMEM, out),
+        out_specs=jax.tree.map(lambda _: where, out),
         scratch_shapes=scratch,
         compiler_params=pltpu.CompilerParams(vmem_limit_bytes=mib * 2**20),
         cost_estimate=pl.CostEstimate(flops=flops, bytes_accessed=moved, transcendentals=0),
@@ -254,32 +279,31 @@
 
 def body(cond_orbitals, val_orbitals, val_index, val_energy, cond_energy, band_list, g_index, chi_old):
     shape = jax.ShapeDtypeStruct
-    piece = lax.dynamic_index_in_dim(val_orbitals, val_index[0], 0, keepdims=False)
-    piece = jnp.pad(piece, (0, 24)).reshape(1, 8, 128)
-    own = lax.all_to_all(
-        jnp.broadcast_to(piece, (64, 8, 128)), ("za", "zb", "yl", "yh"), 0, 0, tiled=True
-    )
+    piece = call(pick_kernel, shape((64, 8, 128), BF16), [SMEM, VMEM], [pltpu.VMEM((8, 1024), F32)])(
+        val_index, val_orbitals.T
+    )
+    own = lax.all_to_all(piece, ("za", "zb", "yl", "yh"), 0, 0, tiled=True)
     orbital = cond_orbitals.astype(F32).reshape(4000, 128)
     low, high = index_parts(g_index)
-    chosen = call(chosen_kernel, shape((256, NG), BF16), [VMEM], moved=2**23)(low.reshape(1, NG))
-    chosen = pltpu.with_memory_space_constraint(chosen, pltpu.HBM)
-    own, orbital, chosen, high = lax.optimization_barrier((own, orbital, chosen, high))
-    own = lax.all_to_all(
-        jnp.broadcast_to(own.reshape(1, 512, 128), (4, 512, 128)), "x", 0, 0, tiled=True
-    ).reshape(2048, 128)
+    own, orbital = lax.optimization_barrier((own, orbital))
+    chosen, done = call(chosen_kernel, (shape((256, NG), BF16), shape((8, 128), F32)), [VMEM], moved=2**23)(
+        low.reshape(1, NG)
+    )
+    spread = call(spread_kernel, shape((4, 512, 128), BF16), [VMEM] * 2)(own.reshape(512, 128), done)
+    own = lax.all_to_all(spread, "x", 0, 0, tiled=True).reshape(2048, 128)
     other = lax.ppermute(own, "core", [(0, 1), (1, 0)])
     first, second, third = tables()
+    first, second, third = jnp.asarray(first, BF16), jnp.asarray(second, BF16), jnp.asarray(third, F32)
+    grids = [pltpu.VMEM((2048, 128), F32), pltpu.VMEM((400, 640), BF16)]
+    half = call(own_kernel, shape((320, 256), F32), [VMEM] * 4, grids)(own, orbital, first, second)
     values = call(
         values_kernel,
         shape((16, 40, 128), BF16),
-        [SMEM] * 4 + [VMEM] * 3 + [pl.BlockSpec(memory_space=pltpu.HBM)] + [VMEM] * 4,
-        [pltpu.VMEM((4096, 128), F32), pltpu.VMEM((800, 640), BF16)]
-        + [pltpu.VMEM((80, 128), F32)] * 2
-        + [pltpu.VMEM((256, NG), BF16), pltpu.SemaphoreType.DMA(())],
-        mib=24,
+        [SMEM] * 4 + [VMEM] * 8,
+        grids + [pltpu.VMEM((80, 128), F32)] * 2,
     )(
-        val_index, band_list, val_energy, cond_energy, own, other, orbital, chosen, high.reshape(1, NG),
-        jnp.asarray(first, BF16), jnp.asarray(second, BF16), jnp.asarray(third, F32),
+        val_index, band_list, val_energy, cond_energy, half, other, orbital, chosen, high.reshape(1, NG),
+        first, second, third,
     )
     gathered = lax.all_to_all(values, ("za", "yh"), 0, 0, tiled=True)
     packed = call(
@@ -293,7 +317,13 @@
     given = call(given_kernel, block, [VMEM])(panel)
     taken = lax.ppermute(given, "core", [(0, 1), (1, 0)])
     kept = call(kept_kernel, block, [VMEM] * 2)(panel, chi_old)
-    return call(finish_kernel, block, [VMEM] * 2)(kept, taken)
+    return call(
+        finish_kernel,
+        block,
+        [VMEM] * 2,
+        [pltpu.VMEM((80, 2560), F32), pltpu.SemaphoreType.DMA((5,))],
+        where=pl.BlockSpec(memory_space=pl.ANY),
+    )(kept, taken)
 
 
 def solution(mesh):

time: 105 us -> 104 us (level)
  blocking collectives: 51.4 us -> 53.1 us
  waiting for transfers between devices: 6.85 us -> 5.35 us
  local copies, waits for them, and re-layouts: 4.57 us -> 3.36 us
  Pallas kernels: 9.54 us -> 8.36 us
    broadcast_in_dim x3 -> x0, local copies, waits for them, and re-layouts: 1.66 us -> none  [the longest x1 0.97 us: body(): jnp.broadcast_to(own.reshape(1, 512, 128), (4, 512, 128))]
    pallas_call x3 -> x6, Pallas kernels: 8.62 us -> 7.45 us  [the longest x1 3.4 us: body(): call(values_kernel, shape((16, 40, 128), BF16), [SMEM] * 4 + [VMEM] * 8,...]
    all_to_all x1, blocking collectives: 18.2 us -> 19.3 us  [body(): gathered = lax.all_to_all(values, ('za', 'yh'), 0, 0, tiled=True)]
  transfers between devices with their start and end apart: 3 -> 3, of which waited for: 3 -> 2; matrix products, arithmetic and copies ran while one was open for 4% -> 5% of each run, Pallas kernels for 1% -> 2%
where the time goes in v3:
time: 104 us; the launch traced here: 103 us
  blocking collectives  53.1 us (51%)
  starting transfers between devices  26.8 us (26%)
  Pallas kernels  8.36 us (8%)
  waiting for transfers between devices  5.35 us (5%)
  other arithmetic  4.76 us (5%)
  local copies, waits for them, and re-layouts  3.36 us (3%)
  between operations  1.47 us (1%)
    all_to_all x1, blocking collectives, body(): lax.all_to_all(packed, ('zb', 'yl', 'x'), 0, 0, tiled=True)  22.8 us
    all_to_all x1, blocking collectives, body(): gathered = lax.all_to_all(values, ('za', 'yh'), 0, 0, tiled=True)  19.3 us
    all_to_all x1, starting transfers between devices, body(): own = lax.all_to_all(piece, ('za', 'zb', 'yl', 'yh'), 0, 0, tiled=True)  17.1 us
    all_to_all x1, blocking collectives, body(): own = lax.all_to_all(spread, 'x', 0, 0, tiled=True).reshape(2048, 128)  11 us
    ppermute x1, starting transfers between devices, body(): other = lax.ppermute(own, 'core', [(0, 1), (1, 0)])  5.59 us
    ppermute x1, starting transfers between devices, body(): taken = lax.ppermute(given, 'core', [(0, 1), (1, 0)])  4.03 us
    reshape x1, other arithmetic, body(): orbital = cond_orbitals.astype(F32).reshape(4000, 128)  3.81 us
    all_to_all x1, waiting for transfers between devices, body(): own = lax.all_to_all(piece, ('za', 'zb', 'yl', 'yh'), 0, 0, tiled=True)  3.79 us
  transfers between devices with their start and end apart: 3, of which 2 were waited for; matrix products, arithmetic and copies ran while one was open for 5% of the time, Pallas kernels for 2%

profile of v3, /device:TPU:1, one launch (start us, length us, event | category | flops | bytes accessed | tf_op | source)
XLA Modules:
  0.0 103.2 jit_solution(11149108941852128383)
XLA Ops:
  0.7 0.0 copy-start.5
  0.7 1.0 copy-done.5
  1.7 0.9 shard_map.109
  2.6 17.1 %all-to-all-start = ((bf16[64,8,128]{2,1,0:T(8,128)(2,1)}), bf16[64,8,128]{2,1,0:T(8,128)(2,1)S(1)}, u32[]{:S(2)}, u32[]{:S(2)}) async-start(bf16[64,8,128]{2,1,0:T(8,128)(2,1)} %shard_map.109), calls=%async_computation | async-start | bytes 262144 | tf_op jit(solution)/shard_map/all_to_all | solution.py:285
  19.8 0.9 fusion.5
  20.7 0.9 shard_map.110
  21.6 0.0 copy-start
  21.6 2.3 %copy-done = bf16[256,10240]{1,0:T(8,128)(2,1)} copy-done((bf16[256,10240]{1,0:T(8,128)(2,1)}, bf16[256,10240]{1,0:T(8,128)(2,1)S(1)}, u32[]{:S(2)}) %copy-start) | copy-done | bytes 5242904
  23.9 0.0 copy-start.2
  23.9 0.0 copy-start.3
  23.9 3.8 %reshape.28 = f32[1,512000]{1,0:T(1,128)S(1)} convert(bf16[1,512000]{1,0:T(2,128)(2,1)} %param.11) | non-fusion elementwise | flops 512000 | bytes 3072000 | tf_op jit(solution)/shard_map/reshape | solution.py:286
  27.7 3.8 %all-to-all-done = bf16[64,8,128]{2,1,0:T(8,128)(2,1)S(1)} async-done(((bf16[64,8,128]{2,1,0:T(8,128)(2,1)}), bf16[64,8,128]{2,1,0:T(8,128)(2,1)S(1)}, u32[]{:S(2)}, u32[]{:S(2)}) %all-to-all-start) | async-done | bytes 131104 | tf_op jit(solution)/shard_map/all_to_all | solution.py:285
  31.5 0.0 copy-start.1
  31.5 0.1 shard_map.111
  31.6 11.0 %all_to_all.20 = bf16[4,512,128]{2,1,0:T(8,128)(2,1)S(1)} all-to-all(bf16[4,512,128]{2,1,0:T(8,128)(2,1)S(1)} %shard_map.111), channel_id=1, replica_groups=mesh['za'=4,'zb'=2,'yl'=2,'core'=2,'x'=4,'yh'=4] {'x'}, dimensions={0} | all-to-all | bytes 1048576 | tf_op jit(solution)/shard_map/all_to_all | solution.py:293
  42.6 0.0 copy-start.6
  42.6 0.0 copy-start.7
  42.6 0.0 copy-start.8
  42.6 5.6 %collective-permute-start = (bf16[2048,128]{1,0:T(8,128)(2,1)S(1)}, bf16[2048,128]{1,0:T(8,128)(2,1)S(1)}, u32[]{:S(2)}, u32[]{:S(2)}) collective-permute-start(bf16[2048,128]{1,0:T(8,128)(2,1)S(1)} %bitcast.11), channel_id=1, source_target_pairs={{0,16},{16,0},{1,17},{17,1},{2,18},{18,2},{3,19},{19,3},{4,20},{20... | collective-permute-start | bytes 1572872 | tf_op jit(solution)/shard_map/ppermute | solution.py:294
  48.8 0.0 copy-done.2
  48.8 0.0 copy-done.3
  48.9 1.3 %shard_map.112.half_ref = f32[320,256]{1,0:T(8,128)S(1)} custom-call(bf16[2048,128]{1,0:T(8,128)(2,1)S(1)} %bitcast.12, f32[4000,128]{1,0:T(8,128)S(1)} %bitcast.7, bf16[640,256]{1,0:T(8,128)(2,1)S(1)} %copy-done.3, bf16[2,320,400]{2,1,0:T(8,128)(2,1)S(1)} %copy-done.2), custom_call_target="tpu_custom_call" | custom-call | tf_op jit(solution)/shard_map/pallas_call | solution.py:298
  50.1 0.0 collective-permute-done.other_ref
  50.1 0.0 copy-done.1
  50.2 0.0 copy-done.6
  50.2 0.0 copy-done.7
  50.2 0.0 copy-done.8
  50.2 3.4 %shard_map.113 = bf16[16,40,128]{2,1,0:T(8,128)(2,1)S(1)} custom-call(s32[1]{0:T(128)S(6)} %copy.12.pick_ref, s32[1]{0:T(128)S(6)} %copy.13.number_ref, f32[256]{0:T(256)S(1)} %copy-done.8, f32[512]{0:T(512)S(1)} %copy-done.7, f32[320,256]{1,0:T(8,128)S(1)} %shard_map.112.half_ref, bf16[2048,128]{1,0:T(8,128)(2,1)S(1)} %collective-permute-done.other_ref, ...), custom_call_target="tpu_custom_call" | custom-call | tf_op jit(solution)/shard_map/pallas_call | solution.py:299
  53.6 19.3 %all_to_all.21.h_ref = bf16[16,40,128]{2,1,0:T(8,128)(2,1)S(1)} all-to-all(bf16[16,40,128]{2,1,0:T(8,128)(2,1)S(1)} %shard_map.113), channel_id=1, replica_groups=mesh['za'=4,'zb'=2,'yl'=2,'core'=2,'x'=4,'yh'=4] {'za','yh'}, dimensions={0} | all-to-all | bytes 327680 | tf_op jit(solution)/shard_map/all_to_all | solution.py:308
  72.9 0.2 shard_map.114
  73.1 0.0 copy-start.4
  73.1 22.8 %all_to_all.22 = bf16[16,16,2816]{2,1,0:T(8,128)(2,1)S(1)} all-to-all(bf16[16,16,2816]{2,1,0:T(8,128)(2,1)S(1)} %shard_map.114), channel_id=1, replica_groups=mesh['za'=4,'zb'=2,'yl'=2,'core'=2,'x'=4,'yh'=4] {'zb','yl','x'}, dimensions={0} | all-to-all | bytes 2883584 | tf_op jit(solution)/shard_map/all_to_all | solution.py:315
  95.9 0.4 shard_map.116
  96.2 4.0 %collective-permute-start.1 = (f32[80,2560]{1,0:T(8,128)S(1)}, f32[80,2560]{1,0:T(8,128)S(1)}, u32[]{:S(2)}, u32[]{:S(2)}) collective-permute-start(f32[80,2560]{1,0:T(8,128)S(1)} %shard_map.116), channel_id=1, source_target_pairs={{0,16},{16,0},{1,17},{17,1},{2,18},{18,2},{3,19},{19,3},{4,20},{20... | collective-permute-start | bytes 2457608 | tf_op jit(solution)/shard_map/ppermute | solution.py:318
  100.3 0.0 copy-done.4
  100.3 0.4 shard_map.115.kept_ref
  100.7 1.6 %collective-permute-done.1.taken_ref = f32[80,2560]{1,0:T(8,128)S(1)} collective-permute-done((f32[80,2560]{1,0:T(8,128)S(1)}, f32[80,2560]{1,0:T(8,128)S(1)}, u32[]{:S(2)}, u32[]{:S(2)}) %collective-permute-start.1) | collective-permute-done | bytes 819232 | tf_op jit(solution)/shard_map/ppermute | solution.py:318
  102.2 0.9 shard_map.117
Async XLA Ops:
  0.7 1.0 %copy-start.5 = (bf16[256,1000]{0,1:T(8,128)(2,1)S(1)}, bf16[256,1000]{0,1:T(8,128)(2,1)}, u32[]{:S(2)}) copy-start(bf16[256,1000]{0,1:T(8,128)(2,1)} %param.12) | copy-start | bytes 1536004
  2.6 28.9 %all-to-all-start = ((bf16[64,8,128]{2,1,0:T(8,128)(2,1)}), bf16[64,8,128]{2,1,0:T(8,128)(2,1)S(1)}, u32[]{:S(2)}, u32[]{:S(2)}) async-start(bf16[64,8,128]{2,1,0:T(8,128)(2,1)} %shard_map.109), calls=%async_computation | async-start | bytes 262144 | tf_op jit(solution)/shard_map/all_to_all | solution.py:285
  21.6 2.3 %copy-start = (bf16[256,10240]{1,0:T(8,128)(2,1)}, bf16[256,10240]{1,0:T(8,128)(2,1)S(1)}, u32[]{:S(2)}) copy-start(bf16[256,10240]{1,0:T(8,128)(2,1)S(1)} %get-tuple-element.12.chosen_ref) | copy-start | bytes 15728644
  23.9 25.0 %copy-start.2 = (bf16[2,320,400]{2,1,0:T(8,128)(2,1)S(1)}, bf16[2,320,400]{2,1,0:T(8,128)(2,1)}, u32[]{:S(2)}) copy-start(bf16[2,320,400]{2,1,0:T(8,128)(2,1)} %constant.71.clone.second_ref) | copy-start | bytes 1536004
  23.9 25.0 %copy-start.3 = (bf16[640,256]{1,0:T(8,128)(2,1)S(1)}, bf16[640,256]{1,0:T(8,128)(2,1)}, u32[]{:S(2)}) copy-start(bf16[640,256]{1,0:T(8,128)(2,1)} %constant.70.clone.first_ref) | copy-start | bytes 983044
  31.5 18.7 %copy-start.1 = (bf16[256,10240]{1,0:T(8,128)(2,1)S(1)}, bf16[256,10240]{1,0:T(8,128)(2,1)}, u32[]{:S(2)}) copy-start(bf16[256,10240]{1,0:T(8,128)(2,1)} %copy-done) | copy-start | bytes 15728644
  42.6 7.6 %copy-start.6 = (f32[32,256]{1,0:T(8,128)S(1)}, f32[32,256]{1,0:T(8,128)}, u32[]{:S(2)}) copy-start(f32[32,256]{1,0:T(8,128)} %constant.72.clone.third_ref) | copy-start | bytes 98308
  42.6 7.6 %copy-start.7 = (f32[512]{0:T(512)S(1)}, f32[512]{0:T(512)}, u32[]{:S(2)}) copy-start(f32[512]{0:T(512)} %cond_energy_ref.1) | copy-start | bytes 6148
  42.6 7.6 %copy-start.8 = (f32[256]{0:T(256)S(1)}, f32[256]{0:T(256)}, u32[]{:S(2)}) copy-start(f32[256]{0:T(256)} %val_energy_ref.1) | copy-start | bytes 3076
  42.6 7.5 %collective-permute-start = (bf16[2048,128]{1,0:T(8,128)(2,1)S(1)}, bf16[2048,128]{1,0:T(8,128)(2,1)S(1)}, u32[]{:S(2)}, u32[]{:S(2)}) collective-permute-start(bf16[2048,128]{1,0:T(8,128)(2,1)S(1)} %bitcast.11), channel_id=1, source_target_pairs={{0,16},{16,0},{1,17},{17,1},{2,18},{18,2},{3,19},{19,3},{4,20},{20... | collective-permute-start | bytes 1572872 | tf_op jit(solution)/shard_map/ppermute | solution.py:294
  73.1 27.2 %copy-start.4 = (f32[80,2560]{1,0:T(8,128)S(1)}, f32[80,2560]{1,0:T(8,128)}, u32[]{:S(2)}) copy-start(f32[80,2560]{1,0:T(8,128)} %chi_ref.1) | copy-start | bytes 2457604
  96.2 6.0 %collective-permute-start.1 = (f32[80,2560]{1,0:T(8,128)S(1)}, f32[80,2560]{1,0:T(8,128)S(1)}, u32[]{:S(2)}, u32[]{:S(2)}) collective-permute-start(f32[80,2560]{1,0:T(8,128)S(1)} %shard_map.116), channel_id=1, source_target_pairs={{0,16},{16,0},{1,17},{17,1},{2,18},{18,2},{3,19},{19,3},{4,20},{20... | collective-permute-start | bytes 2457608 | tf_op jit(solution)/shard_map/ppermute | solution.py:318

commit v4 on v3

--- a/solution.py
+++ b/solution.py
@@ -76,19 +76,9 @@
     return low, high
 
 
-def pick_kernel(pick_ref, val_ref, out_ref, line):
-    chosen = lax.broadcasted_iota(jnp.int32, (8, 256), 1) == pick_ref[0]
-    line[...] = jnp.zeros(line.shape, F32)
-    line[:, 0:PIECE] = lax.dot_general(
-        jnp.where(chosen, 1.0, 0.0).astype(BF16), val_ref[...], (((1,), (1,)), ((), ())), preferred_element_type=F32
-    )
-    row = lax.broadcasted_iota(jnp.int32, (8, 128), 0)
-    piece = line[:, 0:128]
-    for k in range(1, 8):
-        piece = jnp.where(row == k, line[:, 128 * k : 128 * k + 128], piece)
-    piece = piece.astype(BF16)
-    for k in range(64):
-        out_ref[k] = piece
+def widen_kernel(cond_ref, out_ref, done_ref):
+    out_ref[...] = cond_ref[...].astype(F32).reshape(out_ref.shape)
+    done_ref[...] = jnp.zeros((8, 128), F32)
 
 
 def half_grid(core, valence_ref, cond_ref, first_ref, second_ref, val, block):
@@ -202,9 +192,8 @@
         ).astype(BF16)
 
 
-def chosen_kernel(low_ref, out_ref, done_ref):
+def chosen_kernel(low_ref, out_ref):
     width = 1280
-    done_ref[...] = jnp.zeros((8, 128), F32)
     inner = lax.broadcasted_iota(jnp.int32, (256, width), 0)
     for c in range(NG // width):
         part = slice(c * width, (c + 1) * width)
@@ -279,16 +268,15 @@
 
 def body(cond_orbitals, val_orbitals, val_index, val_energy, cond_energy, band_list, g_index, chi_old):
     shape = jax.ShapeDtypeStruct
-    piece = call(pick_kernel, shape((64, 8, 128), BF16), [SMEM, VMEM], [pltpu.VMEM((8, 1024), F32)])(
-        val_index, val_orbitals.T
-    )
-    own = lax.all_to_all(piece, ("za", "zb", "yl", "yh"), 0, 0, tiled=True)
-    orbital = cond_orbitals.astype(F32).reshape(4000, 128)
+    piece = lax.dynamic_index_in_dim(val_orbitals, val_index[0], 0, keepdims=False)
+    piece = jnp.pad(piece, (0, 24)).reshape(1, 8, 128)
+    own = lax.all_to_all(
+        jnp.broadcast_to(piece, (64, 8, 128)), ("za", "zb", "yl", "yh"), 0, 0, tiled=True
+    )
+    orbital, done = call(widen_kernel, (shape((4000, 128), F32), shape((8, 128), F32)), [VMEM])(cond_orbitals)
     low, high = index_parts(g_index)
-    own, orbital = lax.optimization_barrier((own, orbital))
-    chosen, done = call(chosen_kernel, (shape((256, NG), BF16), shape((8, 128), F32)), [VMEM], moved=2**23)(
-        low.reshape(1, NG)
-    )
+    own, low, high = lax.optimization_barrier((own, low, high))
+    chosen = call(chosen_kernel, shape((256, NG), BF16), [VMEM])(low.reshape(1, NG))
     spread = call(spread_kernel, shape((4, 512, 128), BF16), [VMEM] * 2)(own.reshape(512, 128), done)
     own = lax.all_to_all(spread, "x", 0, 0, tiled=True).reshape(2048, 128)
     other = lax.ppermute(own, "core", [(0, 1), (1, 0)])

time: 104 us -> 99.6 us (0.958)
  waiting for transfers between devices: 5.35 us -> 11.2 us
  other arithmetic: 4.76 us -> 0.17 us
  blocking collectives: 53.1 us -> 48.8 us
    all_to_all x1, waiting for transfers between devices: 3.79 us -> 9.63 us  [body(): lax.all_to_all(jnp.broadcast_to(piece, (64, 8, 128)), ('za', 'zb', 'yl',...]
    all_to_all x1, blocking collectives: 19.3 us -> 14.9 us  [body(): gathered = lax.all_to_all(values, ('za', 'yh'), 0, 0, tiled=True)]
    reshape x1 -> x0, other arithmetic: 3.81 us -> none  [body(): orbital = cond_orbitals.astype(F32).reshape(4000, 128)]
    unnamed x18, local copies, waits for them, and re-layouts: 3.36 us -> 2.2 us
  transfers between devices with their start and end apart: 3 -> 3, of which waited for: 2 -> 2; matrix products, arithmetic and copies ran while one was open for 5% -> 0% of each run, Pallas kernels for 2% -> 3%
where the time goes in v4:
time: 99.6 us; the launch traced here: 99.2 us
  blocking collectives  48.8 us (49%)
  starting transfers between devices  26.7 us (27%)
  waiting for transfers between devices  11.2 us (11%)
  Pallas kernels  7.69 us (8%)
  local copies, waits for them, and re-layouts  3.13 us (3%)
  between operations  1.55 us (2%)
    all_to_all x1, blocking collectives, body(): lax.all_to_all(packed, ('zb', 'yl', 'x'), 0, 0, tiled=True)  23.1 us
    all_to_all x1, starting transfers between devices, body(): lax.all_to_all(jnp.broadcast_to(piece, (64, 8, 128)), ('za', 'zb', 'yl',...  17.1 us
    all_to_all x1, blocking collectives, body(): gathered = lax.all_to_all(values, ('za', 'yh'), 0, 0, tiled=True)  14.9 us
    all_to_all x1, blocking collectives, body(): own = lax.all_to_all(spread, 'x', 0, 0, tiled=True).reshape(2048, 128)  10.8 us
    all_to_all x1, waiting for transfers between devices, body(): lax.all_to_all(jnp.broadcast_to(piece, (64, 8, 128)), ('za', 'zb', 'yl',...  9.63 us
    ppermute x1, starting transfers between devices, body(): other = lax.ppermute(own, 'core', [(0, 1), (1, 0)])  5.46 us
    ppermute x1, starting transfers between devices, body(): taken = lax.ppermute(given, 'core', [(0, 1), (1, 0)])  4.13 us
    pallas_call x1, Pallas kernels, body(): call(values_kernel, shape((16, 40, 128), BF16), [SMEM] * 4 + [VMEM] * 8,...  3.37 us
  transfers between devices with their start and end apart: 3, of which 2 were waited for; matrix products, arithmetic and copies ran while one was open for 0% of the time, Pallas kernels for 3%

profile of v4, /device:TPU:1, one launch (start us, length us, event | category | flops | bytes accessed | tf_op | source)
XLA Modules:
  0.0 99.2 jit_solution(17667532593568491473)
XLA Ops:
  0.0 0.0 copy-start
  0.0 0.0 copy-start.8
  0.7 0.3 copy-done
  1.1 0.2 dynamic-slice_reduce_fusion
  1.3 0.7 broadcast_in_dim.8
  2.0 17.1 %all-to-all-start = ((bf16[64,8,128]{2,1,0:T(8,128)(2,1)}), bf16[64,8,128]{2,1,0:T(8,128)(2,1)S(1)}, u32[]{:S(2)}, u32[]{:S(2)}) async-start(bf16[64,8,128]{2,1,0:T(8,128)(2,1)} %broadcast_in_dim.8), calls=%async_computation | async-start | bytes 262144 | tf_op jit(solution)/shard_map/all_to_all | solution.py:273
  19.1 0.0 copy-start.2
  19.1 1.6 %copy-done.2 = bf16[1,512000]{1,0:T(2,128)(2,1)S(1)} copy-done((bf16[1,512000]{1,0:T(2,128)(2,1)S(1)}, bf16[1,512000]{1,0:T(2,128)(2,1)}, u32[]{:S(2)}) %copy-start.2) | copy-done | bytes 1024024
  20.7 0.3 shard_map.109
  21.0 0.0 copy-done.8
  21.1 0.2 fusion.5
  21.2 9.6 %all-to-all-done = bf16[64,8,128]{2,1,0:T(8,128)(2,1)S(1)} async-done(((bf16[64,8,128]{2,1,0:T(8,128)(2,1)}), bf16[64,8,128]{2,1,0:T(8,128)(2,1)S(1)}, u32[]{:S(2)}, u32[]{:S(2)}) %all-to-all-start) | async-done | bytes 131104 | tf_op jit(solution)/shard_map/all_to_all | solution.py:273
  30.9 0.1 shard_map.110
  30.9 10.8 %all_to_all.20 = bf16[4,512,128]{2,1,0:T(8,128)(2,1)S(1)} all-to-all(bf16[4,512,128]{2,1,0:T(8,128)(2,1)S(1)} %shard_map.110), channel_id=1, replica_groups=mesh['za'=4,'zb'=2,'yl'=2,'core'=2,'x'=4,'yh'=4] {'x'}, dimensions={0} | all-to-all | bytes 1048576 | tf_op jit(solution)/shard_map/all_to_all | solution.py:281
  41.7 5.5 %collective-permute-start = (bf16[2048,128]{1,0:T(8,128)(2,1)S(1)}, bf16[2048,128]{1,0:T(8,128)(2,1)S(1)}, u32[]{:S(2)}, u32[]{:S(2)}) collective-permute-start(bf16[2048,128]{1,0:T(8,128)(2,1)S(1)} %bitcast.13), channel_id=1, source_target_pairs={{0,16},{16,0},{1,17},{17,1},{2,18},{18,2},{3,19},{19,3},{4,20},{20... | collective-permute-start | bytes 1572872 | tf_op jit(solution)/shard_map/ppermute | solution.py:282
  47.8 0.0 copy-start.1
  47.8 0.0 copy-start.3
  47.8 0.9 shard_map.112.chosen_ref
  48.7 0.0 copy-start.5
  48.7 0.0 copy-start.6
  48.7 0.0 copy-start.7
  48.7 0.2 copy-done.1
  48.9 0.1 copy-done.3
  49.0 1.2 %shard_map.111.half_ref = f32[320,256]{1,0:T(8,128)S(1)} custom-call(bf16[2048,128]{1,0:T(8,128)(2,1)S(1)} %bitcast.14, f32[4000,128]{1,0:T(8,128)S(1)} %get-tuple-element.12.cond_ref, bf16[640,256]{1,0:T(8,128)(2,1)S(1)} %copy-done.3, bf16[2,320,400]{2,1,0:T(8,128)(2,1)S(1)} %copy-done.1), custom_call_target="tpu_custom_call" | custom-call | tf_op jit(solution)/shard_map/pallas_call | solution.py:286
  50.2 0.0 collective-permute-done.other_ref
  50.2 0.0 copy-done.5
  50.2 0.0 copy-done.6
  50.2 0.0 copy-done.7
  50.2 3.4 %shard_map.113 = bf16[16,40,128]{2,1,0:T(8,128)(2,1)S(1)} custom-call(s32[1]{0:T(128)} %copy.12.pick_ref, s32[1]{0:T(128)S(6)} %copy.13.number_ref, f32[256]{0:T(256)S(1)} %copy-done.7, f32[512]{0:T(512)S(1)} %copy-done.6, f32[320,256]{1,0:T(8,128)S(1)} %shard_map.111.half_ref, bf16[2048,128]{1,0:T(8,128)(2,1)S(1)} %collective-permute-done.other_ref, ...), custom_call_target="tpu_custom_call" | custom-call | tf_op jit(solution)/shard_map/pallas_call | solution.py:287
  53.6 14.9 %all_to_all.21.h_ref = bf16[16,40,128]{2,1,0:T(8,128)(2,1)S(1)} all-to-all(bf16[16,40,128]{2,1,0:T(8,128)(2,1)S(1)} %shard_map.113), channel_id=1, replica_groups=mesh['za'=4,'zb'=2,'yl'=2,'core'=2,'x'=4,'yh'=4] {'za','yh'}, dimensions={0} | all-to-all | bytes 327680 | tf_op jit(solution)/shard_map/all_to_all | solution.py:296
  68.5 0.2 shard_map.114
  68.7 0.0 copy-start.4
  68.7 23.1 %all_to_all.22 = bf16[16,16,2816]{2,1,0:T(8,128)(2,1)S(1)} all-to-all(bf16[16,16,2816]{2,1,0:T(8,128)(2,1)S(1)} %shard_map.114), channel_id=1, replica_groups=mesh['za'=4,'zb'=2,'yl'=2,'core'=2,'x'=4,'yh'=4] {'zb','yl','x'}, dimensions={0} | all-to-all | bytes 2883584 | tf_op jit(solution)/shard_map/all_to_all | solution.py:303
  91.8 0.4 shard_map.116
  92.2 4.1 %collective-permute-start.1 = (f32[80,2560]{1,0:T(8,128)S(1)}, f32[80,2560]{1,0:T(8,128)S(1)}, u32[]{:S(2)}, u32[]{:S(2)}) collective-permute-start(f32[80,2560]{1,0:T(8,128)S(1)} %shard_map.116), channel_id=1, source_target_pairs={{0,16},{16,0},{1,17},{17,1},{2,18},{18,2},{3,19},{19,3},{4,20},{20... | collective-permute-start | bytes 2457608 | tf_op jit(solution)/shard_map/ppermute | solution.py:306
  96.3 0.0 copy-done.4
  96.3 0.4 shard_map.115.kept_ref
  96.7 1.6 %collective-permute-done.1.taken_ref = f32[80,2560]{1,0:T(8,128)S(1)} collective-permute-done((f32[80,2560]{1,0:T(8,128)S(1)}, f32[80,2560]{1,0:T(8,128)S(1)}, u32[]{:S(2)}, u32[]{:S(2)}) %collective-permute-start.1) | collective-permute-done | bytes 819232 | tf_op jit(solution)/shard_map/ppermute | solution.py:306
  98.3 0.9 shard_map.117
  (1 shorter events, 0.0 us)
Async XLA Ops:
  0.0 1.1 %copy-start = (bf16[256,1000]{0,1:T(8,128)(2,1)S(1)}, bf16[256,1000]{0,1:T(8,128)(2,1)}, u32[]{:S(2)}) copy-start(bf16[256,1000]{0,1:T(8,128)(2,1)} %param.12) | copy-start | bytes 1536004
  0.0 21.0 %copy-start.8 = (s32[10240]{0:T(1024)S(1)}, s32[10240]{0:T(1024)}, u32[]{:S(2)}) copy-start(s32[10240]{0:T(1024)} %param.17) | copy-start | bytes 122884
  2.0 28.9 %all-to-all-start = ((bf16[64,8,128]{2,1,0:T(8,128)(2,1)}), bf16[64,8,128]{2,1,0:T(8,128)(2,1)S(1)}, u32[]{:S(2)}, u32[]{:S(2)}) async-start(bf16[64,8,128]{2,1,0:T(8,128)(2,1)} %broadcast_in_dim.8), calls=%async_computation | async-start | bytes 262144 | tf_op jit(solution)/shard_map/all_to_all | solution.py:273
  19.1 1.6 %copy-start.2 = (bf16[1,512000]{1,0:T(2,128)(2,1)S(1)}, bf16[1,512000]{1,0:T(2,128)(2,1)}, u32[]{:S(2)}) copy-start(bf16[1,512000]{1,0:T(2,128)(2,1)} %cond_ref.1) | copy-start | bytes 3072004
  41.7 8.5 %collective-permute-start = (bf16[2048,128]{1,0:T(8,128)(2,1)S(1)}, bf16[2048,128]{1,0:T(8,128)(2,1)S(1)}, u32[]{:S(2)}, u32[]{:S(2)}) collective-permute-start(bf16[2048,128]{1,0:T(8,128)(2,1)S(1)} %bitcast.13), channel_id=1, source_target_pairs={{0,16},{16,0},{1,17},{17,1},{2,18},{18,2},{3,19},{19,3},{4,20},{20... | collective-permute-start | bytes 1572872 | tf_op jit(solution)/shard_map/ppermute | solution.py:282
  47.8 1.1 %copy-start.1 = (bf16[2,320,400]{2,1,0:T(8,128)(2,1)S(1)}, bf16[2,320,400]{2,1,0:T(8,128)(2,1)}, u32[]{:S(2)}) copy-start(bf16[2,320,400]{2,1,0:T(8,128)(2,1)} %constant.79.clone.second_ref) | copy-start | bytes 1536004
  47.8 1.2 %copy-start.3 = (bf16[640,256]{1,0:T(8,128)(2,1)S(1)}, bf16[640,256]{1,0:T(8,128)(2,1)}, u32[]{:S(2)}) copy-start(bf16[640,256]{1,0:T(8,128)(2,1)} %constant.78.clone.first_ref) | copy-start | bytes 983044
  48.7 1.5 %copy-start.5 = (f32[32,256]{1,0:T(8,128)S(1)}, f32[32,256]{1,0:T(8,128)}, u32[]{:S(2)}) copy-start(f32[32,256]{1,0:T(8,128)} %constant.80.clone.third_ref) | copy-start | bytes 98308
  48.7 1.5 %copy-start.6 = (f32[512]{0:T(512)S(1)}, f32[512]{0:T(512)}, u32[]{:S(2)}) copy-start(f32[512]{0:T(512)} %cond_energy_ref.1) | copy-start | bytes 6148
  48.7 1.5 %copy-start.7 = (f32[256]{0:T(256)S(1)}, f32[256]{0:T(256)}, u32[]{:S(2)}) copy-start(f32[256]{0:T(256)} %val_energy_ref.1) | copy-start | bytes 3076
  68.7 27.6 %copy-start.4 = (f32[80,2560]{1,0:T(8,128)S(1)}, f32[80,2560]{1,0:T(8,128)}, u32[]{:S(2)}) copy-start(f32[80,2560]{1,0:T(8,128)} %chi_ref.1) | copy-start | bytes 2457604
  92.2 6.1 %collective-permute-start.1 = (f32[80,2560]{1,0:T(8,128)S(1)}, f32[80,2560]{1,0:T(8,128)S(1)}, u32[]{:S(2)}, u32[]{:S(2)}) collective-permute-start(f32[80,2560]{1,0:T(8,128)S(1)} %shard_map.116), channel_id=1, source_target_pairs={{0,16},{16,0},{1,17},{17,1},{2,18},{18,2},{3,19},{19,3},{4,20},{20... | collective-permute-start | bytes 2457608 | tf_op jit(solution)/shard_map/ppermute | solution.py:306

commit v5 on v4

--- a/solution.py
+++ b/solution.py
@@ -192,15 +192,16 @@
         ).astype(BF16)
 
 
-def chosen_kernel(low_ref, out_ref):
+def chosen_kernel(low_ref, out_ref, done_ref):
     width = 1280
+    done_ref[...] = jnp.zeros((8, 128), F32)
     inner = lax.broadcasted_iota(jnp.int32, (256, width), 0)
     for c in range(NG // width):
         part = slice(c * width, (c + 1) * width)
         out_ref[:, part] = jnp.where(inner == low_ref[:, part], 1.0, 0.0).astype(BF16)
 
 
-def spread_kernel(own_ref, done_ref, out_ref):
+def spread_kernel(own_ref, done_ref, also_ref, out_ref):
     for k in range(4):
         out_ref[k] = own_ref[...]
 
@@ -236,7 +237,7 @@
 
 
 def given_kernel(all_ref, out_ref):
-    out_ref[...] = times(all_ref[:, 2688:2816], all_ref[:, 0:2560])
+    out_ref[...] = times(all_ref[:, 2688:2816], all_ref[:, 0:2560]).astype(BF16)
 
 
 def kept_kernel(all_ref, chi_ref, out_ref):
@@ -247,7 +248,7 @@
     copies = []
     for k in range(5):
         part = pl.ds(16 * k, 16)
-        total[part, :] = kept_ref[part, :] + taken_ref[part, :]
+        total[part, :] = kept_ref[part, :] + taken_ref[part, :].astype(F32)
         copies.append(pltpu.make_async_copy(total.at[part], out_ref.at[part], sent.at[k]))
         copies[-1].start()
     for copy in copies:
@@ -275,9 +276,9 @@
     )
     orbital, done = call(widen_kernel, (shape((4000, 128), F32), shape((8, 128), F32)), [VMEM])(cond_orbitals)
     low, high = index_parts(g_index)
-    own, low, high = lax.optimization_barrier((own, low, high))
-    chosen = call(chosen_kernel, shape((256, NG), BF16), [VMEM])(low.reshape(1, NG))
-    spread = call(spread_kernel, shape((4, 512, 128), BF16), [VMEM] * 2)(own.reshape(512, 128), done)
+    chosen, also = call(chosen_kernel, (shape((256, NG), BF16), shape((8, 128), F32)), [VMEM])(low.reshape(1, NG))
+    own, high = lax.optimization_barrier((own, high))
+    spread = call(spread_kernel, shape((4, 512, 128), BF16), [VMEM] * 3)(own.reshape(512, 128), done, also)
     own = lax.all_to_all(spread, "x", 0, 0, tiled=True).reshape(2048, 128)
     other = lax.ppermute(own, "core", [(0, 1), (1, 0)])
     first, second, third = tables()
@@ -302,7 +303,7 @@
     )(gathered)
     panel = lax.all_to_all(packed, ("zb", "yl", "x"), 0, 0, tiled=True).reshape(256, 2816)
     block = shape((80, 2560), F32)
-    given = call(given_kernel, block, [VMEM])(panel)
+    given = call(given_kernel, shape((80, 2560), BF16), [VMEM])(panel)
     taken = lax.ppermute(given, "core", [(0, 1), (1, 0)])
     kept = call(kept_kernel, block, [VMEM] * 2)(panel, chi_old)
     return call(

time: 99.6 us -> 102 us (1.024)
  waiting for transfers between devices: 11.2 us -> 5.91 us
  blocking collectives: 48.8 us -> 51.8 us
  local copies, waits for them, and re-layouts: 3.13 us -> 5.18 us
  other arithmetic: 0.17 us -> 1.56 us
  Pallas kernels: 7.69 us -> 8.78 us
    all_to_all x1, waiting for transfers between devices: 9.63 us -> 4.94 us  [body(): lax.all_to_all(jnp.broadcast_to(piece, (64, 8, 128)), ('za', 'zb', 'yl',...]
    all_to_all x1, blocking collectives: 14.9 us -> 18.1 us  [body(): gathered = lax.all_to_all(values, ('za', 'yh'), 0, 0, tiled=True)]
    unnamed x18 -> x22, local copies, waits for them, and re-layouts: 2.2 us -> 4.24 us
    add x1, other arithmetic: 0.17 us -> 1.56 us  [index_parts(): low = jnp.abs(y) % 2 * 128 + sign * 16 + jnp.abs(z)]
    pallas_call x3, Pallas kernels: 1.28 us -> 2.34 us  [the longest x1 1.12 us: body(): call(spread_kernel, shape((4, 512, 128), BF16), [VMEM] * 3)]
  transfers between devices with their start and end apart: 3 -> 3, of which waited for: 2 -> 2; matrix products, arithmetic and copies ran while one was open for 0% -> 2% of each run, Pallas kernels for 3% -> 3%
where the time goes in v5:
time: 102 us
  blocking collectives  51.8 us (51%)
  starting transfers between devices  27.1 us (27%)
  Pallas kernels  8.78 us (9%)
  waiting for transfers between devices  5.91 us (6%)
  local copies, waits for them, and re-layouts  5.18 us (5%)
  other arithmetic  1.56 us (2%)
  between operations  1.53 us (2%)
    all_to_all x1, blocking collectives, body(): lax.all_to_all(packed, ('zb', 'yl', 'x'), 0, 0, tiled=True)  22.8 us
    all_to_all x1, blocking collectives, body(): gathered = lax.all_to_all(values, ('za', 'yh'), 0, 0, tiled=True)  18.1 us
    all_to_all x1, starting transfers between devices, body(): lax.all_to_all(jnp.broadcast_to(piece, (64, 8, 128)), ('za', 'zb', 'yl',...  17.5 us
    all_to_all x1, blocking collectives, body(): own = lax.all_to_all(spread, 'x', 0, 0, tiled=True).reshape(2048, 128)  10.9 us
    ppermute x1, starting transfers between devices, body(): other = lax.ppermute(own, 'core', [(0, 1), (1, 0)])  5.6 us
    all_to_all x1, waiting for transfers between devices, body(): lax.all_to_all(jnp.broadcast_to(piece, (64, 8, 128)), ('za', 'zb', 'yl',...  4.94 us
    unnamed x22, local copies, waits for them, and re-layouts  4.24 us
    ppermute x1, starting transfers between devices, body(): taken = lax.ppermute(given, 'core', [(0, 1), (1, 0)])  3.99 us
  transfers between devices with their start and end apart: 3, of which 2 were waited for; matrix products, arithmetic and copies ran while one was open for 2% of the time, Pallas kernels for 3%

profile of v5, /device:TPU:1, one launch (start us, length us, event | category | flops | bytes accessed | tf_op | source)
XLA Modules:
  0.0 101.9 jit_solution(18074852942943452345)
XLA Ops:
  0.0 0.0 copy-start
  0.7 0.3 copy-done
  1.1 0.0 copy-start.5
  1.1 0.2 dynamic-slice_reduce_fusion
  1.3 0.7 broadcast_in_dim.8
  2.0 0.0 copy-start.3
  2.0 17.5 %all-to-all-start = ((bf16[64,8,128]{2,1,0:T(8,128)(2,1)}), bf16[64,8,128]{2,1,0:T(8,128)(2,1)}, u32[]{:S(2)}, u32[]{:S(2)}) async-start(bf16[64,8,128]{2,1,0:T(8,128)(2,1)} %broadcast_in_dim.8), calls=%async_computation | async-start | bytes 262144 | tf_op jit(solution)/shard_map/all_to_all | solution.py:274
  19.5 1.6 %fusion.5 = (s32[10240]{0:T(1024)S(1)}, s32[10240]{0:T(1024)}) fusion(s32[10240]{0:T(1024)} %param.17), kind=kLoop, calls=%fused_computation.18 | loop fusion | flops 706560 | bytes 122880 | tf_op jit(solution)/shard_map/add | solution.py:75
  21.1 0.9 shard_map.110
  21.9 0.0 copy-start.1
  22.0 2.3 %copy-done.1 = bf16[256,10240]{1,0:T(8,128)(2,1)} copy-done((bf16[256,10240]{1,0:T(8,128)(2,1)}, bf16[256,10240]{1,0:T(8,128)(2,1)S(1)}, u32[]{:S(2)}) %copy-start.1) | copy-done | bytes 5242904
  24.3 0.0 copy-start.4
  24.3 1.6 %copy-done.4 = bf16[1,512000]{1,0:T(2,128)(2,1)S(1)} copy-done((bf16[1,512000]{1,0:T(2,128)(2,1)S(1)}, bf16[1,512000]{1,0:T(2,128)(2,1)}, u32[]{:S(2)}) %copy-start.4) | copy-done | bytes 1024024
  25.8 0.3 shard_map.109
  26.2 4.9 %all-to-all-done = bf16[64,8,128]{2,1,0:T(8,128)(2,1)} async-done(((bf16[64,8,128]{2,1,0:T(8,128)(2,1)}), bf16[64,8,128]{2,1,0:T(8,128)(2,1)}, u32[]{:S(2)}, u32[]{:S(2)}) %all-to-all-start) | async-done | bytes 131104 | tf_op jit(solution)/shard_map/all_to_all | solution.py:274
  31.1 0.0 copy-start.2
  31.1 1.1 %shard_map.111 = bf16[4,512,128]{2,1,0:T(8,128)(2,1)S(1)} custom-call(bf16[512,128]{1,0:T(8,128)(2,1)} %bitcast.2.own_ref, f32[8,128]{1,0:T(8,128)S(1)} %get-tuple-element.12.done_ref, f32[8,128]{1,0:T(8,128)S(1)} %get-tuple-element.13.also_ref), custom_call_target="tpu_custom_call" | custom-call | tf_op jit(solution)/shard_map/pallas_call | solution.py:281
  32.2 10.9 %all_to_all.20 = bf16[4,512,128]{2,1,0:T(8,128)(2,1)S(1)} all-to-all(bf16[4,512,128]{2,1,0:T(8,128)(2,1)S(1)} %shard_map.111), channel_id=1, replica_groups=mesh['za'=4,'zb'=2,'yl'=2,'core'=2,'x'=4,'yh'=4] {'x'}, dimensions={0} | all-to-all | bytes 1048576 | tf_op jit(solution)/shard_map/all_to_all | solution.py:282
  43.1 0.0 copy-start.7
  43.1 0.0 copy-start.8
  43.1 0.0 copy-start.9
  43.1 0.0 copy-start.10
  43.1 5.6 %collective-permute-start = (bf16[2048,128]{1,0:T(8,128)(2,1)S(1)}, bf16[2048,128]{1,0:T(8,128)(2,1)S(1)}, u32[]{:S(2)}, u32[]{:S(2)}) collective-permute-start(bf16[2048,128]{1,0:T(8,128)(2,1)S(1)} %bitcast.13), channel_id=1, source_target_pairs={{0,16},{16,0},{1,17},{17,1},{2,18},{18,2},{3,19},{19,3},{4,20},{20... | collective-permute-start | bytes 1572872 | tf_op jit(solution)/shard_map/ppermute | solution.py:283
  49.4 0.0 copy-done.5
  49.4 0.0 copy-done.3
  49.4 1.2 %shard_map.112.half_ref = f32[320,256]{1,0:T(8,128)S(1)} custom-call(bf16[2048,128]{1,0:T(8,128)(2,1)S(1)} %bitcast.14, f32[4000,128]{1,0:T(8,128)S(1)} %get-tuple-element.14.cond_ref, bf16[640,256]{1,0:T(8,128)(2,1)S(1)} %copy-done.5, bf16[2,320,400]{2,1,0:T(8,128)(2,1)S(1)} %copy-done.3), custom_call_target="tpu_custom_call" | custom-call | tf_op jit(solution)/shard_map/pallas_call | solution.py:287
  50.7 0.0 collective-permute-done.other_ref
  50.7 0.0 copy-done.2
  50.7 0.0 copy-done.7
  50.7 0.0 copy-done.8
  50.7 0.0 copy-done.9
  50.7 0.0 copy-done.10
  50.7 3.4 %shard_map.113 = bf16[16,40,128]{2,1,0:T(8,128)(2,1)S(1)} custom-call(s32[1]{0:T(128)} %copy.12.pick_ref, s32[1]{0:T(128)S(6)} %copy.13.number_ref, f32[256]{0:T(256)S(1)} %copy-done.10, f32[512]{0:T(512)S(1)} %copy-done.9, f32[320,256]{1,0:T(8,128)S(1)} %shard_map.112.half_ref, bf16[2048,128]{1,0:T(8,128)(2,1)S(1)} %collective-permute-done.other_ref, ...), custom_call_target="tpu_custom_call" | custom-call | tf_op jit(solution)/shard_map/pallas_call | solution.py:288
  54.1 18.1 %all_to_all.21.h_ref = bf16[16,40,128]{2,1,0:T(8,128)(2,1)S(1)} all-to-all(bf16[16,40,128]{2,1,0:T(8,128)(2,1)S(1)} %shard_map.113), channel_id=1, replica_groups=mesh['za'=4,'zb'=2,'yl'=2,'core'=2,'x'=4,'yh'=4] {'za','yh'}, dimensions={0} | all-to-all | bytes 327680 | tf_op jit(solution)/shard_map/all_to_all | solution.py:297
  72.2 0.2 shard_map.114
  72.4 0.0 copy-start.6
  72.4 22.8 %all_to_all.22 = bf16[16,16,2816]{2,1,0:T(8,128)(2,1)S(1)} all-to-all(bf16[16,16,2816]{2,1,0:T(8,128)(2,1)S(1)} %shard_map.114), channel_id=1, replica_groups=mesh['za'=4,'zb'=2,'yl'=2,'core'=2,'x'=4,'yh'=4] {'zb','yl','x'}, dimensions={0} | all-to-all | bytes 2883584 | tf_op jit(solution)/shard_map/all_to_all | solution.py:304
  95.2 0.4 shard_map.116
  95.6 4.0 %collective-permute-start.1 = (bf16[80,2560]{1,0:T(8,128)(2,1)S(1)}, bf16[80,2560]{1,0:T(8,128)(2,1)S(1)}, u32[]{:S(2)}, u32[]{:S(2)}) collective-permute-start(bf16[80,2560]{1,0:T(8,128)(2,1)S(1)} %shard_map.116), channel_id=1, source_target_pairs={{0,16},{16,0},{1,17},{17,1},{2,18},{18,2},{3,19},{19,3},{4,20},{20... | collective-permute-start | bytes 1228808 | tf_op jit(solution)/shard_map/ppermute | solution.py:307
  99.6 0.0 copy-done.6
  99.6 0.4 shard_map.115.kept_ref
  100.0 1.0 collective-permute-done.1.taken_ref
  100.9 0.9 shard_map.117
  (1 shorter events, 0.0 us)
Async XLA Ops:
  0.0 1.1 %copy-start = (bf16[256,1000]{0,1:T(8,128)(2,1)S(1)}, bf16[256,1000]{0,1:T(8,128)(2,1)}, u32[]{:S(2)}) copy-start(bf16[256,1000]{0,1:T(8,128)(2,1)} %param.12) | copy-start | bytes 1536004
  1.1 48.3 %copy-start.5 = (bf16[640,256]{1,0:T(8,128)(2,1)S(1)}, bf16[640,256]{1,0:T(8,128)(2,1)}, u32[]{:S(2)}) copy-start(bf16[640,256]{1,0:T(8,128)(2,1)} %constant.78.clone.first_ref) | copy-start | bytes 983044
  2.0 47.4 %copy-start.3 = (bf16[2,320,400]{2,1,0:T(8,128)(2,1)S(1)}, bf16[2,320,400]{2,1,0:T(8,128)(2,1)}, u32[]{:S(2)}) copy-start(bf16[2,320,400]{2,1,0:T(8,128)(2,1)} %constant.79.clone.second_ref) | copy-start | bytes 1536004
  2.0 29.1 %all-to-all-start = ((bf16[64,8,128]{2,1,0:T(8,128)(2,1)}), bf16[64,8,128]{2,1,0:T(8,128)(2,1)}, u32[]{:S(2)}, u32[]{:S(2)}) async-start(bf16[64,8,128]{2,1,0:T(8,128)(2,1)} %broadcast_in_dim.8), calls=%async_computation | async-start | bytes 262144 | tf_op jit(solution)/shard_map/all_to_all | solution.py:274
  21.9 2.3 %copy-start.1 = (bf16[256,10240]{1,0:T(8,128)(2,1)}, bf16[256,10240]{1,0:T(8,128)(2,1)S(1)}, u32[]{:S(2)}) copy-start(bf16[256,10240]{1,0:T(8,128)(2,1)S(1)} %get-tuple-element.15.chosen_ref) | copy-start | bytes 15728644
  24.3 1.6 %copy-start.4 = (bf16[1,512000]{1,0:T(2,128)(2,1)S(1)}, bf16[1,512000]{1,0:T(2,128)(2,1)}, u32[]{:S(2)}) copy-start(bf16[1,512000]{1,0:T(2,128)(2,1)} %cond_ref.1) | copy-start | bytes 3072004
  31.1 19.6 %copy-start.2 = (bf16[256,10240]{1,0:T(8,128)(2,1)S(1)}, bf16[256,10240]{1,0:T(8,128)(2,1)}, u32[]{:S(2)}) copy-start(bf16[256,10240]{1,0:T(8,128)(2,1)} %copy-done.1) | copy-start | bytes 15728644
  43.1 7.6 %copy-start.7 = (s32[10240]{0:T(1024)S(1)}, s32[10240]{0:T(1024)}, u32[]{:S(2)}) copy-start(s32[10240]{0:T(1024)} %get-tuple-element.16) | copy-start | bytes 122884
  43.1 7.6 %copy-start.8 = (f32[32,256]{1,0:T(8,128)S(1)}, f32[32,256]{1,0:T(8,128)}, u32[]{:S(2)}) copy-start(f32[32,256]{1,0:T(8,128)} %constant.80.clone.third_ref) | copy-start | bytes 98308
  43.1 7.6 %copy-start.9 = (f32[512]{0:T(512)S(1)}, f32[512]{0:T(512)}, u32[]{:S(2)}) copy-start(f32[512]{0:T(512)} %cond_energy_ref.1) | copy-start | bytes 6148
  43.1 7.6 %copy-start.10 = (f32[256]{0:T(256)S(1)}, f32[256]{0:T(256)}, u32[]{:S(2)}) copy-start(f32[256]{0:T(256)} %val_energy_ref.1) | copy-start | bytes 3076
  43.1 7.5 %collective-permute-start = (bf16[2048,128]{1,0:T(8,128)(2,1)S(1)}, bf16[2048,128]{1,0:T(8,128)(2,1)S(1)}, u32[]{:S(2)}, u32[]{:S(2)}) collective-permute-start(bf16[2048,128]{1,0:T(8,128)(2,1)S(1)} %bitcast.13), channel_id=1, source_target_pairs={{0,16},{16,0},{1,17},{17,1},{2,18},{18,2},{3,19},{19,3},{4,20},{20... | collective-permute-start | bytes 1572872 | tf_op jit(solution)/shard_map/ppermute | solution.py:283
  72.4 27.2 %copy-start.6 = (f32[80,2560]{1,0:T(8,128)S(1)}, f32[80,2560]{1,0:T(8,128)}, u32[]{:S(2)}) copy-start(f32[80,2560]{1,0:T(8,128)} %chi_ref.1) | copy-start | bytes 2457604
  95.6 5.3 %collective-permute-start.1 = (bf16[80,2560]{1,0:T(8,128)(2,1)S(1)}, bf16[80,2560]{1,0:T(8,128)(2,1)S(1)}, u32[]{:S(2)}, u32[]{:S(2)}) collective-permute-start(bf16[80,2560]{1,0:T(8,128)(2,1)S(1)} %shard_map.116), channel_id=1, source_target_pairs={{0,16},{16,0},{1,17},{17,1},{2,18},{18,2},{3,19},{19,3},{4,20},{20... | collective-permute-start | bytes 1228808 | tf_op jit(solution)/shard_map/ppermute | solution.py:307

commit v6 on v4

--- a/solution.py
+++ b/solution.py
@@ -20,7 +20,6 @@
 SIZES = (4, 2, 2, 2, 4, 4)
 BAND = ("za", "zb", "yl", "core")
 VMEM = pl.BlockSpec(memory_space=pltpu.VMEM)
-SMEM = pl.BlockSpec(memory_space=pltpu.SMEM)
 
 
 def tables():
@@ -76,20 +75,27 @@
     return low, high
 
 
-def widen_kernel(cond_ref, out_ref, done_ref):
-    out_ref[...] = cond_ref[...].astype(F32).reshape(out_ref.shape)
+def one_of(values_ref, number_ref):
+    match = lax.broadcasted_iota(jnp.int32, values_ref.shape, 1) == number_ref[...]
+    return jnp.sum(jnp.where(match, values_ref[...], 0.0), axis=1, keepdims=True)
+
+
+def widen_kernel(cond_ref, out_ref, done_ref, wide):
+    wide[...] = cond_ref[...].astype(F32).reshape(wide.shape)
+    for core in range(2):
+        for m in range(125):
+            out_ref[core, m] = wide[pl.ds(m + 125 * core, 16, stride=250), :]
     done_ref[...] = jnp.zeros((8, 128), F32)
 
 
-def half_grid(core, valence_ref, cond_ref, first_ref, second_ref, val, block):
-    val[...] = valence_ref[...].astype(F32)
+def half_grid(core, valence_ref, cond_ref, first_ref, second_ref, block):
     lane = lax.broadcasted_iota(jnp.int32, (16, 128), 1)
     turned = {}
 
     def turn(piece, row):
         if (piece, row) not in turned:
-            at = piece // 4 * 512 + piece % 4 * 8 + row
-            found = val[pl.ds(at, 16, stride=32), :]
+            at = 128 * piece + 16 * row
+            found = valence_ref[at : at + 16, :].astype(F32)
             shift = 104 * piece % 128
             turned[piece, row] = pltpu.roll(found, shift, 1) if shift else found
         return turned[piece, row]
@@ -102,8 +108,7 @@
             for piece, row, begin in segments(m):
                 found = turn(piece, row)
                 valence = found if valence is None else jnp.where(lane >= begin, found, valence)
-            orbital = cond_ref[pl.ds(m + 125 * core, 16, stride=250), :]
-            block[16 * n : 16 * n + 16, 128 * t : 128 * t + 128] = (valence * orbital).astype(BF16)
+            block[16 * n : 16 * n + 16, 128 * t : 128 * t + 128] = (valence * cond_ref[core, m]).astype(BF16)
         if n % 5 == 4:
             parts.append(
                 jnp.dot(
@@ -115,20 +120,23 @@
     return jnp.dot(second_ref[core], jnp.concatenate(parts, axis=0), preferred_element_type=F32)
 
 
-def own_kernel(own_ref, cond_ref, first_ref, second_ref, out_ref, val, block):
+def own_kernel(
+    own_ref, cond_ref, first_ref, second_ref, pick_ref, number_ref, val_energy_ref, cond_energy_ref,
+    out_ref, weight_ref, block,
+):
     core = lax.axis_index("core")
-    out_ref[...] = half_grid(core, own_ref, cond_ref, first_ref, second_ref, val, block)
+    out_ref[...] = half_grid(core, own_ref, cond_ref, first_ref, second_ref, block)
+    gap = one_of(val_energy_ref, pick_ref) - one_of(cond_energy_ref, number_ref)
+    weight_ref[...] = jnp.broadcast_to(4.0 / (gap * math.sqrt(NCOND)), weight_ref.shape)
 
 
 def values_kernel(
-    pick_ref, number_ref, val_energy_ref, cond_energy_ref, half_ref, other_ref, cond_ref, chosen_ref, high_ref,
-    first_ref, second_ref, third_ref, out_ref, val, block, rows, scaled,
+    weight_ref, half_ref, other_ref, cond_ref, chosen_ref, high_ref, first_ref, second_ref,
+    third_ref, out_ref, block, rows, scaled,
 ):
-    e_val = jnp.full((1, 128), val_energy_ref[pick_ref[0]], F32)
-    e_cond = jnp.full((1, 128), cond_energy_ref[number_ref[0]], F32)
-    weight = 4.0 / ((e_val - e_cond) * math.sqrt(NCOND))
+    weight = weight_ref[0:1, :]
     core = 1 - lax.axis_index("core")
-    second = half_ref[...] + half_grid(core, other_ref, cond_ref, first_ref, second_ref, val, block)
+    second = half_ref[...] + half_grid(core, other_ref, cond_ref, first_ref, second_ref, block)
 
     lane = lax.broadcasted_iota(jnp.int32, (16, 128), 1)
     group = lane // 16
@@ -200,9 +208,12 @@
         out_ref[:, part] = jnp.where(inner == low_ref[:, part], 1.0, 0.0).astype(BF16)
 
 
-def spread_kernel(own_ref, done_ref, out_ref):
-    for k in range(4):
-        out_ref[k] = own_ref[...]
+def spread_kernel(own_ref, done_ref, out_ref, wide):
+    wide[...] = own_ref[...].astype(F32)
+    for m in range(32):
+        found = wide[pl.ds(m, 16, stride=32), :].astype(BF16)
+        for k in range(4):
+            out_ref[k, 16 * m : 16 * m + 16, :] = found
 
 
 def pack_kernel(h_ref, out_ref, wide, full):
@@ -236,7 +247,7 @@
 
 
 def given_kernel(all_ref, out_ref):
-    out_ref[...] = times(all_ref[:, 2688:2816], all_ref[:, 0:2560])
+    out_ref[...] = times(all_ref[:, 2688:2816], all_ref[:, 0:2560]).astype(BF16)
 
 
 def kept_kernel(all_ref, chi_ref, out_ref):
@@ -247,7 +258,7 @@
     copies = []
     for k in range(5):
         part = pl.ds(16 * k, 16)
-        total[part, :] = kept_ref[part, :] + taken_ref[part, :]
+        total[part, :] = kept_ref[part, :] + taken_ref[part, :].astype(F32)
         copies.append(pltpu.make_async_copy(total.at[part], out_ref.at[part], sent.at[k]))
         copies[-1].start()
     for copy in copies:
@@ -273,24 +284,32 @@
     own = lax.all_to_all(
         jnp.broadcast_to(piece, (64, 8, 128)), ("za", "zb", "yl", "yh"), 0, 0, tiled=True
     )
-    orbital, done = call(widen_kernel, (shape((4000, 128), F32), shape((8, 128), F32)), [VMEM])(cond_orbitals)
+    orbital, done = call(
+        widen_kernel,
+        (shape((2, 125, 16, 128), F32), shape((8, 128), F32)),
+        [VMEM],
+        [pltpu.VMEM((4000, 128), F32)],
+    )(cond_orbitals)
     low, high = index_parts(g_index)
     own, low, high = lax.optimization_barrier((own, low, high))
     chosen = call(chosen_kernel, shape((256, NG), BF16), [VMEM])(low.reshape(1, NG))
-    spread = call(spread_kernel, shape((4, 512, 128), BF16), [VMEM] * 2)(own.reshape(512, 128), done)
+    spread = call(spread_kernel, shape((4, 512, 128), BF16), [VMEM] * 2, [pltpu.VMEM((512, 128), F32)])(own.reshape(512, 128), done)
     own = lax.all_to_all(spread, "x", 0, 0, tiled=True).reshape(2048, 128)
     other = lax.ppermute(own, "core", [(0, 1), (1, 0)])
     first, second, third = tables()
     first, second, third = jnp.asarray(first, BF16), jnp.asarray(second, BF16), jnp.asarray(third, F32)
-    grids = [pltpu.VMEM((2048, 128), F32), pltpu.VMEM((400, 640), BF16)]
-    half = call(own_kernel, shape((320, 256), F32), [VMEM] * 4, grids)(own, orbital, first, second)
+    grids = [pltpu.VMEM((400, 640), BF16)]
+    half, weight = call(own_kernel, (shape((320, 256), F32), shape((8, 128), F32)), [VMEM] * 8, grids)(
+        own, orbital, first, second, val_index.reshape(1, 1), band_list.reshape(1, 1), val_energy.reshape(1, -1),
+        cond_energy.reshape(1, -1),
+    )
     values = call(
         values_kernel,
         shape((16, 40, 128), BF16),
-        [SMEM] * 4 + [VMEM] * 8,
+        [VMEM] * 9,
         grids + [pltpu.VMEM((80, 128), F32)] * 2,
     )(
-        val_index, band_list, val_energy, cond_energy, half, other, orbital, chosen, high.reshape(1, NG),
+        weight, half, other, orbital, chosen, high.reshape(1, NG),
         first, second, third,
     )
     gathered = lax.all_to_all(values, ("za", "yh"), 0, 0, tiled=True)
@@ -302,7 +321,7 @@
     )(gathered)
     panel = lax.all_to_all(packed, ("zb", "yl", "x"), 0, 0, tiled=True).reshape(256, 2816)
     block = shape((80, 2560), F32)
-    given = call(given_kernel, block, [VMEM])(panel)
+    given = call(given_kernel, shape((80, 2560), BF16), [VMEM])(panel)
     taken = lax.ppermute(given, "core", [(0, 1), (1, 0)])
     kept = call(kept_kernel, block, [VMEM] * 2)(panel, chi_old)
     return call(

time: 99.6 us -> 97.2 us (0.976)
  Pallas kernels: 7.69 us -> 6.32 us
    pallas_call x5, Pallas kernels: 5.34 us -> 3.98 us  [the longest x1 2.22 us: body(): call(values_kernel, shape((16, 40, 128), BF16), [VMEM] * 9, grids + [pltp...]
where the time goes in v6:
time: 97.2 us; the launch traced here: 96.8 us
  blocking collectives  48.3 us (50%)
  starting transfers between devices  26.9 us (28%)
  waiting for transfers between devices  10.4 us (11%)
  Pallas kernels  6.32 us (7%)
  local copies, waits for them, and re-layouts  3.13 us (3%)
  between operations  1.54 us (2%)
    all_to_all x1, blocking collectives, body(): lax.all_to_all(packed, ('zb', 'yl', 'x'), 0, 0, tiled=True)  22.7 us
    all_to_all x1, starting transfers between devices, body(): lax.all_to_all(jnp.broadcast_to(piece, (64, 8, 128)), ('za', 'zb', 'yl',...  17.1 us
    all_to_all x1, blocking collectives, body(): gathered = lax.all_to_all(values, ('za', 'yh'), 0, 0, tiled=True)  14.8 us
    all_to_all x1, blocking collectives, body(): own = lax.all_to_all(spread, 'x', 0, 0, tiled=True).reshape(2048, 128)  10.8 us
    all_to_all x1, waiting for transfers between devices, body(): lax.all_to_all(jnp.broadcast_to(piece, (64, 8, 128)), ('za', 'zb', 'yl',...  9.41 us
    ppermute x1, starting transfers between devices, body(): other = lax.ppermute(own, 'core', [(0, 1), (1, 0)])  5.46 us
    ppermute x1, starting transfers between devices, body(): taken = lax.ppermute(given, 'core', [(0, 1), (1, 0)])  4.33 us
    pallas_call x1, Pallas kernels, body(): call(values_kernel, shape((16, 40, 128), BF16), [VMEM] * 9, grids + [pltp...  2.22 us
  transfers between devices with their start and end apart: 3, of which 2 were waited for; matrix products, arithmetic and copies ran while one was open for 0% of the time, Pallas kernels for 3%

profile of v6, /device:TPU:1, one launch (start us, length us, event | category | flops | bytes accessed | tf_op | source)
XLA Modules:
  0.0 96.8 jit_solution(4776690766595726271)
XLA Ops:
  0.0 0.0 copy-start
  0.0 0.0 copy-start.8
  0.7 0.3 copy-done
  1.1 0.2 dynamic-slice_reduce_fusion
  1.3 0.7 broadcast_in_dim.8
  2.0 17.1 %all-to-all-start = ((bf16[64,8,128]{2,1,0:T(8,128)(2,1)}), bf16[64,8,128]{2,1,0:T(8,128)(2,1)S(1)}, u32[]{:S(2)}, u32[]{:S(2)}) async-start(bf16[64,8,128]{2,1,0:T(8,128)(2,1)} %broadcast_in_dim.8), calls=%async_computation | async-start | bytes 262144 | tf_op jit(solution)/shard_map/all_to_all | solution.py:284
  19.1 0.0 copy-start.2
  19.1 1.6 %copy-done.2 = bf16[1,512000]{1,0:T(2,128)(2,1)S(1)} copy-done((bf16[1,512000]{1,0:T(2,128)(2,1)S(1)}, bf16[1,512000]{1,0:T(2,128)(2,1)}, u32[]{:S(2)}) %copy-start.2) | copy-done | bytes 1024024
  20.7 0.5 shard_map.109
  21.3 0.0 copy-done.8
  21.3 0.2 fusion.5
  21.5 9.4 %all-to-all-done = bf16[64,8,128]{2,1,0:T(8,128)(2,1)S(1)} async-done(((bf16[64,8,128]{2,1,0:T(8,128)(2,1)}), bf16[64,8,128]{2,1,0:T(8,128)(2,1)S(1)}, u32[]{:S(2)}, u32[]{:S(2)}) %all-to-all-start) | async-done | bytes 131104 | tf_op jit(solution)/shard_map/all_to_all | solution.py:284
  30.9 0.2 shard_map.110
  31.0 10.8 %all_to_all.20 = bf16[4,512,128]{2,1,0:T(8,128)(2,1)S(1)} all-to-all(bf16[4,512,128]{2,1,0:T(8,128)(2,1)S(1)} %shard_map.110), channel_id=1, replica_groups=mesh['za'=4,'zb'=2,'yl'=2,'core'=2,'x'=4,'yh'=4] {'x'}, dimensions={0} | all-to-all | bytes 1048576 | tf_op jit(solution)/shard_map/all_to_all | solution.py:297
  41.8 5.5 %collective-permute-start = (bf16[2048,128]{1,0:T(8,128)(2,1)S(1)}, bf16[2048,128]{1,0:T(8,128)(2,1)S(1)}, u32[]{:S(2)}, u32[]{:S(2)}) collective-permute-start(bf16[2048,128]{1,0:T(8,128)(2,1)S(1)} %bitcast.19), channel_id=1, source_target_pairs={{0,16},{16,0},{1,17},{17,1},{2,18},{18,2},{3,19},{19,3},{4,20},{20... | collective-permute-start | bytes 1572872 | tf_op jit(solution)/shard_map/ppermute | solution.py:298
  47.9 0.0 copy-start.1
  47.9 0.0 copy-start.3
  47.9 0.0 copy-start.6
  48.0 0.0 copy-start.7
  48.0 0.9 shard_map.112.chosen_ref
  48.8 0.0 copy-start.5
  48.8 0.2 copy-done.1
  49.0 0.1 copy-done.3
  49.1 0.0 copy-done.6
  49.1 0.0 copy-done.7
  49.1 0.7 shard_map.111
  49.8 0.0 collective-permute-done.other_ref
  49.8 0.0 copy-done.5
  49.8 2.2 %shard_map.113 = bf16[16,40,128]{2,1,0:T(8,128)(2,1)S(1)} custom-call(f32[8,128]{1,0:T(8,128)S(1)} %get-tuple-element.15.weight_ref, f32[320,256]{1,0:T(8,128)S(1)} %get-tuple-element.16.half_ref, bf16[2048,128]{1,0:T(8,128)(2,1)S(1)} %collective-permute-done.other_ref, f32[2,125,16,128]{3,2,1,0:T(8,128)S(1)} %get-tuple-element.14.cond_ref, ...), custom_call_target="tpu_custom_call" | custom-call | tf_op jit(solution)/shard_map/pallas_call | solution.py:306
  52.0 14.8 %all_to_all.21.h_ref = bf16[16,40,128]{2,1,0:T(8,128)(2,1)S(1)} all-to-all(bf16[16,40,128]{2,1,0:T(8,128)(2,1)S(1)} %shard_map.113), channel_id=1, replica_groups=mesh['za'=4,'zb'=2,'yl'=2,'core'=2,'x'=4,'yh'=4] {'za','yh'}, dimensions={0} | all-to-all | bytes 327680 | tf_op jit(solution)/shard_map/all_to_all | solution.py:315
  66.9 0.2 shard_map.114
  67.1 0.0 copy-start.4
  67.1 22.7 %all_to_all.22 = bf16[16,16,2816]{2,1,0:T(8,128)(2,1)S(1)} all-to-all(bf16[16,16,2816]{2,1,0:T(8,128)(2,1)S(1)} %shard_map.114), channel_id=1, replica_groups=mesh['za'=4,'zb'=2,'yl'=2,'core'=2,'x'=4,'yh'=4] {'zb','yl','x'}, dimensions={0} | all-to-all | bytes 2883584 | tf_op jit(solution)/shard_map/all_to_all | solution.py:322
  89.8 0.4 shard_map.116
  90.2 4.3 %collective-permute-start.1 = (bf16[80,2560]{1,0:T(8,128)(2,1)S(1)}, bf16[80,2560]{1,0:T(8,128)(2,1)S(1)}, u32[]{:S(2)}, u32[]{:S(2)}) collective-permute-start(bf16[80,2560]{1,0:T(8,128)(2,1)S(1)} %shard_map.116), channel_id=1, source_target_pairs={{0,16},{16,0},{1,17},{17,1},{2,18},{18,2},{3,19},{19,3},{4,20},{20... | collective-permute-start | bytes 1228808 | tf_op jit(solution)/shard_map/ppermute | solution.py:325
  94.5 0.0 copy-done.4
  94.5 0.4 shard_map.115.kept_ref
  94.9 1.0 %collective-permute-done.1.taken_ref = bf16[80,2560]{1,0:T(8,128)(2,1)S(1)} collective-permute-done((bf16[80,2560]{1,0:T(8,128)(2,1)S(1)}, bf16[80,2560]{1,0:T(8,128)(2,1)S(1)}, u32[]{:S(2)}, u32[]{:S(2)}) %collective-permute-start.1) | collective-permute-done | bytes 409632 | tf_op jit(solution)/shard_map/ppermute | solution.py:325
  95.9 0.9 shard_map.117
  (1 shorter events, 0.0 us)
Async XLA Ops:
  0.0 1.1 %copy-start = (bf16[256,1000]{0,1:T(8,128)(2,1)S(1)}, bf16[256,1000]{0,1:T(8,128)(2,1)}, u32[]{:S(2)}) copy-start(bf16[256,1000]{0,1:T(8,128)(2,1)} %param.12) | copy-start | bytes 1536004
  0.0 21.3 %copy-start.8 = (s32[10240]{0:T(1024)S(1)}, s32[10240]{0:T(1024)}, u32[]{:S(2)}) copy-start(s32[10240]{0:T(1024)} %param.17) | copy-start | bytes 122884
  2.0 28.9 %all-to-all-start = ((bf16[64,8,128]{2,1,0:T(8,128)(2,1)}), bf16[64,8,128]{2,1,0:T(8,128)(2,1)S(1)}, u32[]{:S(2)}, u32[]{:S(2)}) async-start(bf16[64,8,128]{2,1,0:T(8,128)(2,1)} %broadcast_in_dim.8), calls=%async_computation | async-start | bytes 262144 | tf_op jit(solution)/shard_map/all_to_all | solution.py:284
  19.1 1.6 %copy-start.2 = (bf16[1,512000]{1,0:T(2,128)(2,1)S(1)}, bf16[1,512000]{1,0:T(2,128)(2,1)}, u32[]{:S(2)}) copy-start(bf16[1,512000]{1,0:T(2,128)(2,1)} %cond_ref.1) | copy-start | bytes 3072004
  41.8 8.0 %collective-permute-start = (bf16[2048,128]{1,0:T(8,128)(2,1)S(1)}, bf16[2048,128]{1,0:T(8,128)(2,1)S(1)}, u32[]{:S(2)}, u32[]{:S(2)}) collective-permute-start(bf16[2048,128]{1,0:T(8,128)(2,1)S(1)} %bitcast.19), channel_id=1, source_target_pairs={{0,16},{16,0},{1,17},{17,1},{2,18},{18,2},{3,19},{19,3},{4,20},{20... | collective-permute-start | bytes 1572872 | tf_op jit(solution)/shard_map/ppermute | solution.py:298
  47.9 1.1 %copy-start.1 = (bf16[2,320,400]{2,1,0:T(8,128)(2,1)S(1)}, bf16[2,320,400]{2,1,0:T(8,128)(2,1)}, u32[]{:S(2)}) copy-start(bf16[2,320,400]{2,1,0:T(8,128)(2,1)} %constant.79.clone.second_ref) | copy-start | bytes 1536004
  47.9 1.2 %copy-start.3 = (bf16[640,256]{1,0:T(8,128)(2,1)S(1)}, bf16[640,256]{1,0:T(8,128)(2,1)}, u32[]{:S(2)}) copy-start(bf16[640,256]{1,0:T(8,128)(2,1)} %constant.78.clone.first_ref) | copy-start | bytes 983044
  47.9 1.2 %copy-start.6 = (f32[512]{0:T(512)S(1)}, f32[512]{0:T(512)}, u32[]{:S(2)}) copy-start(f32[512]{0:T(512)} %param.15) | copy-start | bytes 6148
  48.0 1.1 %copy-start.7 = (f32[256]{0:T(256)S(1)}, f32[256]{0:T(256)}, u32[]{:S(2)}) copy-start(f32[256]{0:T(256)} %param.14) | copy-start | bytes 3076
  48.8 1.0 copy-start.5
  67.1 27.5 %copy-start.4 = (f32[80,2560]{1,0:T(8,128)S(1)}, f32[80,2560]{1,0:T(8,128)}, u32[]{:S(2)}) copy-start(f32[80,2560]{1,0:T(8,128)} %chi_ref.1) | copy-start | bytes 2457604
  90.2 5.7 %collective-permute-start.1 = (bf16[80,2560]{1,0:T(8,128)(2,1)S(1)}, bf16[80,2560]{1,0:T(8,128)(2,1)S(1)}, u32[]{:S(2)}, u32[]{:S(2)}) collective-permute-start(bf16[80,2560]{1,0:T(8,128)(2,1)S(1)} %shard_map.116), channel_id=1, source_target_pairs={{0,16},{16,0},{1,17},{17,1},{2,18},{18,2},{3,19},{19,3},{4,20},{20... | collective-permute-start | bytes 1228808 | tf_op jit(solution)/shard_map/ppermute | solution.py:325

commit v7 on v6

--- a/solution.py
+++ b/solution.py
@@ -75,17 +75,17 @@
     return low, high
 
 
-def one_of(values_ref, number_ref):
-    match = lax.broadcasted_iota(jnp.int32, values_ref.shape, 1) == number_ref[...]
+def one_of(values_ref, number):
+    match = lax.broadcasted_iota(jnp.int32, values_ref.shape, 1) == number
     return jnp.sum(jnp.where(match, values_ref[...], 0.0), axis=1, keepdims=True)
 
 
-def widen_kernel(cond_ref, out_ref, done_ref, wide):
+def widen_kernel(cond_ref, number_ref, out_ref, number_out_ref, wide):
     wide[...] = cond_ref[...].astype(F32).reshape(wide.shape)
     for core in range(2):
         for m in range(125):
             out_ref[core, m] = wide[pl.ds(m + 125 * core, 16, stride=250), :]
-    done_ref[...] = jnp.zeros((8, 128), F32)
+    number_out_ref[...] = jnp.broadcast_to(number_ref[...].reshape(1, 1), number_out_ref.shape)
 
 
 def half_grid(core, valence_ref, cond_ref, first_ref, second_ref, block):
@@ -126,7 +126,8 @@
 ):
     core = lax.axis_index("core")
     out_ref[...] = half_grid(core, own_ref, cond_ref, first_ref, second_ref, block)
-    gap = one_of(val_energy_ref, pick_ref) - one_of(cond_energy_ref, number_ref)
+    e_val = one_of(val_energy_ref, pick_ref[...].reshape(1, 1))
+    gap = e_val - one_of(cond_energy_ref, number_ref[0:1, 0:1])
     weight_ref[...] = jnp.broadcast_to(4.0 / (gap * math.sqrt(NCOND)), weight_ref.shape)
 
 
@@ -208,7 +209,7 @@
         out_ref[:, part] = jnp.where(inner == low_ref[:, part], 1.0, 0.0).astype(BF16)
 
 
-def spread_kernel(own_ref, done_ref, out_ref, wide):
+def spread_kernel(own_ref, number_ref, out_ref, wide):
     wide[...] = own_ref[...].astype(F32)
     for m in range(32):
         found = wide[pl.ds(m, 16, stride=32), :].astype(BF16)
@@ -227,7 +228,7 @@
         out_ref[k, :, 0:2560] = cols
         pieces = []
         for c in range(2):
-            begin = 80 * (k // 4 * 8 + 4 * c + k % 4)
+            begin = 80 * (k % 4 * 8 + 4 * c + k // 4)
             first, shift = 2560 + begin // 128 * 128, begin % 128
             found = full[:, first : first + 128]
             if shift:
@@ -284,23 +285,23 @@
     own = lax.all_to_all(
         jnp.broadcast_to(piece, (64, 8, 128)), ("za", "zb", "yl", "yh"), 0, 0, tiled=True
     )
-    orbital, done = call(
+    orbital, number = call(
         widen_kernel,
-        (shape((2, 125, 16, 128), F32), shape((8, 128), F32)),
-        [VMEM],
+        (shape((2, 125, 16, 128), F32), shape((8, 128), jnp.int32)),
+        [VMEM] * 2,
         [pltpu.VMEM((4000, 128), F32)],
-    )(cond_orbitals)
+    )(cond_orbitals, band_list)
     low, high = index_parts(g_index)
     own, low, high = lax.optimization_barrier((own, low, high))
     chosen = call(chosen_kernel, shape((256, NG), BF16), [VMEM])(low.reshape(1, NG))
-    spread = call(spread_kernel, shape((4, 512, 128), BF16), [VMEM] * 2, [pltpu.VMEM((512, 128), F32)])(own.reshape(512, 128), done)
+    spread = call(spread_kernel, shape((4, 512, 128), BF16), [VMEM] * 2, [pltpu.VMEM((512, 128), F32)])(own.reshape(512, 128), number)
     own = lax.all_to_all(spread, "x", 0, 0, tiled=True).reshape(2048, 128)
     other = lax.ppermute(own, "core", [(0, 1), (1, 0)])
     first, second, third = tables()
     first, second, third = jnp.asarray(first, BF16), jnp.asarray(second, BF16), jnp.asarray(third, F32)
     grids = [pltpu.VMEM((400, 640), BF16)]
     half, weight = call(own_kernel, (shape((320, 256), F32), shape((8, 128), F32)), [VMEM] * 8, grids)(
-        own, orbital, first, second, val_index.reshape(1, 1), band_list.reshape(1, 1), val_energy.reshape(1, -1),
+        own, orbital, first, second, val_index, number, val_energy.reshape(1, -1),
         cond_energy.reshape(1, -1),
     )
     values = call(
@@ -319,7 +320,7 @@
         [VMEM],
         [pltpu.VMEM((640, 128), F32), pltpu.VMEM((16, 5120), F32)],
     )(gathered)
-    panel = lax.all_to_all(packed, ("zb", "yl", "x"), 0, 0, tiled=True).reshape(256, 2816)
+    panel = lax.all_to_all(packed, ("x", "zb", "yl"), 0, 0, tiled=True).reshape(256, 2816)
     block = shape((80, 2560), F32)
     given = call(given_kernel, shape((80, 2560), BF16), [VMEM])(panel)
     taken = lax.ppermute(given, "core", [(0, 1), (1, 0)])

time: 97.2 us -> 95.3 us (0.980)
  blocking collectives: 48.3 us -> 45.9 us
  starting transfers between devices: 26.9 us -> 28.1 us
    all_to_all x1, blocking collectives: 22.7 us -> 20.3 us  [body(): lax.all_to_all(packed, ('x', 'zb', 'yl'), 0, 0, tiled=True)]
    ppermute x1, starting transfers between devices: 4.33 us -> 5.49 us  [body(): taken = lax.ppermute(given, 'core', [(0, 1), (1, 0)])]
where the time goes in v7:
time: 95.3 us; the launch traced here: 94.9 us
  blocking collectives  45.9 us (48%)
  starting transfers between devices  28.1 us (29%)
  waiting for transfers between devices  9.73 us (10%)
  Pallas kernels  6.36 us (7%)
  local copies, waits for them, and re-layouts  3.13 us (3%)
  between operations  1.54 us (2%)
    all_to_all x1, blocking collectives, body(): lax.all_to_all(packed, ('x', 'zb', 'yl'), 0, 0, tiled=True)  20.3 us
    all_to_all x1, starting transfers between devices, body(): lax.all_to_all(jnp.broadcast_to(piece, (64, 8, 128)), ('za', 'zb', 'yl',...  17.1 us
    all_to_all x1, blocking collectives, body(): gathered = lax.all_to_all(values, ('za', 'yh'), 0, 0, tiled=True)  14.8 us
    all_to_all x1, blocking collectives, body(): own = lax.all_to_all(spread, 'x', 0, 0, tiled=True).reshape(2048, 128)  10.8 us
    all_to_all x1, waiting for transfers between devices, body(): lax.all_to_all(jnp.broadcast_to(piece, (64, 8, 128)), ('za', 'zb', 'yl',...  8.76 us
    ppermute x1, starting transfers between devices, body(): taken = lax.ppermute(given, 'core', [(0, 1), (1, 0)])  5.49 us
    ppermute x1, starting transfers between devices, body(): other = lax.ppermute(own, 'core', [(0, 1), (1, 0)])  5.46 us
    pallas_call x1, Pallas kernels, body(): call(values_kernel, shape((16, 40, 128), BF16), [VMEM] * 9, grids + [pltp...  2.23 us
  transfers between devices with their start and end apart: 3, of which 2 were waited for; matrix products, arithmetic and copies ran while one was open for 0% of the time, Pallas kernels for 3%

profile of v7, /device:TPU:1, one launch (start us, length us, event | category | flops | bytes accessed | tf_op | source)
XLA Modules:
  0.0 94.9 jit_solution(11575686366446671410)
XLA Ops:
  0.0 0.0 copy-start
  0.0 0.0 copy-start.8
  0.7 0.3 copy-done
  1.1 0.2 dynamic-slice_reduce_fusion
  1.3 0.7 broadcast_in_dim.8
  2.0 17.1 %all-to-all-start = ((bf16[64,8,128]{2,1,0:T(8,128)(2,1)}), bf16[64,8,128]{2,1,0:T(8,128)(2,1)S(1)}, u32[]{:S(2)}, u32[]{:S(2)}) async-start(bf16[64,8,128]{2,1,0:T(8,128)(2,1)} %broadcast_in_dim.8), calls=%async_computation | async-start | bytes 262144 | tf_op jit(solution)/shard_map/all_to_all | solution.py:285
  19.8 0.0 copy-start.2
  19.8 1.6 %copy-done.2 = bf16[1,512000]{1,0:T(2,128)(2,1)S(1)} copy-done((bf16[1,512000]{1,0:T(2,128)(2,1)S(1)}, bf16[1,512000]{1,0:T(2,128)(2,1)}, u32[]{:S(2)}) %copy-start.2) | copy-done | bytes 1024024
  21.4 0.6 shard_map.109
  21.9 0.0 copy-done.8
  21.9 0.2 fusion.5
  22.1 8.8 %all-to-all-done = bf16[64,8,128]{2,1,0:T(8,128)(2,1)S(1)} async-done(((bf16[64,8,128]{2,1,0:T(8,128)(2,1)}), bf16[64,8,128]{2,1,0:T(8,128)(2,1)S(1)}, u32[]{:S(2)}, u32[]{:S(2)}) %all-to-all-start) | async-done | bytes 131104 | tf_op jit(solution)/shard_map/all_to_all | solution.py:285
  30.9 0.2 shard_map.110
  31.0 10.8 %all_to_all.20 = bf16[4,512,128]{2,1,0:T(8,128)(2,1)S(1)} all-to-all(bf16[4,512,128]{2,1,0:T(8,128)(2,1)S(1)} %shard_map.110), channel_id=1, replica_groups=mesh['za'=4,'zb'=2,'yl'=2,'core'=2,'x'=4,'yh'=4] {'x'}, dimensions={0} | all-to-all | bytes 1048576 | tf_op jit(solution)/shard_map/all_to_all | solution.py:298
  41.8 5.5 %collective-permute-start = (bf16[2048,128]{1,0:T(8,128)(2,1)S(1)}, bf16[2048,128]{1,0:T(8,128)(2,1)S(1)}, u32[]{:S(2)}, u32[]{:S(2)}) collective-permute-start(bf16[2048,128]{1,0:T(8,128)(2,1)S(1)} %bitcast.15), channel_id=1, source_target_pairs={{0,16},{16,0},{1,17},{17,1},{2,18},{18,2},{3,19},{19,3},{4,20},{20... | collective-permute-start | bytes 1572872 | tf_op jit(solution)/shard_map/ppermute | solution.py:299
  47.3 0.0 copy-start.1
  47.3 0.0 copy-start.3
  47.3 0.0 copy-start.6
  47.3 0.0 copy-start.7
  47.3 0.9 shard_map.112.chosen_ref
  48.2 0.0 copy-start.5
  48.2 0.2 copy-done.1
  48.4 0.1 copy-done.3
  48.4 0.0 copy-done.6
  48.5 0.0 copy-done.7
  48.5 0.7 shard_map.111
  49.1 0.0 collective-permute-done.other_ref
  49.1 0.0 copy-done.5
  49.2 2.2 %shard_map.113 = bf16[16,40,128]{2,1,0:T(8,128)(2,1)S(1)} custom-call(f32[8,128]{1,0:T(8,128)S(1)} %get-tuple-element.15.weight_ref, f32[320,256]{1,0:T(8,128)S(1)} %get-tuple-element.16.half_ref, bf16[2048,128]{1,0:T(8,128)(2,1)S(1)} %collective-permute-done.other_ref, f32[2,125,16,128]{3,2,1,0:T(8,128)S(1)} %get-tuple-element.14.cond_ref, ...), custom_call_target="tpu_custom_call" | custom-call | tf_op jit(solution)/shard_map/pallas_call | solution.py:307
  51.4 14.8 %all_to_all.21.h_ref = bf16[16,40,128]{2,1,0:T(8,128)(2,1)S(1)} all-to-all(bf16[16,40,128]{2,1,0:T(8,128)(2,1)S(1)} %shard_map.113), channel_id=1, replica_groups=mesh['za'=4,'zb'=2,'yl'=2,'core'=2,'x'=4,'yh'=4] {'za','yh'}, dimensions={0} | all-to-all | bytes 327680 | tf_op jit(solution)/shard_map/all_to_all | solution.py:316
  66.2 0.2 shard_map.114
  66.4 0.0 copy-start.4
  66.5 20.3 %all_to_all.22 = bf16[16,16,2816]{2,1,0:T(8,128)(2,1)S(1)} all-to-all(bf16[16,16,2816]{2,1,0:T(8,128)(2,1)S(1)} %shard_map.114), channel_id=1, replica_groups=mesh['za'=4,'zb'=2,'yl'=2,'core'=2,'x'=4,'yh'=4] {'x','zb','yl'}, dimensions={0} | all-to-all | bytes 2883584 | tf_op jit(solution)/shard_map/all_to_all | solution.py:323
  86.8 0.4 shard_map.116
  87.2 5.5 %collective-permute-start.1 = (bf16[80,2560]{1,0:T(8,128)(2,1)S(1)}, bf16[80,2560]{1,0:T(8,128)(2,1)S(1)}, u32[]{:S(2)}, u32[]{:S(2)}) collective-permute-start(bf16[80,2560]{1,0:T(8,128)(2,1)S(1)} %shard_map.116), channel_id=1, source_target_pairs={{0,16},{16,0},{1,17},{17,1},{2,18},{18,2},{3,19},{19,3},{4,20},{20... | collective-permute-start | bytes 1228808 | tf_op jit(solution)/shard_map/ppermute | solution.py:326
  92.7 0.0 copy-done.4
  92.7 0.4 shard_map.115.kept_ref
  93.0 1.0 %collective-permute-done.1.taken_ref = bf16[80,2560]{1,0:T(8,128)(2,1)S(1)} collective-permute-done((bf16[80,2560]{1,0:T(8,128)(2,1)S(1)}, bf16[80,2560]{1,0:T(8,128)(2,1)S(1)}, u32[]{:S(2)}, u32[]{:S(2)}) %collective-permute-start.1) | collective-permute-done | bytes 409632 | tf_op jit(solution)/shard_map/ppermute | solution.py:326
  94.0 0.9 shard_map.117
  (1 shorter events, 0.0 us)
Async XLA Ops:
  0.0 1.1 %copy-start = (bf16[256,1000]{0,1:T(8,128)(2,1)S(1)}, bf16[256,1000]{0,1:T(8,128)(2,1)}, u32[]{:S(2)}) copy-start(bf16[256,1000]{0,1:T(8,128)(2,1)} %param.12) | copy-start | bytes 1536004
  0.0 21.9 %copy-start.8 = (s32[10240]{0:T(1024)S(1)}, s32[10240]{0:T(1024)}, u32[]{:S(2)}) copy-start(s32[10240]{0:T(1024)} %param.17) | copy-start | bytes 122884
  2.0 28.9 %all-to-all-start = ((bf16[64,8,128]{2,1,0:T(8,128)(2,1)}), bf16[64,8,128]{2,1,0:T(8,128)(2,1)S(1)}, u32[]{:S(2)}, u32[]{:S(2)}) async-start(bf16[64,8,128]{2,1,0:T(8,128)(2,1)} %broadcast_in_dim.8), calls=%async_computation | async-start | bytes 262144 | tf_op jit(solution)/shard_map/all_to_all | solution.py:285
  19.8 1.6 %copy-start.2 = (bf16[1,512000]{1,0:T(2,128)(2,1)S(1)}, bf16[1,512000]{1,0:T(2,128)(2,1)}, u32[]{:S(2)}) copy-start(bf16[1,512000]{1,0:T(2,128)(2,1)} %cond_ref.1) | copy-start | bytes 3072004
  41.8 7.3 %collective-permute-start = (bf16[2048,128]{1,0:T(8,128)(2,1)S(1)}, bf16[2048,128]{1,0:T(8,128)(2,1)S(1)}, u32[]{:S(2)}, u32[]{:S(2)}) collective-permute-start(bf16[2048,128]{1,0:T(8,128)(2,1)S(1)} %bitcast.15), channel_id=1, source_target_pairs={{0,16},{16,0},{1,17},{17,1},{2,18},{18,2},{3,19},{19,3},{4,20},{20... | collective-permute-start | bytes 1572872 | tf_op jit(solution)/shard_map/ppermute | solution.py:299
  47.3 1.1 %copy-start.1 = (bf16[2,320,400]{2,1,0:T(8,128)(2,1)S(1)}, bf16[2,320,400]{2,1,0:T(8,128)(2,1)}, u32[]{:S(2)}) copy-start(bf16[2,320,400]{2,1,0:T(8,128)(2,1)} %constant.79.clone.second_ref) | copy-start | bytes 1536004
  47.3 1.2 %copy-start.3 = (bf16[640,256]{1,0:T(8,128)(2,1)S(1)}, bf16[640,256]{1,0:T(8,128)(2,1)}, u32[]{:S(2)}) copy-start(bf16[640,256]{1,0:T(8,128)(2,1)} %constant.78.clone.first_ref) | copy-start | bytes 983044
  47.3 1.2 %copy-start.6 = (f32[512]{0:T(512)S(1)}, f32[512]{0:T(512)}, u32[]{:S(2)}) copy-start(f32[512]{0:T(512)} %param.15) | copy-start | bytes 6148
  47.3 1.1 %copy-start.7 = (f32[256]{0:T(256)S(1)}, f32[256]{0:T(256)}, u32[]{:S(2)}) copy-start(f32[256]{0:T(256)} %param.14) | copy-start | bytes 3076
  48.2 1.0 %copy-start.5 = (f32[32,256]{1,0:T(8,128)S(1)}, f32[32,256]{1,0:T(8,128)}, u32[]{:S(2)}) copy-start(f32[32,256]{1,0:T(8,128)} %constant.80.clone.third_ref) | copy-start | bytes 98308
  66.4 26.2 %copy-start.4 = (f32[80,2560]{1,0:T(8,128)S(1)}, f32[80,2560]{1,0:T(8,128)}, u32[]{:S(2)}) copy-start(f32[80,2560]{1,0:T(8,128)} %chi_ref.1) | copy-start | bytes 2457604
  87.2 6.9 %collective-permute-start.1 = (bf16[80,2560]{1,0:T(8,128)(2,1)S(1)}, bf16[80,2560]{1,0:T(8,128)(2,1)S(1)}, u32[]{:S(2)}, u32[]{:S(2)}) collective-permute-start(bf16[80,2560]{1,0:T(8,128)(2,1)S(1)} %shard_map.116), channel_id=1, source_target_pairs={{0,16},{16,0},{1,17},{17,1},{2,18},{18,2},{3,19},{19,3},{4,20},{20... | collective-permute-start | bytes 1228808 | tf_op jit(solution)/shard_map/ppermute | solution.py:326

commit v8 on v7

--- a/solution.py
+++ b/solution.py
@@ -195,7 +195,7 @@
             rows[at : at + 1, :] = piece
             scaled[at : at + 1, :] = weight * piece
     for k in range(16):
-        yh, za = k % 4, k // 4
+        yh, za = k // 4, k % 4
         out_ref[k] = jnp.concatenate(
             [rows[20 * yh : 20 * yh + 20, :], scaled[20 * za : 20 * za + 20, :]], axis=0
         ).astype(BF16)
@@ -228,7 +228,7 @@
         out_ref[k, :, 0:2560] = cols
         pieces = []
         for c in range(2):
-            begin = 80 * (k % 4 * 8 + 4 * c + k // 4)
+            begin = 80 * ((k // 2 % 2) * 16 + (k % 2) * 8 + 4 * c + k // 4 % 4)
             first, shift = 2560 + begin // 128 * 128, begin % 128
             found = full[:, first : first + 128]
             if shift:
@@ -313,7 +313,7 @@
         weight, half, other, orbital, chosen, high.reshape(1, NG),
         first, second, third,
     )
-    gathered = lax.all_to_all(values, ("za", "yh"), 0, 0, tiled=True)
+    gathered = lax.all_to_all(values, ("yh", "za"), 0, 0, tiled=True)
     packed = call(
         pack_kernel,
         shape((16, 16, 2816), BF16),

time: 95.3 us -> 95.4 us (level)
  no operation moved by 1% of the time
where the time goes in v8:
time: 95.4 us; the launch traced here: 95 us
  blocking collectives  46 us (48%)
  starting transfers between devices  28.1 us (29%)
  waiting for transfers between devices  9.73 us (10%)
  Pallas kernels  6.36 us (7%)
  local copies, waits for them, and re-layouts  3.13 us (3%)
  between operations  1.54 us (2%)
    all_to_all x1, blocking collectives, body(): lax.all_to_all(packed, ('x', 'zb', 'yl'), 0, 0, tiled=True)  21.1 us
    all_to_all x1, starting transfers between devices, body(): lax.all_to_all(jnp.broadcast_to(piece, (64, 8, 128)), ('za', 'zb', 'yl',...  17.1 us
    all_to_all x1, blocking collectives, body(): gathered = lax.all_to_all(values, ('yh', 'za'), 0, 0, tiled=True)  14.1 us
    all_to_all x1, blocking collectives, body(): own = lax.all_to_all(spread, 'x', 0, 0, tiled=True).reshape(2048, 128)  10.8 us
    all_to_all x1, waiting for transfers between devices, body(): lax.all_to_all(jnp.broadcast_to(piece, (64, 8, 128)), ('za', 'zb', 'yl',...  8.76 us
    ppermute x1, starting transfers between devices, body(): taken = lax.ppermute(given, 'core', [(0, 1), (1, 0)])  5.49 us
    ppermute x1, starting transfers between devices, body(): other = lax.ppermute(own, 'core', [(0, 1), (1, 0)])  5.46 us
    pallas_call x1, Pallas kernels, body(): call(values_kernel, shape((16, 40, 128), BF16), [VMEM] * 9, grids + [pltp...  2.23 us
  transfers between devices with their start and end apart: 3, of which 2 were waited for; matrix products, arithmetic and copies ran while one was open for 0% of the time, Pallas kernels for 3%

profile of v8, /device:TPU:1, one launch (start us, length us, event | category | flops | bytes accessed | tf_op | source)
XLA Modules:
  0.0 95.0 jit_solution(16999428195941839362)
XLA Ops:
  0.0 0.0 copy-start
  0.0 0.0 copy-start.8
  0.7 0.3 copy-done
  1.1 0.2 dynamic-slice_reduce_fusion
  1.3 0.7 broadcast_in_dim.8
  2.0 17.1 %all-to-all-start = ((bf16[64,8,128]{2,1,0:T(8,128)(2,1)}), bf16[64,8,128]{2,1,0:T(8,128)(2,1)S(1)}, u32[]{:S(2)}, u32[]{:S(2)}) async-start(bf16[64,8,128]{2,1,0:T(8,128)(2,1)} %broadcast_in_dim.8), calls=%async_computation | async-start | bytes 262144 | tf_op jit(solution)/shard_map/all_to_all | solution.py:285
  19.8 0.0 copy-start.2
  19.8 1.6 %copy-done.2 = bf16[1,512000]{1,0:T(2,128)(2,1)S(1)} copy-done((bf16[1,512000]{1,0:T(2,128)(2,1)S(1)}, bf16[1,512000]{1,0:T(2,128)(2,1)}, u32[]{:S(2)}) %copy-start.2) | copy-done | bytes 1024024
  21.4 0.6 shard_map.109
  21.9 0.0 copy-done.8
  21.9 0.2 fusion.5
  22.1 8.8 %all-to-all-done = bf16[64,8,128]{2,1,0:T(8,128)(2,1)S(1)} async-done(((bf16[64,8,128]{2,1,0:T(8,128)(2,1)}), bf16[64,8,128]{2,1,0:T(8,128)(2,1)S(1)}, u32[]{:S(2)}, u32[]{:S(2)}) %all-to-all-start) | async-done | bytes 131104 | tf_op jit(solution)/shard_map/all_to_all | solution.py:285
  30.9 0.2 shard_map.110
  31.0 10.8 %all_to_all.20 = bf16[4,512,128]{2,1,0:T(8,128)(2,1)S(1)} all-to-all(bf16[4,512,128]{2,1,0:T(8,128)(2,1)S(1)} %shard_map.110), channel_id=1, replica_groups=mesh['za'=4,'zb'=2,'yl'=2,'core'=2,'x'=4,'yh'=4] {'x'}, dimensions={0} | all-to-all | bytes 1048576 | tf_op jit(solution)/shard_map/all_to_all | solution.py:298
  41.8 5.5 %collective-permute-start = (bf16[2048,128]{1,0:T(8,128)(2,1)S(1)}, bf16[2048,128]{1,0:T(8,128)(2,1)S(1)}, u32[]{:S(2)}, u32[]{:S(2)}) collective-permute-start(bf16[2048,128]{1,0:T(8,128)(2,1)S(1)} %bitcast.15), channel_id=1, source_target_pairs={{0,16},{16,0},{1,17},{17,1},{2,18},{18,2},{3,19},{19,3},{4,20},{20... | collective-permute-start | bytes 1572872 | tf_op jit(solution)/shard_map/ppermute | solution.py:299
  47.3 0.0 copy-start.1
  47.3 0.0 copy-start.3
  47.3 0.0 copy-start.6
  47.3 0.0 copy-start.7
  47.3 0.9 shard_map.112.chosen_ref
  48.2 0.0 copy-start.5
  48.2 0.2 copy-done.1
  48.4 0.1 copy-done.3
  48.4 0.0 copy-done.6
  48.5 0.0 copy-done.7
  48.5 0.7 shard_map.111
  49.1 0.0 collective-permute-done.other_ref
  49.1 0.0 copy-done.5
  49.2 2.2 %shard_map.113 = bf16[16,40,128]{2,1,0:T(8,128)(2,1)S(1)} custom-call(f32[8,128]{1,0:T(8,128)S(1)} %get-tuple-element.15.weight_ref, f32[320,256]{1,0:T(8,128)S(1)} %get-tuple-element.16.half_ref, bf16[2048,128]{1,0:T(8,128)(2,1)S(1)} %collective-permute-done.other_ref, f32[2,125,16,128]{3,2,1,0:T(8,128)S(1)} %get-tuple-element.14.cond_ref, ...), custom_call_target="tpu_custom_call" | custom-call | tf_op jit(solution)/shard_map/pallas_call | solution.py:307
  51.4 14.1 %all_to_all.21.h_ref = bf16[16,40,128]{2,1,0:T(8,128)(2,1)S(1)} all-to-all(bf16[16,40,128]{2,1,0:T(8,128)(2,1)S(1)} %shard_map.113), channel_id=1, replica_groups=mesh['za'=4,'zb'=2,'yl'=2,'core'=2,'x'=4,'yh'=4] {'yh','za'}, dimensions={0} | all-to-all | bytes 327680 | tf_op jit(solution)/shard_map/all_to_all | solution.py:316
  65.5 0.2 shard_map.114
  65.7 0.0 copy-start.4
  65.7 21.1 %all_to_all.22 = bf16[16,16,2816]{2,1,0:T(8,128)(2,1)S(1)} all-to-all(bf16[16,16,2816]{2,1,0:T(8,128)(2,1)S(1)} %shard_map.114), channel_id=1, replica_groups=mesh['za'=4,'zb'=2,'yl'=2,'core'=2,'x'=4,'yh'=4] {'x','zb','yl'}, dimensions={0} | all-to-all | bytes 2883584 | tf_op jit(solution)/shard_map/all_to_all | solution.py:323
  86.9 0.4 shard_map.116
  87.2 5.5 %collective-permute-start.1 = (bf16[80,2560]{1,0:T(8,128)(2,1)S(1)}, bf16[80,2560]{1,0:T(8,128)(2,1)S(1)}, u32[]{:S(2)}, u32[]{:S(2)}) collective-permute-start(bf16[80,2560]{1,0:T(8,128)(2,1)S(1)} %shard_map.116), channel_id=1, source_target_pairs={{0,16},{16,0},{1,17},{17,1},{2,18},{18,2},{3,19},{19,3},{4,20},{20... | collective-permute-start | bytes 1228808 | tf_op jit(solution)/shard_map/ppermute | solution.py:326
  92.7 0.0 copy-done.4
  92.8 0.4 shard_map.115.kept_ref
  93.1 1.0 %collective-permute-done.1.taken_ref = bf16[80,2560]{1,0:T(8,128)(2,1)S(1)} collective-permute-done((bf16[80,2560]{1,0:T(8,128)(2,1)S(1)}, bf16[80,2560]{1,0:T(8,128)(2,1)S(1)}, u32[]{:S(2)}, u32[]{:S(2)}) %collective-permute-start.1) | collective-permute-done | bytes 409632 | tf_op jit(solution)/shard_map/ppermute | solution.py:326
  94.1 0.9 shard_map.117
  (1 shorter events, 0.0 us)
Async XLA Ops:
  0.0 1.1 %copy-start = (bf16[256,1000]{0,1:T(8,128)(2,1)S(1)}, bf16[256,1000]{0,1:T(8,128)(2,1)}, u32[]{:S(2)}) copy-start(bf16[256,1000]{0,1:T(8,128)(2,1)} %param.12) | copy-start | bytes 1536004
  0.0 21.9 %copy-start.8 = (s32[10240]{0:T(1024)S(1)}, s32[10240]{0:T(1024)}, u32[]{:S(2)}) copy-start(s32[10240]{0:T(1024)} %param.17) | copy-start | bytes 122884
  2.0 28.9 %all-to-all-start = ((bf16[64,8,128]{2,1,0:T(8,128)(2,1)}), bf16[64,8,128]{2,1,0:T(8,128)(2,1)S(1)}, u32[]{:S(2)}, u32[]{:S(2)}) async-start(bf16[64,8,128]{2,1,0:T(8,128)(2,1)} %broadcast_in_dim.8), calls=%async_computation | async-start | bytes 262144 | tf_op jit(solution)/shard_map/all_to_all | solution.py:285
  19.8 1.6 %copy-start.2 = (bf16[1,512000]{1,0:T(2,128)(2,1)S(1)}, bf16[1,512000]{1,0:T(2,128)(2,1)}, u32[]{:S(2)}) copy-start(bf16[1,512000]{1,0:T(2,128)(2,1)} %cond_ref.1) | copy-start | bytes 3072004
  41.8 7.3 %collective-permute-start = (bf16[2048,128]{1,0:T(8,128)(2,1)S(1)}, bf16[2048,128]{1,0:T(8,128)(2,1)S(1)}, u32[]{:S(2)}, u32[]{:S(2)}) collective-permute-start(bf16[2048,128]{1,0:T(8,128)(2,1)S(1)} %bitcast.15), channel_id=1, source_target_pairs={{0,16},{16,0},{1,17},{17,1},{2,18},{18,2},{3,19},{19,3},{4,20},{20... | collective-permute-start | bytes 1572872 | tf_op jit(solution)/shard_map/ppermute | solution.py:299
  47.3 1.1 %copy-start.1 = (bf16[2,320,400]{2,1,0:T(8,128)(2,1)S(1)}, bf16[2,320,400]{2,1,0:T(8,128)(2,1)}, u32[]{:S(2)}) copy-start(bf16[2,320,400]{2,1,0:T(8,128)(2,1)} %constant.79.clone.second_ref) | copy-start | bytes 1536004
  47.3 1.2 %copy-start.3 = (bf16[640,256]{1,0:T(8,128)(2,1)S(1)}, bf16[640,256]{1,0:T(8,128)(2,1)}, u32[]{:S(2)}) copy-start(bf16[640,256]{1,0:T(8,128)(2,1)} %constant.78.clone.first_ref) | copy-start | bytes 983044
  47.3 1.2 %copy-start.6 = (f32[512]{0:T(512)S(1)}, f32[512]{0:T(512)}, u32[]{:S(2)}) copy-start(f32[512]{0:T(512)} %param.15) | copy-start | bytes 6148
  47.3 1.1 %copy-start.7 = (f32[256]{0:T(256)S(1)}, f32[256]{0:T(256)}, u32[]{:S(2)}) copy-start(f32[256]{0:T(256)} %param.14) | copy-start | bytes 3076
  48.2 1.0 %copy-start.5 = (f32[32,256]{1,0:T(8,128)S(1)}, f32[32,256]{1,0:T(8,128)}, u32[]{:S(2)}) copy-start(f32[32,256]{1,0:T(8,128)} %constant.80.clone.third_ref) | copy-start | bytes 98308
  65.7 27.0 %copy-start.4 = (f32[80,2560]{1,0:T(8,128)S(1)}, f32[80,2560]{1,0:T(8,128)}, u32[]{:S(2)}) copy-start(f32[80,2560]{1,0:T(8,128)} %chi_ref.1) | copy-start | bytes 2457604
  87.2 6.9 %collective-permute-start.1 = (bf16[80,2560]{1,0:T(8,128)(2,1)S(1)}, bf16[80,2560]{1,0:T(8,128)(2,1)S(1)}, u32[]{:S(2)}, u32[]{:S(2)}) collective-permute-start(bf16[80,2560]{1,0:T(8,128)(2,1)S(1)} %shard_map.116), channel_id=1, source_target_pairs={{0,16},{16,0},{1,17},{17,1},{2,18},{18,2},{3,19},{19,3},{4,20},{20... | collective-permute-start | bytes 1228808 | tf_op jit(solution)/shard_map/ppermute | solution.py:326

commit v9 on v7

--- a/solution.py
+++ b/solution.py
@@ -193,7 +193,7 @@
             at = c * (width // 128) + k
             piece = found[:, 128 * k : 128 * k + 128]
             rows[at : at + 1, :] = piece
-            scaled[at : at + 1, :] = weight * piece
+    scaled[...] = weight * rows[...]
     for k in range(16):
         yh, za = k % 4, k // 4
         out_ref[k] = jnp.concatenate(

time: 95.3 us -> 95.3 us (level)
  no operation moved by 1% of the time
where the time goes in v9:
time: 95.3 us; the launch traced here: 94.9 us
  blocking collectives  45.9 us (48%)
  starting transfers between devices  28.1 us (29%)
  waiting for transfers between devices  9.73 us (10%)
  Pallas kernels  6.35 us (7%)
  local copies, waits for them, and re-layouts  3.13 us (3%)
  between operations  1.53 us (2%)
    all_to_all x1, blocking collectives, body(): lax.all_to_all(packed, ('x', 'zb', 'yl'), 0, 0, tiled=True)  20.3 us
    all_to_all x1, starting transfers between devices, body(): lax.all_to_all(jnp.broadcast_to(piece, (64, 8, 128)), ('za', 'zb', 'yl',...  17.1 us
    all_to_all x1, blocking collectives, body(): gathered = lax.all_to_all(values, ('za', 'yh'), 0, 0, tiled=True)  14.8 us
    all_to_all x1, blocking collectives, body(): own = lax.all_to_all(spread, 'x', 0, 0, tiled=True).reshape(2048, 128)  10.8 us
    all_to_all x1, waiting for transfers between devices, body(): lax.all_to_all(jnp.broadcast_to(piece, (64, 8, 128)), ('za', 'zb', 'yl',...  8.76 us
    ppermute x1, starting transfers between devices, body(): taken = lax.ppermute(given, 'core', [(0, 1), (1, 0)])  5.49 us
    ppermute x1, starting transfers between devices, body(): other = lax.ppermute(own, 'core', [(0, 1), (1, 0)])  5.46 us
    pallas_call x1, Pallas kernels, body(): call(values_kernel, shape((16, 40, 128), BF16), [VMEM] * 9, grids + [pltp...  2.21 us
  transfers between devices with their start and end apart: 3, of which 2 were waited for; matrix products, arithmetic and copies ran while one was open for 0% of the time, Pallas kernels for 3%

profile of v9, /device:TPU:1, one launch (start us, length us, event | category | flops | bytes accessed | tf_op | source)
XLA Modules:
  0.0 94.9 jit_solution(11078785064844074991)
XLA Ops:
  0.0 0.0 copy-start
  0.0 0.0 copy-start.8
  0.7 0.3 copy-done
  1.1 0.2 dynamic-slice_reduce_fusion
  1.3 0.7 broadcast_in_dim.8
  2.0 17.1 %all-to-all-start = ((bf16[64,8,128]{2,1,0:T(8,128)(2,1)}), bf16[64,8,128]{2,1,0:T(8,128)(2,1)S(1)}, u32[]{:S(2)}, u32[]{:S(2)}) async-start(bf16[64,8,128]{2,1,0:T(8,128)(2,1)} %broadcast_in_dim.8), calls=%async_computation | async-start | bytes 262144 | tf_op jit(solution)/shard_map/all_to_all | solution.py:285
  19.8 0.0 copy-start.2
  19.8 1.6 %copy-done.2 = bf16[1,512000]{1,0:T(2,128)(2,1)S(1)} copy-done((bf16[1,512000]{1,0:T(2,128)(2,1)S(1)}, bf16[1,512000]{1,0:T(2,128)(2,1)}, u32[]{:S(2)}) %copy-start.2) | copy-done | bytes 1024024
  21.4 0.6 shard_map.109
  21.9 0.0 copy-done.8
  21.9 0.2 fusion.5
  22.1 8.8 %all-to-all-done = bf16[64,8,128]{2,1,0:T(8,128)(2,1)S(1)} async-done(((bf16[64,8,128]{2,1,0:T(8,128)(2,1)}), bf16[64,8,128]{2,1,0:T(8,128)(2,1)S(1)}, u32[]{:S(2)}, u32[]{:S(2)}) %all-to-all-start) | async-done | bytes 131104 | tf_op jit(solution)/shard_map/all_to_all | solution.py:285
  30.9 0.2 shard_map.110
  31.0 10.8 %all_to_all.20 = bf16[4,512,128]{2,1,0:T(8,128)(2,1)S(1)} all-to-all(bf16[4,512,128]{2,1,0:T(8,128)(2,1)S(1)} %shard_map.110), channel_id=1, replica_groups=mesh['za'=4,'zb'=2,'yl'=2,'core'=2,'x'=4,'yh'=4] {'x'}, dimensions={0} | all-to-all | bytes 1048576 | tf_op jit(solution)/shard_map/all_to_all | solution.py:298
  41.8 5.5 %collective-permute-start = (bf16[2048,128]{1,0:T(8,128)(2,1)S(1)}, bf16[2048,128]{1,0:T(8,128)(2,1)S(1)}, u32[]{:S(2)}, u32[]{:S(2)}) collective-permute-start(bf16[2048,128]{1,0:T(8,128)(2,1)S(1)} %bitcast.15), channel_id=1, source_target_pairs={{0,16},{16,0},{1,17},{17,1},{2,18},{18,2},{3,19},{19,3},{4,20},{20... | collective-permute-start | bytes 1572872 | tf_op jit(solution)/shard_map/ppermute | solution.py:299
  47.3 0.0 copy-start.1
  47.3 0.0 copy-start.3
  47.3 0.0 copy-start.6
  47.3 0.0 copy-start.7
  47.3 0.9 shard_map.112.chosen_ref
  48.2 0.0 copy-start.5
  48.2 0.2 copy-done.1
  48.4 0.1 copy-done.3
  48.4 0.0 copy-done.6
  48.5 0.0 copy-done.7
  48.5 0.7 shard_map.111
  49.1 0.0 collective-permute-done.other_ref
  49.1 0.0 copy-done.5
  49.2 2.2 %shard_map.113 = bf16[16,40,128]{2,1,0:T(8,128)(2,1)S(1)} custom-call(f32[8,128]{1,0:T(8,128)S(1)} %get-tuple-element.15.weight_ref, f32[320,256]{1,0:T(8,128)S(1)} %get-tuple-element.16.half_ref, bf16[2048,128]{1,0:T(8,128)(2,1)S(1)} %collective-permute-done.other_ref, f32[2,125,16,128]{3,2,1,0:T(8,128)S(1)} %get-tuple-element.14.cond_ref, ...), custom_call_target="tpu_custom_call" | custom-call | tf_op jit(solution)/shard_map/pallas_call | solution.py:307
  51.4 14.8 %all_to_all.21.h_ref = bf16[16,40,128]{2,1,0:T(8,128)(2,1)S(1)} all-to-all(bf16[16,40,128]{2,1,0:T(8,128)(2,1)S(1)} %shard_map.113), channel_id=1, replica_groups=mesh['za'=4,'zb'=2,'yl'=2,'core'=2,'x'=4,'yh'=4] {'za','yh'}, dimensions={0} | all-to-all | bytes 327680 | tf_op jit(solution)/shard_map/all_to_all | solution.py:316
  66.2 0.2 shard_map.114
  66.4 0.0 copy-start.4
  66.4 20.3 %all_to_all.22 = bf16[16,16,2816]{2,1,0:T(8,128)(2,1)S(1)} all-to-all(bf16[16,16,2816]{2,1,0:T(8,128)(2,1)S(1)} %shard_map.114), channel_id=1, replica_groups=mesh['za'=4,'zb'=2,'yl'=2,'core'=2,'x'=4,'yh'=4] {'x','zb','yl'}, dimensions={0} | all-to-all | bytes 2883584 | tf_op jit(solution)/shard_map/all_to_all | solution.py:323
  86.8 0.4 shard_map.116
  87.1 5.5 %collective-permute-start.1 = (bf16[80,2560]{1,0:T(8,128)(2,1)S(1)}, bf16[80,2560]{1,0:T(8,128)(2,1)S(1)}, u32[]{:S(2)}, u32[]{:S(2)}) collective-permute-start(bf16[80,2560]{1,0:T(8,128)(2,1)S(1)} %shard_map.116), channel_id=1, source_target_pairs={{0,16},{16,0},{1,17},{17,1},{2,18},{18,2},{3,19},{19,3},{4,20},{20... | collective-permute-start | bytes 1228808 | tf_op jit(solution)/shard_map/ppermute | solution.py:326
  92.6 0.0 copy-done.4
  92.6 0.4 shard_map.115.kept_ref
  93.0 1.0 %collective-permute-done.1.taken_ref = bf16[80,2560]{1,0:T(8,128)(2,1)S(1)} collective-permute-done((bf16[80,2560]{1,0:T(8,128)(2,1)S(1)}, bf16[80,2560]{1,0:T(8,128)(2,1)S(1)}, u32[]{:S(2)}, u32[]{:S(2)}) %collective-permute-start.1) | collective-permute-done | bytes 409632 | tf_op jit(solution)/shard_map/ppermute | solution.py:326
  94.0 0.9 shard_map.117
  (1 shorter events, 0.0 us)
Async XLA Ops:
  0.0 1.1 %copy-start = (bf16[256,1000]{0,1:T(8,128)(2,1)S(1)}, bf16[256,1000]{0,1:T(8,128)(2,1)}, u32[]{:S(2)}) copy-start(bf16[256,1000]{0,1:T(8,128)(2,1)} %param.12) | copy-start | bytes 1536004
  0.0 21.9 %copy-start.8 = (s32[10240]{0:T(1024)S(1)}, s32[10240]{0:T(1024)}, u32[]{:S(2)}) copy-start(s32[10240]{0:T(1024)} %param.17) | copy-start | bytes 122884
  2.0 28.9 %all-to-all-start = ((bf16[64,8,128]{2,1,0:T(8,128)(2,1)}), bf16[64,8,128]{2,1,0:T(8,128)(2,1)S(1)}, u32[]{:S(2)}, u32[]{:S(2)}) async-start(bf16[64,8,128]{2,1,0:T(8,128)(2,1)} %broadcast_in_dim.8), calls=%async_computation | async-start | bytes 262144 | tf_op jit(solution)/shard_map/all_to_all | solution.py:285
  19.8 1.6 %copy-start.2 = (bf16[1,512000]{1,0:T(2,128)(2,1)S(1)}, bf16[1,512000]{1,0:T(2,128)(2,1)}, u32[]{:S(2)}) copy-start(bf16[1,512000]{1,0:T(2,128)(2,1)} %cond_ref.1) | copy-start | bytes 3072004
  41.8 7.3 %collective-permute-start = (bf16[2048,128]{1,0:T(8,128)(2,1)S(1)}, bf16[2048,128]{1,0:T(8,128)(2,1)S(1)}, u32[]{:S(2)}, u32[]{:S(2)}) collective-permute-start(bf16[2048,128]{1,0:T(8,128)(2,1)S(1)} %bitcast.15), channel_id=1, source_target_pairs={{0,16},{16,0},{1,17},{17,1},{2,18},{18,2},{3,19},{19,3},{4,20},{20... | collective-permute-start | bytes 1572872 | tf_op jit(solution)/shard_map/ppermute | solution.py:299
  47.3 1.1 %copy-start.1 = (bf16[2,320,400]{2,1,0:T(8,128)(2,1)S(1)}, bf16[2,320,400]{2,1,0:T(8,128)(2,1)}, u32[]{:S(2)}) copy-start(bf16[2,320,400]{2,1,0:T(8,128)(2,1)} %constant.79.clone.second_ref) | copy-start | bytes 1536004
  47.3 1.2 %copy-start.3 = (bf16[640,256]{1,0:T(8,128)(2,1)S(1)}, bf16[640,256]{1,0:T(8,128)(2,1)}, u32[]{:S(2)}) copy-start(bf16[640,256]{1,0:T(8,128)(2,1)} %constant.78.clone.first_ref) | copy-start | bytes 983044
  47.3 1.2 %copy-start.6 = (f32[512]{0:T(512)S(1)}, f32[512]{0:T(512)}, u32[]{:S(2)}) copy-start(f32[512]{0:T(512)} %param.15) | copy-start | bytes 6148
  47.3 1.1 %copy-start.7 = (f32[256]{0:T(256)S(1)}, f32[256]{0:T(256)}, u32[]{:S(2)}) copy-start(f32[256]{0:T(256)} %param.14) | copy-start | bytes 3076
  48.2 1.0 %copy-start.5 = (f32[32,256]{1,0:T(8,128)S(1)}, f32[32,256]{1,0:T(8,128)}, u32[]{:S(2)}) copy-start(f32[32,256]{1,0:T(8,128)} %constant.80.clone.third_ref) | copy-start | bytes 98308
  66.4 26.2 %copy-start.4 = (f32[80,2560]{1,0:T(8,128)S(1)}, f32[80,2560]{1,0:T(8,128)}, u32[]{:S(2)}) copy-start(f32[80,2560]{1,0:T(8,128)} %chi_ref.1) | copy-start | bytes 2457604
  87.1 6.8 %collective-permute-start.1 = (bf16[80,2560]{1,0:T(8,128)(2,1)S(1)}, bf16[80,2560]{1,0:T(8,128)(2,1)S(1)}, u32[]{:S(2)}, u32[]{:S(2)}) collective-permute-start(bf16[80,2560]{1,0:T(8,128)(2,1)S(1)} %shard_map.116), channel_id=1, source_target_pairs={{0,16},{16,0},{1,17},{17,1},{2,18},{18,2},{3,19},{19,3},{4,20},{20... | collective-permute-start | bytes 1228808 | tf_op jit(solution)/shard_map/ppermute | solution.py:326
